TPU v7x, 32 devices: a whole 2x2x4 slice. The times are simulated.
32 devices in a mesh: seq: 16 (over z, y, x), head: 2 (over core).
Axes of the slice: x: 2, y: 2, z: 4, core: 2. Of those that a mesh axis runs over, the one named last changes fastest.
Arguments:
- tokens: bfloat16 [16384, 1024], P('seq'), may hold values from -6 to 6
- memory: bfloat16 [16384, 1024], P('seq'), may hold values from -6 to 6
- cotangent: bfloat16 [16384, 1024], P('seq'), may hold values from -6 to 6
- tgt_lengths: int32 [32], replicated, may hold values from 1 to 1792, as said below
- mem_lengths: int32 [32], replicated, may hold values from 1 to 1792, as said below
- self_query: bfloat16 [1024, 1024], P(None, 'head'), may hold values from -0.1875 to 0.1875
- self_key: bfloat16 [1024, 1024], P(None, 'head'), may hold values from -0.1875 to 0.1875
- self_value: bfloat16 [1024, 1024], P(None, 'head'), may hold values from -0.1875 to 0.1875
- self_output: bfloat16 [1024, 1024], P('head'), may hold values from -0.75 to 0.75
- cross_query: bfloat16 [1024, 1024], P(None, 'head'), may hold values from -0.1875 to 0.1875
- cross_key: bfloat16 [1024, 1024], P(None, 'head'), may hold values from -0.1875 to 0.1875
- cross_value: bfloat16 [1024, 1024], P(None, 'head'), may hold values from -0.1875 to 0.1875
- cross_output: bfloat16 [1024, 1024], P('head'), may hold values from -0.75 to 0.75
- hidden_in: bfloat16 [1024, 4096], P(None, 'head'), may hold values from -0.1875 to 0.1875
- hidden_out: bfloat16 [4096, 1024], P('head'), may hold values from -0.09375 to 0.09375
- prefix_keys: float32 [30, 1024], P(None, 'head'), may hold values from -6 to 6
- prefix_values: float32 [30, 1024], P(None, 'head'), may hold values from -6 to 6
- adapter_down: float32 [1024, 512], P(None, 'head'), may hold values from -0.1875 to 0.1875
- adapter_down_bias: float32 [512], P('head'), may hold values from -3 to 3
- adapter_up: float32 [512, 1024], P('head'), may hold values from -0.25 to 0.25
- adapter_up_bias: float32 [1024], replicated, may hold values from -1.2 to 1.2
Outputs:
- outputs: bfloat16 [16384, 1024], P('seq')
- grad_tokens: float32 [16384, 1024], P('seq')
- grad_memory: float32 [16384, 1024], P('seq')
- grad_prefix_keys: float32 [30, 1024], P(None, 'head')
- grad_prefix_values: float32 [30, 1024], P(None, 'head')
- grad_adapter_down: float32 [1024, 512], P(None, 'head')
- grad_adapter_down_bias: float32 [512], P('head')
- grad_adapter_up: float32 [512, 1024], P('head')
- grad_adapter_up_bias: float32 [1024], replicated
Inputs may be any that keep to these rules, and one draw needn't show every extreme that they name: `tgt_lengths`: target sequences are packed in order; each holds at most 1792 tokens and one holds exactly 1792. `mem_lengths`: target sequence j reads encoder sequence j, both packed in order; where encoder sequence j ends in the packed encoder rows differs from where target sequence j ends in the packed target tokens by at most 128, and by exactly 128 for some j; each encoder sequence holds at most 1792 rows and one holds exactly 1792.
All inputs are finite; a program needn't handle non-finite values.
Results may differ from a plain program's by a relative error of at most 0.03.
Values may be sent and summed in bfloat16 or wider, within the bound.
No kernel may reach another device: no remote copies, remote signals or barrier semaphores. Data moves between devices by JAX's collectives and lax.ppermute only.
A program may use at most 768 MiB of HBM per device.

v0:
```python
import jax
import jax.numpy as jnp
from jax import lax
from jax.sharding import PartitionSpec as P

HEAD_DIM = 64


EPS = 1e-05
MASKED = -1e30


def from_behind(block, axis, distance):
    devices = range(lax.axis_size(axis))
    route = [(i - distance, i) for i in devices if i - distance in devices]
    return lax.ppermute(block, axis, route)


def product(left, right):
    return jnp.dot(left, right, preferred_element_type=jnp.float32)


def product_right_t(left, right):
    return jnp.einsum("rk,ck->rc", left, right, preferred_element_type=jnp.float32)


def product_left_t(left, right):
    return jnp.einsum("rk,rc->kc", left, right, preferred_element_type=jnp.float32)


def norm_rows(value):
    center = value - jnp.mean(value, axis=-1, keepdims=True)
    spread = jnp.mean(center * center, axis=-1, keepdims=True)
    return center * lax.rsqrt(spread + EPS)


def gelu_exact(value):
    return jax.nn.gelu(value, approximate=False)


def doc_ids(lengths, places):
    bounds = jnp.cumsum(lengths)
    return jnp.sum((places[:, None] >= bounds[None, :]).astype(jnp.int32), axis=1)


def norm_backward(value, grad):
    return jax.vjp(norm_rows, value)[1](grad)[0]


def gelu_backward(value, grad):
    return jax.vjp(gelu_exact, value)[1](grad)[0]


def slices(value, count, rows):
    return [value[index * rows : (index + 1) * rows] for index in range(count)]


def attend(query, keys, values, allowed, prefix_keys, prefix_values):
    factor = HEAD_DIM ** (-0.5)
    results = []
    logsums = []
    for head in range(query.shape[1] // HEAD_DIM):
        offset = head * HEAD_DIM
        head_query = query[:, offset : offset + HEAD_DIM]
        scores = jnp.where(
            allowed,
            product_right_t(head_query, keys[:, offset : offset + HEAD_DIM]) * factor,
            MASKED,
        )
        row_max = jnp.max(scores, axis=1, keepdims=True)
        if prefix_keys is not None:
            prefix_scores = (
                product_right_t(head_query, prefix_keys[:, offset : offset + HEAD_DIM]) * factor
            )
            row_max = jnp.maximum(row_max, jnp.max(prefix_scores, axis=1, keepdims=True))
        weights = jnp.exp(scores - row_max)
        row_total = jnp.sum(weights, axis=1, keepdims=True)
        if prefix_keys is not None:
            prefix_weights = jnp.exp(prefix_scores - row_max)
            row_total = row_total + jnp.sum(prefix_weights, axis=1, keepdims=True)
        result = product(
            (weights / row_total).astype(jnp.bfloat16), values[:, offset : offset + HEAD_DIM]
        )
        if prefix_keys is not None:
            result = result + product(
                (prefix_weights / row_total).astype(jnp.bfloat16),
                prefix_values[:, offset : offset + HEAD_DIM],
            )
        results.append(result)
        logsums.append(row_max + jnp.log(row_total))
    return (jnp.concatenate(results, axis=1), logsums)


def attend_back(query, keys, values, allowed, logsums, grad_out, prefix_keys, prefix_values):
    factor = HEAD_DIM ** (-0.5)
    query_parts = []
    key_parts = []
    value_parts = []
    prefix_key_parts = []
    prefix_value_parts = []
    for head in range(query.shape[1] // HEAD_DIM):
        offset = head * HEAD_DIM
        head_query = query[:, offset : offset + HEAD_DIM]
        head_keys = keys[:, offset : offset + HEAD_DIM]
        head_values = values[:, offset : offset + HEAD_DIM]
        head_grad = grad_out[:, offset : offset + HEAD_DIM]
        scores = jnp.where(allowed, product_right_t(head_query, head_keys) * factor, MASKED)
        weights = jnp.exp(scores - logsums[head])
        grad_weights = product_right_t(head_grad, head_values)
        central = jnp.sum(weights * grad_weights, axis=1, keepdims=True)
        if prefix_keys is not None:
            prefix_head_keys = prefix_keys[:, offset : offset + HEAD_DIM]
            prefix_head_values = prefix_values[:, offset : offset + HEAD_DIM]
            prefix_weights = jnp.exp(
                product_right_t(head_query, prefix_head_keys) * factor - logsums[head]
            )
            prefix_grad = product_right_t(head_grad, prefix_head_values)
            central = central + jnp.sum(prefix_weights * prefix_grad, axis=1, keepdims=True)
        grad_scores = (weights * (grad_weights - central)).astype(jnp.bfloat16)
        query_grad = product(grad_scores, head_keys) * factor
        key_parts.append(product_left_t(grad_scores, head_query) * factor)
        value_parts.append(product_left_t(weights.astype(jnp.bfloat16), head_grad))
        if prefix_keys is not None:
            prefix_scores_grad = (prefix_weights * (prefix_grad - central)).astype(jnp.bfloat16)
            query_grad = query_grad + product(prefix_scores_grad, prefix_head_keys) * factor
            prefix_key_parts.append(product_left_t(prefix_scores_grad, head_query) * factor)
            prefix_value_parts.append(
                product_left_t(prefix_weights.astype(jnp.bfloat16), head_grad)
            )
        query_parts.append(query_grad)
    joined = (
        jnp.concatenate(query_parts, axis=1),
        jnp.concatenate(key_parts, axis=1),
        jnp.concatenate(value_parts, axis=1),
    )
    if prefix_keys is None:
        return joined + (None, None)
    return joined + (
        jnp.concatenate(prefix_key_parts, axis=1),
        jnp.concatenate(prefix_value_parts, axis=1),
    )


def on_device(
    tokens,
    memory,
    cotangent,
    tgt_lengths,
    mem_lengths,
    self_query,
    self_key,
    self_value,
    self_output,
    cross_query,
    cross_key,
    cross_value,
    cross_output,
    hidden_in,
    hidden_out,
    prefix_keys,
    prefix_values,
    adapter_down,
    adapter_down_bias,
    adapter_up,
    adapter_up_bias,
):
    bf16 = jnp.bfloat16
    rows = tokens.shape[0]
    shards = lax.axis_size("seq")
    position = lax.axis_index("seq")
    total_rows = rows * shards
    tok_place = position * rows + jnp.arange(rows, dtype=jnp.int32)
    self_place = (position - 2) * rows + jnp.arange(3 * rows, dtype=jnp.int32)
    mem_place = (position - 2) * rows + jnp.arange(5 * rows, dtype=jnp.int32)
    query_doc = doc_ids(tgt_lengths, tok_place)
    self_doc = doc_ids(tgt_lengths, self_place)
    mem_doc = doc_ids(mem_lengths, mem_place)
    self_allowed = (
        (query_doc[:, None] == self_doc[None, :])
        & (self_place[None, :] <= tok_place[:, None])
        & (self_place[None, :] >= 0)
    )
    mem_valid = (mem_place >= 0) & (mem_place < total_rows)
    cross_allowed = (query_doc[:, None] == mem_doc[None, :]) & mem_valid[None, :]
    tokens_f = tokens.astype(jnp.float32)
    query = product(tokens, self_query).astype(bf16)
    key_local = product(tokens, self_key).astype(bf16)
    value_local = product(tokens, self_value).astype(bf16)
    earlier = []
    for step_by in (2, 1):
        earlier.append(from_behind((key_local, value_local, memory), "seq", step_by))
    later = []
    for step_by in (1, 2):
        later.append(from_behind(memory, "seq", -step_by))
    keys = jnp.concatenate([earlier[0][0], earlier[1][0], key_local], axis=0)
    values = jnp.concatenate([earlier[0][1], earlier[1][1], value_local], axis=0)
    encoder = jnp.concatenate([earlier[0][2], earlier[1][2], memory, later[0], later[1]], axis=0)
    mem_keys = product(encoder, cross_key).astype(bf16)
    mem_values = product(encoder, cross_value).astype(bf16)
    prefix_k = prefix_keys.astype(bf16)
    prefix_v = prefix_values.astype(bf16)
    attended, self_logsums = attend(query, keys, values, self_allowed, prefix_k, prefix_v)
    attended = attended.astype(bf16)
    self_sum = lax.psum(product(attended, self_output).astype(jnp.bfloat16), "head").astype(
        jnp.float32
    )
    pre_first = tokens_f + self_sum
    first = norm_rows(pre_first)
    first_low = first.astype(bf16)
    cross_q = product(first_low, cross_query).astype(bf16)
    crossed, cross_logsums = attend(cross_q, mem_keys, mem_values, cross_allowed, None, None)
    crossed = crossed.astype(bf16)
    cross_sum = lax.psum(product(crossed, cross_output).astype(jnp.bfloat16), "head").astype(
        jnp.float32
    )
    pre_second = first + cross_sum
    second = norm_rows(pre_second)
    second_low = second.astype(bf16)
    inner = product(second_low, hidden_in)
    gated = gelu_exact(inner).astype(bf16)
    down_low = adapter_down.astype(bf16)
    up_low = adapter_up.astype(bf16)
    down = product(second_low, down_low) + adapter_down_bias
    adapted = gelu_exact(down).astype(bf16)
    branch_part = product(gated, hidden_out) + 4.0 * product(adapted, up_low)
    branch = (
        lax.psum(branch_part.astype(jnp.bfloat16), "head").astype(jnp.float32)
        + 4.0 * adapter_up_bias
    )
    pre_third = second + branch
    outputs = norm_rows(pre_third).astype(bf16)
    d_third = norm_backward(pre_third, cotangent.astype(jnp.float32))
    grad_branch = d_third.astype(bf16)
    grad_up_bias = 4.0 * jnp.sum(grad_branch, axis=0, dtype=jnp.float32)
    grad_up = 4.0 * product_left_t(adapted, grad_branch)
    grad_inner = gelu_backward(inner, product_right_t(grad_branch, hidden_out)).astype(bf16)
    grad_down = gelu_backward(down, 4.0 * product_right_t(grad_branch, up_low)).astype(bf16)
    grad_down_w = product_left_t(second_low, grad_down)
    grad_down_bias = jnp.sum(grad_down, axis=0, dtype=jnp.float32)
    second_part = product_right_t(grad_inner, hidden_in) + product_right_t(grad_down, down_low)
    d_second = d_third + lax.psum(second_part.astype(jnp.bfloat16), "head").astype(jnp.float32)
    d_cross = norm_backward(pre_second, d_second)
    d_crossed = product_right_t(d_cross.astype(bf16), cross_output).astype(bf16)
    cross_q_grad, mem_key_grad, mem_value_grad, unused_k, unused_v = attend_back(
        cross_q, mem_keys, mem_values, cross_allowed, cross_logsums, d_crossed, None, None
    )
    first_part = product_right_t(cross_q_grad.astype(bf16), cross_query)
    d_first = d_cross + lax.psum(first_part.astype(jnp.bfloat16), "head").astype(jnp.float32)
    d_tokens = norm_backward(pre_first, d_first)
    d_attended = product_right_t(d_tokens.astype(bf16), self_output).astype(bf16)
    query_grad, key_grad, value_grad, prefix_key_grad, prefix_value_grad = attend_back(
        query, keys, values, self_allowed, self_logsums, d_attended, prefix_k, prefix_v
    )
    key_slots = slices(key_grad, 3, rows)
    value_slots = slices(value_grad, 3, rows)
    mem_key_slots = slices(mem_key_grad, 5, rows)
    mem_value_slots = slices(mem_value_grad, 5, rows)
    key_mine = key_slots[2]
    value_mine = value_slots[2]
    mem_key_mine = mem_key_slots[2]
    mem_value_mine = mem_value_slots[2]
    for step_by in (1, 2):
        arrived = (
            from_behind(key_slots[2 - step_by].astype(jnp.bfloat16), "seq", -step_by).astype(
                jnp.float32
            ),
            from_behind(value_slots[2 - step_by].astype(jnp.bfloat16), "seq", -step_by).astype(
                jnp.float32
            ),
            from_behind(mem_key_slots[2 - step_by].astype(jnp.bfloat16), "seq", -step_by).astype(
                jnp.float32
            ),
            from_behind(mem_value_slots[2 - step_by].astype(jnp.bfloat16), "seq", -step_by).astype(
                jnp.float32
            ),
        )
        key_mine = key_mine + arrived[0]
        value_mine = value_mine + arrived[1]
        mem_key_mine = mem_key_mine + arrived[2]
        mem_value_mine = mem_value_mine + arrived[3]
    for step_by in (1, 2):
        arrived = (
            from_behind(mem_key_slots[2 + step_by].astype(jnp.bfloat16), "seq", step_by).astype(
                jnp.float32
            ),
            from_behind(mem_value_slots[2 + step_by].astype(jnp.bfloat16), "seq", step_by).astype(
                jnp.float32
            ),
        )
        mem_key_mine = mem_key_mine + arrived[0]
        mem_value_mine = mem_value_mine + arrived[1]
    token_part = (
        product_right_t(query_grad.astype(bf16), self_query)
        + product_right_t(key_mine.astype(bf16), self_key)
        + product_right_t(value_mine.astype(bf16), self_value)
    )
    memory_part = product_right_t(mem_key_mine.astype(bf16), cross_key) + product_right_t(
        mem_value_mine.astype(bf16), cross_value
    )
    token_sum, memory_sum = (
        lax.psum(token_part.astype(jnp.bfloat16), "head").astype(jnp.float32),
        lax.psum(memory_part.astype(jnp.bfloat16), "head").astype(jnp.float32),
    )
    grad_tokens = d_tokens + token_sum
    (
        grad_prefix_keys,
        grad_prefix_values,
        grad_adapter_down,
        grad_adapter_down_bias,
        grad_adapter_up,
        grad_adapter_up_bias,
    ) = (
        lax.psum(prefix_key_grad.astype(jnp.bfloat16), "seq").astype(jnp.float32),
        lax.psum(prefix_value_grad.astype(jnp.bfloat16), "seq").astype(jnp.float32),
        lax.psum(grad_down_w.astype(jnp.bfloat16), "seq").astype(jnp.float32),
        lax.psum(grad_down_bias.astype(jnp.bfloat16), "seq").astype(jnp.float32),
        lax.psum(grad_up.astype(jnp.bfloat16), "seq").astype(jnp.float32),
        lax.psum(grad_up_bias.astype(jnp.bfloat16), "seq").astype(jnp.float32),
    )
    return (
        outputs,
        grad_tokens,
        memory_sum,
        grad_prefix_keys,
        grad_prefix_values,
        grad_adapter_down,
        grad_adapter_down_bias,
        grad_adapter_up,
        grad_adapter_up_bias,
    )


def solution(mesh):
    in_specs = (
        P("seq", None),
        P("seq", None),
        P("seq", None),
        P(),
        P(),
        P(None, "head"),
        P(None, "head"),
        P(None, "head"),
        P("head", None),
        P(None, "head"),
        P(None, "head"),
        P(None, "head"),
        P("head", None),
        P(None, "head"),
        P("head", None),
        P(None, "head"),
        P(None, "head"),
        P(None, "head"),
        P("head"),
        P("head", None),
        P(),
    )
    out_specs = (
        P("seq", None),
        P("seq", None),
        P("seq", None),
        P(None, "head"),
        P(None, "head"),
        P(None, "head"),
        P("head"),
        P("head", None),
        P(),
    )
    return jax.shard_map(
        on_device, mesh=mesh, in_specs=in_specs, out_specs=out_specs, check_vma=False
    )
```

profile of v0, /device:TPU:0, one launch (start us, length us, event | category | flops | bytes accessed | tf_op | source)
XLA Modules:
  0.0 1741.9 jit_solution(6218630687404857010)
XLA Ops:
  41.9 64.7 %collective-permute-done.1 = bf16[1024,512]{1,0:T(8,128)(2,1)} collective-permute-done((bf16[1024,512]{1,0:T(8,128)(2,1)}, bf16[1024,512]{1,0:T(8,128)(2,1)}, u32[]{:S(2)}, u32[]{:S(2)}) %collective-permute-start.1) | collective-permute-done | bytes 1048608 | tf_op jit(solution)/shard_map/ppermute | solution.py:16
  321.2 29.1 %all-reduce.11.cloned.1.call-done = bf16[1024,1024]{1,0:T(8,128)(2,1)} async-done(((bf16[1024,1024]{1,0:T(8,128)(2,1)}), bf16[1024,1024]{1,0:T(8,128)(2,1)}) %all-reduce.11.cloned.1.call-update) | async-done | bytes 2097168 | tf_op jit(solution)/shard_map/psum | solution.py:204
  449.9 11.8 fusion.5
  578.1 25.0 %all-reduce.13.cloned.1.call-done = bf16[1024,1024]{1,0:T(8,128)(2,1)} async-done(((bf16[1024,1024]{1,0:T(8,128)(2,1)}), bf16[1024,1024]{1,0:T(8,128)(2,1)}) %all-reduce.13.cloned.1.call-update) | async-done | bytes 2097168 | tf_op jit(solution)/shard_map/psum | solution.py:213
  608.0 22.2 %fusion.64 = (f32[1024,2048]{1,0:T(8,128)S(1)}, f32[1024,2048]{1,0:T(8,128)}) fusion(bf16[1024,1024]{1,0:T(8,128)(2,1)S(1)} %multiply_convert_fusion.19, bf16[1024,2048]{1,0:T(8,128)(2,1)S(1)} %copy-done.202), kind=kOutput, calls=%fused_computation.155 | convolution fusion | flops 4424990720 | bytes 23068672 | tf_op jit(solution)/shard_map/dot_general | solution.py:20
  644.7 22.5 %all-reduce.15.cloned.1.call-done = bf16[1024,1024]{1,0:T(8,128)(2,1)} async-done(((bf16[1024,1024]{1,0:T(8,128)(2,1)}), bf16[1024,1024]{1,0:T(8,128)(2,1)}) %all-reduce.15.cloned.1.call-update) | async-done | bytes 2097168 | tf_op jit(solution)/shard_map/psum | solution.py:227
  678.0 20.1 %fusion.137 = f32[1024,1024]{1,0:T(8,128)} fusion(bf16[1024,2048]{1,0:T(8,128)(2,1)} %param.34, f32[1024,2048]{1,0:T(8,128)} %copy-done.211, f32[1024,2048]{1,0:T(8,128)} %get-tuple-element.113, bf16[1024,1024]{1,0:T(8,128)(2,1)S(1)} %get-tuple-element.20, bf16[2048,1024]{1,0:T(8,128)(2,1)} %param.35), kind=kOutput, calls=%fused_computation.246 | convolution fusion | flops 8619294720 | bytes 31457280 | tf_op jit(solution)/shard_map/rk,ck->rc/dot_general | solution.py:24
  708.0 20.5 %all-reduce.17.cloned.1.call-done = bf16[1024,1024]{1,0:T(8,128)(2,1)} async-done(((bf16[1024,1024]{1,0:T(8,128)(2,1)}), bf16[1024,1024]{1,0:T(8,128)(2,1)}) %all-reduce.17.cloned.1.call-update) | async-done | bytes 2097168 | tf_op jit(solution)/shard_map/psum | solution.py:241
  750.0 13.2 multiply_reduce_fusion.7
  763.1 14.4 multiply_convert_fusion.7
  786.5 14.7 multiply_reduce_fusion.6
  810.0 14.0 multiply_reduce_fusion.5
  832.8 14.1 multiply_reduce_fusion.4
  855.6 14.3 multiply_reduce_fusion.3
  878.7 14.1 multiply_reduce_fusion.2
  901.6 14.0 multiply_reduce_fusion.1
  924.4 13.1 multiply_reduce_fusion
  968.6 15.0 multiply_convert_fusion.6
  990.0 20.1 %multiply_convert_fusion.5 = bf16[1024,5120]{1,0:T(8,128)(2,1)} fusion(f32[1024,5120]{1,0:T(8,128)} %get-tuple-element.120, f32[1024,5120]{1,0:T(8,128)} %get-tuple-element.101, f32[1024]{0:T(1024)S(1)} %copy-done.143, f32[1024]{0:T(1024)S(1)} %copy-done.122), kind=kLoop, calls=%fused_computation.15 | loop fusion | flops 20971520 | bytes 52436992 | tf_op jit(solution)/shard_map/convert_element_type | solution.py:119
  1024.9 14.7 multiply_convert_fusion.4
  1050.2 20.1 %multiply_convert_fusion.3 = bf16[1024,5120]{1,0:T(8,128)(2,1)} fusion(f32[1024,5120]{1,0:T(8,128)} %get-tuple-element.124, f32[1024,5120]{1,0:T(8,128)} %get-tuple-element.105, f32[1024]{0:T(1024)S(1)} %copy-done.141, f32[1024]{0:T(1024)S(1)} %copy-done.118), kind=kLoop, calls=%fused_computation.9 | loop fusion | flops 20971520 | bytes 52436992 | tf_op jit(solution)/shard_map/convert_element_type | solution.py:119
  1085.1 14.6 multiply_convert_fusion.2
  1110.2 20.1 %multiply_convert_fusion = bf16[1024,5120]{1,0:T(8,128)(2,1)} fusion(f32[1024,5120]{1,0:T(8,128)} %get-tuple-element.130, f32[1024,5120]{1,0:T(8,128)} %get-tuple-element.111, f32[1024]{0:T(1024)S(1)} %get-tuple-element.129, f32[1024]{0:T(1024)S(1)} %copy-done.115), kind=kLoop, calls=%fused_computation | loop fusion | flops 20971520 | bytes 52436992 | tf_op jit(solution)/shard_map/convert_element_type | solution.py:119
  1133.0 15.0 multiply_convert_fusion.1
  1214.0 46.5 %collective-permute-done.15 = bf16[1024,512]{0,1:T(8,128)(2,1)} collective-permute-done((bf16[1024,512]{0,1:T(8,128)(2,1)}, bf16[1024,512]{0,1:T(8,128)(2,1)}, u32[]{:S(2)}, u32[]{:S(2)}) %collective-permute-start.15) | collective-permute-done | bytes 1048608 | tf_op jit(solution)/shard_map/ppermute | solution.py:16
  1430.2 12.7 multiply_convert_fusion.8
  1443.0 12.9 multiply_convert_fusion.9
  1457.0 12.6 multiply_convert_fusion.10
  1470.8 12.7 multiply_convert_fusion.11
  1484.5 12.7 multiply_convert_fusion.12
  1498.4 12.7 multiply_convert_fusion.13
  1619.7 104.8 %all-reduce = (bf16[30,512]{1,0:T(8,128)(2,1)S(1)}, bf16[30,512]{1,0:T(8,128)(2,1)S(1)}, bf16[256]{0:T(256)(128)(2,1)S(1)}, bf16[1024]{0:T(1024)(128)(2,1)S(1)}) all-reduce(bf16[30,512]{1,0:T(8,128)(2,1)S(1)} %concatenate.56, bf16[30,512]{1,0:T(8,128)(2,1)S(1)} %concatenate.57, ...), channel_id=1, replica_groups=mesh['seq'=16,'head'=2] {'seq'}, use_global_device_ids=true, to_apply=%region_96.97 | all-reduce | flops 32000 | bytes 128000 | tf_op jit(solution)/shard_map/psum | solution.py:313
  (938 shorter events, 1035.0 us)
Async XLA Ops:
  7.2 298.6 %copy-start = (bf16[1024,512]{1,0:T(8,128)(2,1)S(1)}, bf16[1024,512]{1,0:T(8,128)(2,1)}, u32[]{:S(2)}) copy-start(bf16[1024,512]{1,0:T(8,128)(2,1)} %param.32) | copy-start | bytes 3145732
  7.2 343.1 %all-reduce.11.cloned.1.call-start = ((), (), s32[]{:S(2)}) async-start(), calls=%async_computation | async-start | bytes 4194304 | tf_op jit(solution)/shard_map/psum | solution.py:204
  11.5 232.4 %collective-permute-start.3 = (bf16[1024,512]{1,0:T(8,128)(2,1)}, bf16[1024,512]{1,0:T(8,128)(2,1)}, u32[]{:S(2)}, u32[]{:S(2)}) collective-permute-start(bf16[1024,512]{1,0:T(8,128)(2,1)} %convolution_convert_fusion.5), channel_id=1, source_target_pairs={{0,2},{2,4},{4,6},{6,8},{8,10},{10,12},{12,14},{14,16},{16,18},{18... | collective-permute-start | bytes 3145736 | tf_op jit(solution)/shard_map/ppermute | solution.py:16
  17.5 227.7 %collective-permute-start.2 = (bf16[1024,512]{1,0:T(8,128)(2,1)}, bf16[1024,512]{1,0:T(8,128)(2,1)}, u32[]{:S(2)}, u32[]{:S(2)}) collective-permute-start(bf16[1024,512]{1,0:T(8,128)(2,1)} %convolution_convert_fusion.5), channel_id=1, source_target_pairs={{0,4},{2,6},{4,8},{6,10},{8,12},{10,14},{12,16},{14,18},{16,20},{1... | collective-permute-start | bytes 3145736 | tf_op jit(solution)/shard_map/ppermute | solution.py:16
  23.2 83.5 %collective-permute-start.1 = (bf16[1024,512]{1,0:T(8,128)(2,1)}, bf16[1024,512]{1,0:T(8,128)(2,1)}, u32[]{:S(2)}, u32[]{:S(2)}) collective-permute-start(bf16[1024,512]{1,0:T(8,128)(2,1)} %convolution_convert_fusion.6), channel_id=1, source_target_pairs={{0,2},{2,4},{4,6},{6,8},{8,10},{10,12},{12,14},{14,16},{16,18},{18... | collective-permute-start | bytes 3145736 | tf_op jit(solution)/shard_map/ppermute | solution.py:16
  27.5 84.8 %collective-permute-start = (bf16[1024,512]{1,0:T(8,128)(2,1)}, bf16[1024,512]{1,0:T(8,128)(2,1)}, u32[]{:S(2)}, u32[]{:S(2)}) collective-permute-start(bf16[1024,512]{1,0:T(8,128)(2,1)} %convolution_convert_fusion.6), channel_id=1, source_target_pairs={{0,4},{2,6},{4,8},{6,10},{8,12},{10,14},{12,16},{14,18},{16,20},{1... | collective-permute-start | bytes 3145736 | tf_op jit(solution)/shard_map/ppermute | solution.py:16
  30.0 272.3 %collective-permute-start.6 = (bf16[1024,1024]{1,0:T(8,128)(2,1)}, bf16[1024,1024]{1,0:T(8,128)(2,1)}, u32[]{:S(2)}, u32[]{:S(2)}) collective-permute-start(bf16[1024,1024]{1,0:T(8,128)(2,1)} %param.22), channel_id=1, source_target_pairs={{2,0},{4,2},{6,4},{8,6},{10,8},{12,10},{14,12},{16,14},{18,16},{20... | collective-permute-start | bytes 6291464 | tf_op jit(solution)/shard_map/ppermute | solution.py:16
  34.6 209.0 %copy-start.31 = (f32[1024,30]{0,1:T(8,128)}, f32[1024,30]{0,1:T(8,128)S(1)}, u32[]{:S(2)}) copy-start(f32[1024,30]{0,1:T(8,128)S(1)} %get-tuple-element.67) | copy-start | bytes 368644
  34.9 207.8 %copy-start.34 = (f32[1024,30]{0,1:T(8,128)}, f32[1024,30]{0,1:T(8,128)S(1)}, u32[]{:S(2)}) copy-start(f32[1024,30]{0,1:T(8,128)S(1)} %get-tuple-element.71) | copy-start | bytes 368644
  36.5 247.7 %copy-start.87 = (bf16[30,512]{1,0:T(8,128)(2,1)}, bf16[30,512]{1,0:T(8,128)(2,1)S(1)}, u32[]{:S(2)}) copy-start(bf16[30,512]{1,0:T(8,128)(2,1)S(1)} %convert_element_type.446) | copy-start | bytes 92164
  41.9 242.4 %copy-start.47 = (f32[1024,30]{0,1:T(8,128)}, f32[1024,30]{0,1:T(8,128)S(1)}, u32[]{:S(2)}) copy-start(f32[1024,30]{0,1:T(8,128)S(1)} %get-tuple-element.95) | copy-start | bytes 368644
  106.6 192.1 %collective-permute-start.5 = (bf16[1024,1024]{1,0:T(8,128)(2,1)}, bf16[1024,1024]{1,0:T(8,128)(2,1)}, u32[]{:S(2)}, u32[]{:S(2)}) collective-permute-start(bf16[1024,1024]{1,0:T(8,128)(2,1)} %param.22), channel_id=1, source_target_pairs={{0,2},{2,4},{4,6},{6,8},{8,10},{10,12},{12,14},{14,16},{16,18},{18... | collective-permute-start | bytes 6291464 | tf_op jit(solution)/shard_map/ppermute | solution.py:16
  112.4 184.5 %collective-permute-start.4 = (bf16[1024,1024]{1,0:T(8,128)(2,1)}, bf16[1024,1024]{1,0:T(8,128)(2,1)}, u32[]{:S(2)}, u32[]{:S(2)}) collective-permute-start(bf16[1024,1024]{1,0:T(8,128)(2,1)} %param.22), channel_id=1, source_target_pairs={{0,4},{2,6},{4,8},{6,10},{8,12},{10,14},{12,16},{14,18},{16,20},{1... | collective-permute-start | bytes 6291464 | tf_op jit(solution)/shard_map/ppermute | solution.py:16
  243.9 60.1 %collective-permute-start.7 = (bf16[1024,1024]{1,0:T(8,128)(2,1)}, bf16[1024,1024]{1,0:T(8,128)(2,1)}, u32[]{:S(2)}, u32[]{:S(2)}) collective-permute-start(bf16[1024,1024]{1,0:T(8,128)(2,1)} %param.22), channel_id=1, source_target_pairs={{4,0},{6,2},{8,4},{10,6},{12,8},{14,10},{16,12},{18,14},{20,16},{2... | collective-permute-start | bytes 6291464 | tf_op jit(solution)/shard_map/ppermute | solution.py:16
  296.9 306.2 %all-reduce.13.cloned.1.call-start = ((), (), s32[]{:S(2)}) async-start(), calls=%async_computation.1 | async-start | bytes 4194304 | tf_op jit(solution)/shard_map/psum | solution.py:213
  578.1 89.1 %all-reduce.15.cloned.1.call-start = ((), (), s32[]{:S(2)}) async-start(), calls=%async_computation.2 | async-start | bytes 4194304 | tf_op jit(solution)/shard_map/psum | solution.py:227
  644.6 83.8 %all-reduce.17.cloned.1.call-start = ((), (), s32[]{:S(2)}) async-start(), calls=%async_computation.3 | async-start | bytes 4194304 | tf_op jit(solution)/shard_map/psum | solution.py:241
  705.9 561.0 %all-reduce.19.cloned.1.call-start = ((), (), s32[]{:S(2)}) async-start(), calls=%async_computation.4 | async-start | bytes 4194304 | tf_op jit(solution)/shard_map/psum | solution.py:248
  955.7 229.2 %collective-permute-start.16 = (bf16[1024,512]{0,1:T(8,128)(2,1)}, bf16[1024,512]{0,1:T(8,128)(2,1)}, u32[]{:S(2)}, u32[]{:S(2)}) collective-permute-start(bf16[1024,512]{0,1:T(8,128)(2,1)} %get-tuple-element.53), channel_id=1, source_target_pairs={{2,0},{4,2},{6,4},{8,6},{10,8},{12,10},{14,12},{16,14},{18,16},{20... | collective-permute-start | bytes 3145736 | tf_op jit(solution)/shard_map/ppermute | solution.py:16
  957.0 234.5 %collective-permute-start.19 = (bf16[1024,512]{0,1:T(8,128)(2,1)}, bf16[1024,512]{0,1:T(8,128)(2,1)}, u32[]{:S(2)}, u32[]{:S(2)}) collective-permute-start(bf16[1024,512]{0,1:T(8,128)(2,1)} %get-tuple-element.54), channel_id=1, source_target_pairs={{0,4},{2,6},{4,8},{6,10},{8,12},{10,14},{12,16},{14,18},{16,20},{1... | collective-permute-start | bytes 3145736 | tf_op jit(solution)/shard_map/ppermute | solution.py:16
  963.8 232.5 %collective-permute-start.18 = (bf16[1024,512]{0,1:T(8,128)(2,1)}, bf16[1024,512]{0,1:T(8,128)(2,1)}, u32[]{:S(2)}, u32[]{:S(2)}) collective-permute-start(bf16[1024,512]{0,1:T(8,128)(2,1)} %get-tuple-element.55), channel_id=1, source_target_pairs={{0,2},{2,4},{4,6},{6,8},{8,10},{10,12},{12,14},{14,16},{16,18},{18... | collective-permute-start | bytes 3145736 | tf_op jit(solution)/shard_map/ppermute | solution.py:16
  967.2 233.7 %collective-permute-start.17 = (bf16[1024,512]{0,1:T(8,128)(2,1)}, bf16[1024,512]{0,1:T(8,128)(2,1)}, u32[]{:S(2)}, u32[]{:S(2)}) collective-permute-start(bf16[1024,512]{0,1:T(8,128)(2,1)} %get-tuple-element.56), channel_id=1, source_target_pairs={{4,0},{6,2},{8,4},{10,6},{12,8},{14,10},{16,12},{18,14},{20,16},{2... | collective-permute-start | bytes 3145736 | tf_op jit(solution)/shard_map/ppermute | solution.py:16
  1161.4 439.8 %all-reduce.21.cloned.1.call-start = ((), (), s32[]{:S(2)}) async-start(), calls=%async_computation.5 | async-start | bytes 2097152 | tf_op jit(solution)/shard_map/psum | solution.py:315
  1183.5 30.5 %collective-permute-start.12 = (bf16[1024,512]{0,1:T(8,128)(2,1)}, bf16[1024,512]{0,1:T(8,128)(2,1)}, u32[]{:S(2)}, u32[]{:S(2)}) collective-permute-start(bf16[1024,512]{0,1:T(8,128)(2,1)} %get-tuple-element.49), channel_id=1, source_target_pairs={{2,0},{4,2},{6,4},{8,6},{10,8},{12,10},{14,12},{16,14},{18,16},{20... | collective-permute-start | bytes 3145736 | tf_op jit(solution)/shard_map/ppermute | solution.py:16
  1185.0 75.5 %collective-permute-start.15 = (bf16[1024,512]{0,1:T(8,128)(2,1)}, bf16[1024,512]{0,1:T(8,128)(2,1)}, u32[]{:S(2)}, u32[]{:S(2)}) collective-permute-start(bf16[1024,512]{0,1:T(8,128)(2,1)} %get-tuple-element.50), channel_id=1, source_target_pairs={{0,4},{2,6},{4,8},{6,10},{8,12},{10,14},{12,16},{14,18},{16,20},{1... | collective-permute-start | bytes 3145736 | tf_op jit(solution)/shard_map/ppermute | solution.py:16
  1191.5 69.0 %collective-permute-start.14 = (bf16[1024,512]{0,1:T(8,128)(2,1)}, bf16[1024,512]{0,1:T(8,128)(2,1)}, u32[]{:S(2)}, u32[]{:S(2)}) collective-permute-start(bf16[1024,512]{0,1:T(8,128)(2,1)} %get-tuple-element.51), channel_id=1, source_target_pairs={{0,2},{2,4},{4,6},{6,8},{8,10},{10,12},{12,14},{14,16},{16,18},{18... | collective-permute-start | bytes 3145736 | tf_op jit(solution)/shard_map/ppermute | solution.py:16
  1196.2 64.3 %collective-permute-start.13 = (bf16[1024,512]{0,1:T(8,128)(2,1)}, bf16[1024,512]{0,1:T(8,128)(2,1)}, u32[]{:S(2)}, u32[]{:S(2)}) collective-permute-start(bf16[1024,512]{0,1:T(8,128)(2,1)} %get-tuple-element.52), channel_id=1, source_target_pairs={{4,0},{6,2},{8,4},{10,6},{12,8},{14,10},{16,12},{18,14},{20,16},{2... | collective-permute-start | bytes 3145736 | tf_op jit(solution)/shard_map/ppermute | solution.py:16
  1200.7 526.2 %all-reduce.23.cloned.1.call-start = ((), (), s32[]{:S(2)}) async-start(), calls=%async_computation.6 | async-start | bytes 8388608 | tf_op jit(solution)/shard_map/psum | solution.py:301
  1427.5 168.6 %collective-permute-start.10 = (bf16[1024,512]{0,1:T(8,128)(2,1)}, bf16[1024,512]{0,1:T(8,128)(2,1)}, u32[]{:S(2)}, u32[]{:S(2)}) collective-permute-start(bf16[1024,512]{0,1:T(8,128)(2,1)} %get-tuple-element.58), channel_id=1, source_target_pairs={{2,0},{4,2},{6,4},{8,6},{10,8},{12,10},{14,12},{16,14},{18,16},{20... | collective-permute-start | bytes 3145736 | tf_op jit(solution)/shard_map/ppermute | solution.py:16
  1428.8 167.4 %collective-permute-start.11 = (bf16[1024,512]{0,1:T(8,128)(2,1)}, bf16[1024,512]{0,1:T(8,128)(2,1)}, u32[]{:S(2)}, u32[]{:S(2)}) collective-permute-start(bf16[1024,512]{0,1:T(8,128)(2,1)} %get-tuple-element.59), channel_id=1, source_target_pairs={{4,0},{6,2},{8,4},{10,6},{12,8},{14,10},{16,12},{18,14},{20,16},{2... | collective-permute-start | bytes 3145736 | tf_op jit(solution)/shard_map/ppermute | solution.py:16
  1559.0 33.6 %collective-permute-start.8 = (bf16[1024,512]{0,1:T(8,128)(2,1)}, bf16[1024,512]{0,1:T(8,128)(2,1)S(1)}, u32[]{:S(2)}, u32[]{:S(2)}) collective-permute-start(bf16[1024,512]{0,1:T(8,128)(2,1)} %get-tuple-element.60), channel_id=1, source_target_pairs={{2,0},{4,2},{6,4},{8,6},{10,8},{12,10},{14,12},{16,14},{18,16},{20... | collective-permute-start | bytes 3145736 | tf_op jit(solution)/shard_map/ppermute | solution.py:16
  1560.3 32.3 %collective-permute-start.9 = (bf16[1024,512]{0,1:T(8,128)(2,1)S(1)}, bf16[1024,512]{0,1:T(8,128)(2,1)}, u32[]{:S(2)}, u32[]{:S(2)}) collective-permute-start(bf16[1024,512]{0,1:T(8,128)(2,1)S(1)} %get-tuple-element.61), channel_id=1, source_target_pairs={{4,0},{6,2},{8,4},{10,6},{12,8},{14,10},{16,12},{18,14},{20,16},{2... | collective-permute-start | bytes 3145736 | tf_op jit(solution)/shard_map/ppermute | solution.py:16
  (279 other events, 6114.8 us)
Sparse Core Ops, SparseCore 0:
  297.0 53.2 all-reduce.10
  578.2 24.8 all-reduce.12
  644.8 22.3 all-reduce.14
  706.0 22.3 all-reduce.16
  1161.5 22.3 all-reduce.18
  1200.8 158.6 all-reduce.20
  1601.3 65.1 all-reduce.22
where the time goes:
time: 1750 us; the launch traced here: 1740 us
  matrix products  869 us (50%)
  other arithmetic  432 us (25%)
  waiting for transfers between devices  217 us (12%)
  blocking collectives  105 us (6%)
  starting transfers between devices  65 us (4%)
  local copies, waits for them, and re-layouts  37 us (2%)
  between operations  18 us (1%)
    dot_general x59, matrix products, product_right_t(): jnp.einsum('rk,ck->rc', left, right, preferred_element_type=jnp.float32)  399 us
    dot_general x60, matrix products, product(): return jnp.dot(left, right, preferred_element_type=jnp.float32)  264 us
    convert_element_type x16, other arithmetic, attend_back(): grad_scores = (weights * (grad_weights - central)).astype(jnp.bfloat16)  228 us
    dot_general x50, matrix products, product_left_t(): jnp.einsum('rk,rc->kc', left, right, preferred_element_type=jnp.float32)  205 us
    reduce_sum x16, other arithmetic, attend(): row_total = jnp.sum(weights, axis=1, keepdims=True)  124 us
    ppermute x20, waiting for transfers between devices, from_behind(): return lax.ppermute(block, axis, route)  120 us
    psum x1, blocking collectives, on_device(): lax.psum(prefix_key_grad.astype(jnp.bfloat16), 'seq').astype(jnp.float32)  105 us
    ppermute x20, starting transfers between devices, from_behind(): return lax.ppermute(block, axis, route)  64.5 us
  transfers between devices with their start and end apart: 27, of which 7 were waited for; matrix products, arithmetic and copies ran while one was open for 45% of the time, Pallas kernels for 0%

commit v1 on v0

v1 whole, which is shorter than its diff:
```python
import functools
from typing import NamedTuple

import jax
import jax.numpy as jnp
from jax import lax
from jax.experimental import pallas as pl
from jax.experimental.pallas import tpu as pltpu
from jax.sharding import PartitionSpec as P

HEAD_DIM = 64
MASKED = -1e30
LN2 = 0.6931471805599453
LOG2E = 1.4426950408889634
EPS = 1e-05
SEQ_MAX = 1792
DRIFT = 128
PAD = 128
BLOCK = 256
f32 = jnp.float32
bf16 = jnp.bfloat16


def dot(left, right):
    return jnp.dot(left, right, preferred_element_type=f32)


def dot_nt(left, right):
    return lax.dot_general(left, right, (((1,), (1,)), ((), ())), preferred_element_type=f32)


def dot_tn(left, right):
    return lax.dot_general(left, right, (((0,), (0,)), ((), ())), preferred_element_type=f32)


def split_rows(pair):
    zero = jnp.zeros((HEAD_DIM, pair.shape[1]), pair.dtype)
    return [
        jnp.concatenate([pair[:HEAD_DIM], zero], axis=0),
        jnp.concatenate([zero, pair[HEAD_DIM:]], axis=0),
    ]


def stack_lanes(pair):
    first = lax.broadcasted_iota(jnp.int32, pair.shape, 1) < HEAD_DIM
    zero = jnp.zeros_like(pair)
    return jnp.concatenate([jnp.where(first, pair, zero), jnp.where(first, zero, pair)], axis=0)


def over_range(low, high, body):
    def step(i, carry):
        body(pl.ds(pl.multiple_of(low + i * 128, 128), 128))
        return carry

    lax.fori_loop(0, pl.cdiv(high - low, 128), step, 0)


def over_tiles(info, segments, block, tile):
    def one_segment(segment, carry):
        first, count, low, high = (info[4 * segment + i, block] for i in range(4))

        def full(i, carry):
            tile(pl.multiple_of(first + i * BLOCK, 128), segment, False)
            return carry

        def edge(j, carry):
            i = jnp.where(j < low, j, j - low + high)
            tile(pl.multiple_of(first + i * BLOCK, 128), segment, True)
            return carry

        lax.fori_loop(low, high, full, 0)
        lax.fori_loop(0, low + count - high, edge, 0)
        return carry

    if segments == 1:
        one_segment(0, 0)
    else:
        lax.fori_loop(0, segments, one_segment, 0)


def owned(info, segments, cores, before, length):
    owner = lax.rem(info[4 * segments + 2, 0] + cores - before, cores)
    return pl.ds(pl.multiple_of(owner * length, length), length)


def allowed(row, start, end):
    place = row + lax.broadcasted_iota(jnp.int32, (BLOCK, start.shape[1]), 0)
    return (place >= start) & (place < end)


def pair_cols(head):
    return slice(head // 2 * 128, head // 2 * 128 + 128)


def head_rows(head):
    return slice(head * HEAD_DIM, head * HEAD_DIM + HEAD_DIM)


def attend_kernel(prefix, resume, last, segments, pieces, cores, info, *refs):
    refs = list(refs)
    q, start, end = refs[:3]
    del refs[:3]
    if pieces is None:
        k, v = refs[:2]
        del refs[:2]
    else:
        wk, wv = refs[:2]
        del refs[:2]
        parts = []
        for length, raw in pieces:
            count = cores if raw else 2
            parts.append(refs[:count])
            del refs[:count]
    if prefix:
        pk, pv = refs[:2]
        del refs[:2]
    if resume:
        top_in, total_in, acc_in = refs[:3]
        del refs[:3]
    outs = refs[: 2 if last else 3]
    del refs[: len(outs)]
    if pieces is not None:
        k, v = refs[:2]
        del refs[:2]
    vt = refs.pop(0)
    if last:
        out, lse = outs
        top, total, acc = refs[:3]
        del refs[:3]
    else:
        top, total, acc = outs
    block = pl.program_id(0)
    heads = q.shape[1] // HEAD_DIM
    least, most = info[4 * segments, 0], info[4 * segments + 1, 0]

    def bring(piece, offset, length, sem):
        window = pl.ds(offset, length)
        return (
            pltpu.make_async_copy(piece[0], k.at[window, :], sem.at[0]),
            pltpu.make_async_copy(piece[1], v.at[window, :], sem.at[1]),
        )

    def project(piece, offset, length):
        def rows_at(row, size):
            window = pl.ds(offset + row, size)

            @pl.when((offset + row < most) & (offset + row + size > least))
            def _():
                source = pl.ds(row, size)
                depth = piece[0].shape[1]
                new_k, new_v = 0.0, 0.0
                for core, part in enumerate(piece):
                    some = owned(info, segments, cores, core, depth)
                    value = part[source, :]
                    new_k = new_k + dot(value, wk[some, :])
                    new_v = new_v + dot(value, wv[some, :])
                k[window, :] = new_k.astype(bf16)
                new_v = new_v.astype(bf16)
                v[window, :] = new_v
                vt[:, window] = new_v.T

        def step(i, carry):
            rows_at(pl.multiple_of(i * BLOCK, BLOCK), BLOCK)
            return carry

        full = length // BLOCK
        lax.fori_loop(0, full, step, 0)
        if length % BLOCK:
            rows_at(full * BLOCK, length % BLOCK)

    def turn_over(window):
        vt[:, window] = v[window, :].T

    @pl.when(block == 0)
    def _():
        if pieces is None:
            over_range(least, most, turn_over)
        else:
            offset, ready = 0, []
            for (length, raw), piece in zip(pieces, parts):
                if not raw:
                    ready.append((offset, length))
                    for copy in bring(piece, offset, length, refs[0]):
                        copy.start()
                offset += length
            rest = slice(offset, k.shape[0])
            k[rest, :] = jnp.zeros((k.shape[0] - offset, k.shape[1]), bf16)
            v[rest, :] = jnp.zeros((k.shape[0] - offset, k.shape[1]), bf16)
            vt[:, rest] = jnp.zeros((k.shape[1], k.shape[0] - offset), bf16)
            offset = 0
            for (length, raw), piece in zip(pieces, parts):
                if raw:
                    project(piece, offset, length)
                offset += length
            offset = 0
            for (length, raw), piece in zip(pieces, parts):
                if not raw:
                    for copy in bring(piece, offset, length, refs[0]):
                        copy.wait()
                    over_range(jnp.maximum(least, offset), jnp.minimum(most, offset + length), turn_over)
                offset += length

    qs = []
    for pair in range(heads // 2):
        qs.extend(split_rows(q[:, pair * 128 : pair * 128 + 128].T))
    if resume:
        top[...] = top_in[...]
        total[...] = total_in[...]
        acc[...] = acc_in[...]
    elif prefix:
        there = lax.broadcasted_iota(jnp.int32, (32, BLOCK), 0) < prefix
        for head in range(heads):
            scores = jnp.where(there, dot(pk[:, pair_cols(head)], qs[head]), MASKED)
            peak = jnp.max(scores, axis=0, keepdims=True)
            weights = jnp.exp2(scores - peak)
            top[head : head + 1] = peak
            total[head : head + 1] = jnp.sum(weights, axis=0, keepdims=True)
            turned = pv[:, pair_cols(head)].T
            acc[head_rows(head)] = dot(turned[head_rows(head % 2)], weights.astype(bf16))
    else:
        top[...] = jnp.full(top.shape, MASKED, f32)
        total[...] = jnp.zeros(total.shape, f32)
        acc[...] = jnp.zeros(acc.shape, f32)

    def tile(row, segment, edge):
        window = pl.ds(row, BLOCK)
        if edge:
            seen = pl.ds(segment, 1)
            open_ = allowed(row, start[seen, :], end[seen, :])
        scores = [dot(k[window, pair_cols(head)], qs[head]) for head in range(heads)]
        for head in range(heads):
            score = scores[head]
            if edge:
                score = jnp.where(open_, score, MASKED)
            old = top[head : head + 1]
            peak = jnp.maximum(old, jnp.max(score, axis=0, keepdims=True))
            weights = jnp.exp2(score - peak)
            scale = jnp.exp2(old - peak)
            top[head : head + 1] = peak
            total[head : head + 1] = total[head : head + 1] * scale + jnp.sum(
                weights, axis=0, keepdims=True
            )
            acc[head_rows(head)] = acc[head_rows(head)] * scale + dot(
                vt[head_rows(head), window], weights.astype(bf16)
            )

    over_tiles(info, segments, block, tile)
    if last:
        for pair in range(heads // 2):
            parts = [
                acc[head_rows(head)] * (1.0 / total[head : head + 1])
                for head in (2 * pair, 2 * pair + 1)
            ]
            out[:, pair * 128 : pair * 128 + 128] = (
                jnp.concatenate(parts, axis=0).T.astype(bf16)
            )
        lse[...] = top[...] + jnp.log2(total[...])


def kernel_params():
    return pltpu.CompilerParams(
        dimension_semantics=("arbitrary",), vmem_limit_bytes=60 << 20
    )


class Rows(NamedTuple):
    parts: list
    length: int
    place: int = 0


def attend(query, keys, values, start, end, info, prefix=None, state=None, last=True, weights=None):
    rows, cols = query.shape
    heads = cols // HEAD_DIM
    by_rows = pl.BlockSpec((BLOCK, cols), lambda b, info: (b, 0))
    by_lanes = lambda count: pl.BlockSpec((count, BLOCK), lambda b, info: (0, b))
    whole = lambda count, wide=cols: pl.BlockSpec((count, wide), lambda b, info: (0, 0))
    segments = start.shape[0]
    operands = [query, start, end]
    specs = [by_rows, by_lanes(segments), by_lanes(segments)]
    pieces, cores = None, 1
    if weights is None:
        window = keys.shape[0]
        operands += [keys, values]
        specs += [whole(window)] * 2
    else:
        pieces = tuple(
            (piece.length, True) if isinstance(piece, Rows) else (piece[0].shape[0], False)
            for piece in keys
        )
        window = sum(length for length, raw in pieces) + PAD
        operands += list(weights)
        specs += [whole(weights[0].shape[0])] * 2
        for (length, raw), piece in zip(pieces, keys):
            if raw:
                cores = len(piece.parts)
                operands += list(piece.parts)
                place = piece.place
                specs += [
                    pl.BlockSpec((length, part.shape[1]), lambda b, info, place=place: (place, 0))
                    for part in piece.parts
                ]
            else:
                operands += list(piece)
                specs += [pl.BlockSpec(memory_space=pl.ANY)] * 2
    if prefix is not None:
        operands += [prefix[0], prefix[1]]
        specs += [whole(32), whole(32)]
    state_specs = [by_lanes(heads), by_lanes(heads), by_lanes(cols)]
    if state is not None:
        operands += list(state)
        specs += state_specs
    shape = jax.ShapeDtypeStruct
    scratch = [pltpu.VMEM((cols, window), bf16)]
    if last:
        outs = [shape((rows, cols), bf16), shape((heads, rows), f32)]
        out_specs = [by_rows, by_lanes(heads)]
        scratch += [pltpu.VMEM((n, BLOCK), f32) for n in (heads, heads, cols)]
    else:
        outs = [shape((n, rows), f32) for n in (heads, heads, cols)]
        out_specs = list(state_specs)
    if weights is not None:
        outs += [shape((window, cols), bf16)] * 2
        out_specs += [whole(window)] * 2
        scratch.append(pltpu.SemaphoreType.DMA((2,)))
    return pl.pallas_call(
        functools.partial(
            attend_kernel, 0 if prefix is None else prefix[2], state is not None, last, segments,
            pieces, cores,
        ),
        out_shape=tuple(outs),
        grid_spec=pltpu.PrefetchScalarGridSpec(
            num_scalar_prefetch=1,
            grid=(rows // BLOCK,),
            in_specs=specs,
            out_specs=tuple(out_specs),
            scratch_shapes=scratch,
        ),
        compiler_params=kernel_params(),
    )(info, *operands)


def attend_back_kernel(prefix, resume, own, final, cuts, cores, segments, info, *refs):
    refs = list(refs)
    q, d_out, out, k, v, start, end, lse, wk, wv = refs[:10]
    del refs[:10]
    if prefix:
        pk, pv = refs[:2]
        del refs[:2]
    if resume:
        dq_in = refs.pop(0)
    if own:
        wq = refs.pop(0)
    pieces = len(cuts) - 1
    grads = [refs[i * cores : i * cores + cores] for i in range(pieces)]
    del refs[: pieces * cores]
    if prefix:
        dpk, dpv = refs[:2]
        del refs[:2]
    if not own:
        dq_out = refs.pop(0)
    kt, dk, dv = refs[:3]
    del refs[:3]
    if own:
        dq, dq_low = refs
    elif final:
        (dq,) = refs
    else:
        dq = dq_out
    block = pl.program_id(0)
    heads = q.shape[1] // HEAD_DIM
    pairs = heads // 2

    @pl.when(block == 0)
    def _():
        def prepare(window):
            kt[:, window] = k[window, :].T
            dk[window, :] = jnp.zeros((128, dk.shape[1]), f32)
            dv[window, :] = jnp.zeros((128, dv.shape[1]), f32)

        over_range(info[4 * segments, 0], info[4 * segments + 1, 0], prepare)
        if prefix:
            dpk[...] = jnp.zeros(dpk.shape, f32)
            dpv[...] = jnp.zeros(dpv.shape, f32)

    qs, ds, delta, q_stack, d_stack = [], [], [], [], []
    for pair in range(pairs):
        cols = slice(pair * 128, pair * 128 + 128)
        q_pair, d_pair = q[:, cols], d_out[:, cols]
        qs.extend(split_rows(q_pair.T))
        ds.extend(split_rows(d_pair.T))
        both = (d_pair.astype(f32) * out[:, cols].astype(f32)).T
        delta.append(jnp.sum(both[:HEAD_DIM], axis=0, keepdims=True))
        delta.append(jnp.sum(both[HEAD_DIM:], axis=0, keepdims=True))
        q_stack.append(stack_lanes(q_pair))
        d_stack.append(stack_lanes(d_pair))
    if resume:
        dq[...] = dq_in[...]
    else:
        dq[...] = jnp.zeros(dq.shape, f32)
    if prefix:
        there = lax.broadcasted_iota(jnp.int32, (32, BLOCK), 0) < prefix
        for pair in range(pairs):
            cols = slice(pair * 128, pair * 128 + 128)
            turned = pk[:, cols].T
            ws, gs = [], []
            for head in (2 * pair, 2 * pair + 1):
                scores = dot(pk[:, cols], qs[head])
                weights = jnp.where(there, jnp.exp2(scores - lse[head : head + 1]), 0.0)
                grad = (weights * (dot(pv[:, cols], ds[head]) - delta[head])).astype(bf16)
                dq[head_rows(head)] += dot(turned[head_rows(head % 2)], grad)
                ws.append(weights.astype(bf16))
                gs.append(grad)
            dpv[:, cols] += dot(jnp.concatenate(ws, axis=1), d_stack[pair])
            dpk[:, cols] += dot(jnp.concatenate(gs, axis=1), q_stack[pair]) * LN2

    def tile(row, segment, edge):
        window = pl.ds(row, BLOCK)
        if edge:
            seen = pl.ds(segment, 1)
            open_ = allowed(row, start[seen, :], end[seen, :])
        scores = [dot(k[window, pair_cols(head)], qs[head]) for head in range(heads)]
        inner = [dot(v[window, pair_cols(head)], ds[head]) for head in range(heads)]
        for pair in range(pairs):
            cols = slice(pair * 128, pair * 128 + 128)
            ws, gs = [], []
            for head in (2 * pair, 2 * pair + 1):
                weights = jnp.exp2(scores[head] - lse[head : head + 1])
                if edge:
                    weights = jnp.where(open_, weights, 0.0)
                grad = (weights * (inner[head] - delta[head])).astype(bf16)
                dq[head_rows(head)] += dot(kt[head_rows(head), window], grad)
                ws.append(weights.astype(bf16))
                gs.append(grad)
            dv[window, cols] += dot(jnp.concatenate(ws, axis=1), d_stack[pair])
            dk[window, cols] += dot(jnp.concatenate(gs, axis=1), q_stack[pair])

    over_tiles(info, segments, block, tile)
    if own:
        dq_low[pl.ds(pl.multiple_of(block * BLOCK, BLOCK), BLOCK), :] = (
            (dq[...] * 0.125).T.astype(bf16)
        )
    elif final:
        dq_out[...] = (dq[...] * 0.125).T.astype(bf16)

    @pl.when(block == pl.num_programs(0) - 1)
    def _():
        least, most = info[4 * segments, 0], info[4 * segments + 1, 0]

        def project(row, size, piece, offset):
            window = pl.ds(row, size)
            target = pl.ds(offset, size)
            touched = (row < most) & (row + size > least)
            width = grads[piece][0].shape[1]

            @pl.when(touched)
            def _():
                place = row + lax.broadcasted_iota(jnp.int32, (size, dk.shape[1]), 0)
                there = (place >= least) & (place < most)
                dk_low = jnp.where(there, dk[window, :] * LN2, 0.0).astype(bf16)
                dv_low = jnp.where(there, dv[window, :], 0.0).astype(bf16)
                for core in range(cores):
                    part = owned(info, segments, cores, core, width)
                    value = dot_nt(dk_low, wk[part, :]) + dot_nt(dv_low, wv[part, :])
                    if own:
                        value += dot_nt(dq_low[target, :], wq[part, :])
                    grads[piece][core][target, :] = value.astype(bf16)

            @pl.when(jnp.logical_not(touched))
            def _():
                for core in range(cores):
                    value = jnp.zeros((size, width), f32)
                    if own:
                        part = owned(info, segments, cores, core, width)
                        value = dot_nt(dq_low[target, :], wq[part, :])
                    grads[piece][core][target, :] = value.astype(bf16)

        for piece in range(pieces):
            length = cuts[piece + 1] - cuts[piece]
            whole = length // BLOCK

            def step(i, carry, piece=piece):
                offset = pl.multiple_of(i * BLOCK, BLOCK)
                project(pl.multiple_of(cuts[piece] + offset, 128), BLOCK, piece, offset)
                return carry

            lax.fori_loop(0, whole, step, 0)
            rest = length - whole * BLOCK
            if rest:
                project(cuts[piece] + whole * BLOCK, rest, piece, whole * BLOCK)


def attend_back(
    query, d_out, out, keys, values, start, end, lse, info, key_weight, value_weight, cuts, cores,
    prefix=None, state=None, query_weight=None, final=False,
):
    rows, cols = query.shape
    window = cuts[-1] + (0 if query_weight is not None else PAD)
    width = key_weight.shape[0]
    heads = cols // HEAD_DIM
    own = query_weight is not None
    segments = start.shape[0]
    by_rows = pl.BlockSpec((BLOCK, cols), lambda b, info: (b, 0))
    by_lanes = lambda count: pl.BlockSpec((count, BLOCK), lambda b, info: (0, b))
    whole = lambda count, wide=cols: pl.BlockSpec((count, wide), lambda b, info: (0, 0))
    operands = [query, d_out, out, keys, values, start, end, lse, key_weight, value_weight]
    specs = [by_rows] * 3 + [whole(window)] * 2 + [by_lanes(segments)] * 2 + [by_lanes(heads)]
    specs += [whole(width)] * 2
    if prefix is not None:
        operands += [prefix[0], prefix[1]]
        specs += [whole(32), whole(32)]
    if state is not None:
        operands.append(state)
        specs.append(by_lanes(cols))
    if own:
        operands.append(query_weight)
        specs.append(whole(width))
    shape = jax.ShapeDtypeStruct
    outs, out_specs = [], []
    for piece in range(len(cuts) - 1):
        length = cuts[piece + 1] - cuts[piece]
        outs += [shape((length, width // cores), bf16)] * cores
        out_specs += [whole(length, width // cores)] * cores
    if prefix is not None:
        outs += [shape((32, cols), f32)] * 2
        out_specs += [whole(32)] * 2
    scratch = [
        pltpu.VMEM((cols, window), bf16),
        pltpu.VMEM((window, cols), f32),
        pltpu.VMEM((window, cols), f32),
    ]
    if own:
        scratch += [pltpu.VMEM((cols, BLOCK), f32), pltpu.VMEM((rows, cols), bf16)]
    elif final:
        scratch.append(pltpu.VMEM((cols, BLOCK), f32))
        outs.append(shape((rows, cols), bf16))
        out_specs.append(by_rows)
    else:
        outs.append(shape((cols, rows), f32))
        out_specs.append(by_lanes(cols))
    result = pl.pallas_call(
        functools.partial(
            attend_back_kernel,
            0 if prefix is None else prefix[2], state is not None, own, final, tuple(cuts), cores,
            segments,
        ),
        out_shape=tuple(outs),
        grid_spec=pltpu.PrefetchScalarGridSpec(
            num_scalar_prefetch=1,
            grid=(rows // BLOCK,),
            in_specs=specs,
            out_specs=tuple(out_specs),
            scratch_shapes=scratch,
        ),
        compiler_params=kernel_params(),
    )(info, *operands)
    pieces = [
        list(result[i * cores : i * cores + cores]) for i in range(len(cuts) - 1)
    ]
    return pieces, *result[(len(cuts) - 1) * cores :]


class Span(NamedTuple):
    segments: tuple
    step: int = 128
    causal: bool = True


def spans_kernel(spans, total, rows, tgt, mem, at, *refs):
    here, core = at[0], at[1]
    place = here + lax.broadcasted_iota(jnp.int32, (1, rows), 1)

    def one(j, carry):
        begin, mem_begin, start, mem_start, mem_end = carry
        end, mem_stop = begin + tgt[j], mem_begin + mem[j]
        past = place >= end
        start = jnp.where(past, end, start)
        mem_start = jnp.where(past, mem_stop, mem_start)
        mem_end = jnp.where(place >= begin, mem_stop, mem_end)
        return end, mem_stop, start, mem_start, mem_end

    zero = jnp.zeros((1, rows), jnp.int32)
    begin, _, start, mem_start, mem_end = lax.fori_loop(
        0, tgt.shape[0], one, (0, 0, zero, zero, zero)
    )
    mem_end = jnp.where(place >= begin, total, mem_end)
    blocks = rows // BLOCK

    def least(value, block):
        part = value[:, block * BLOCK : block * BLOCK + BLOCK].astype(f32)
        return jnp.min(part).astype(jnp.int32)

    def most(value, block):
        part = value[:, block * BLOCK : block * BLOCK + BLOCK].astype(f32)
        return jnp.max(part).astype(jnp.int32)

    ends = [
        [(least(value, b), most(value, b)) for b in range(blocks)]
        for value in (start - here, mem_start - here, mem_end - here)
    ]
    for i, span in enumerate(spans):
        starts_out, ends_out, info = refs[3 * i : 3 * i + 3]
        lowest, highest = 1 << 20, 0
        for segment, (base, low, high) in enumerate(span.segments):
            clip = lambda value: jnp.clip(value + base, low, high)
            if span.causal:
                lows, highs = start - here, place - here + 1
                corners = [(ends[0][b], (b * BLOCK + 1, b * BLOCK + BLOCK)) for b in range(blocks)]
            else:
                lows, highs = mem_start - here, mem_end - here
                corners = [(ends[1][b], ends[2][b]) for b in range(blocks)]
            starts_out[segment : segment + 1, :] = clip(lows)
            ends_out[segment : segment + 1, :] = clip(highs)
            for b, ((s0, s1), (e0, e1)) in enumerate(corners):
                s0, s1, e0, e1 = clip(s0), clip(s1), clip(e0), clip(e1)
                some = e1 > s0
                first = jnp.where(some, s0 // span.step * span.step, 0)
                count = jnp.where(some, (e1 - first + BLOCK - 1) // BLOCK, 0)
                from_ = jnp.clip((s1 - first + BLOCK - 1) // BLOCK, 0, count)
                to = jnp.clip((e0 - first) // BLOCK, from_, count)
                for row, value in enumerate((first, count, from_, to)):
                    info[4 * segment + row, b] = value
                lowest = jnp.where(some, jnp.minimum(lowest, first), lowest)
                highest = jnp.where(some, jnp.maximum(highest, first + count * BLOCK), highest)
        tail = 4 * len(span.segments)
        for b in range(blocks):
            info[tail, b] = jnp.minimum(lowest, highest)
            info[tail + 1, b] = highest
            info[tail + 2, b] = core
            info[tail + 3, b] = 0


def see(spans, total, rows, tgt, mem, at):
    outs, specs = [], []
    for span in spans:
        count = len(span.segments)
        outs += [jax.ShapeDtypeStruct((count, rows), jnp.int32)] * 2
        outs.append(jax.ShapeDtypeStruct((4 * count + 4, rows // BLOCK), jnp.int32))
        specs += [pl.BlockSpec((count, rows), lambda i, *scalars: (0, 0))] * 2
        specs.append(pl.BlockSpec(memory_space=pltpu.SMEM))
    result = pl.pallas_call(
        functools.partial(spans_kernel, spans, total, rows),
        out_shape=tuple(outs),
        grid_spec=pltpu.PrefetchScalarGridSpec(
            num_scalar_prefetch=3, grid=(1,), in_specs=[], out_specs=tuple(specs)
        ),
    )(tgt, mem, at)
    return [result[3 * i : 3 * i + 3] for i in range(len(spans))]


def norm_parts(value):
    center = value - jnp.mean(value, axis=-1, keepdims=True)
    scale = lax.rsqrt(jnp.mean(center * center, axis=-1, keepdims=True) + EPS)
    return center * scale, scale


def norm_back(normal, scale, grad):
    return scale * (
        grad
        - jnp.mean(grad, axis=-1, keepdims=True)
        - normal * jnp.mean(grad * normal, axis=-1, keepdims=True)
    )


def gelu_pair(value):
    size = jnp.abs(value)
    bell = jnp.exp(-0.5 * value * value)
    under = 1.0 + (0.3275911 * 0.7071067811865476) * size
    t = pl.reciprocal(under, approx=True)
    t = t * (2.0 - under * t)
    poly = ((((1.061405429 * t - 1.453152027) * t + 1.421413741) * t - 0.284496736) * t + 0.254829592) * t
    tail = 0.5 * poly * bell
    cdf = jnp.where(value >= 0, 1.0 - tail, tail)
    return value * cdf, cdf + value * (0.3989422804014327 * bell)


def ffn_kernel(cores, chunk, core, *refs):
    refs = list(refs)

    def take(count):
        taken = refs[:count]
        del refs[:count]
        return taken

    crossed = take(cores)
    cross_outs = take(cores)
    first, cot = take(2)
    downs = take(cores)
    biases = take(cores)
    ups = take(cores)
    (up_bias,) = take(1)
    hins, houts = take(2)
    cross_outs, downs, ups = ([ref.at[0] for ref in part] for part in (cross_outs, downs, ups))
    out, d_cross = take(2)
    d_crossed = take(cores)
    adapter_grads = take(cores)
    hin, hout, in_sem, out_sem, slope, bufs0, bufs1, branch, second, second_low, adapted, down_slope, low = refs
    per = hins.shape[2] // chunk
    count = per * cores
    adapt = downs[0].shape[1]

    def copies(j):
        c, i = divmod(j, per)
        part = pl.ds(i * chunk, chunk)
        return (
            pltpu.make_async_copy(hins.at[c, :, part], hin.at[j], in_sem.at[j]),
            pltpu.make_async_copy(houts.at[c, part, :], hout.at[j], out_sem.at[j]),
        )

    for j in range(count):
        for copy in copies(j):
            copy.start()
    total = first[...]
    for value, weight in zip(crossed, cross_outs):
        total = total + dot(value[...], weight[...])
    normal, scale2 = norm_parts(total)
    second[...] = normal
    second_low[...] = normal.astype(bf16)

    wide = 4.0 * up_bias[...]
    acc = jnp.zeros(branch.shape, f32)
    for c in range(cores):
        part = slice(c * adapt, (c + 1) * adapt)
        value, grad = gelu_pair(dot(second_low[...], downs[c][...]) + biases[c][...])
        adapted[:, part] = value.astype(bf16)
        down_slope[:, part] = grad
        acc = acc + dot(adapted[:, part], ups[c][...])
    branch[...] = 4.0 * acc + wide

    for j in range(count):
        for copy in copies(j):
            copy.wait()
    bufs0[...] = dot(second_low[...], hin[0])

    def forward(j, now, later):
        later[...] = dot(second_low[...], hin[jnp.minimum(j + 1, count - 1)])
        value, grad = gelu_pair(now[...])
        slope[j] = grad.astype(bf16)
        branch[...] += dot(value.astype(bf16), hout[j])

    def forward_two(i, _):
        forward(2 * i, bufs0, bufs1)
        forward(2 * i + 1, bufs1, bufs0)
        return 0

    lax.fori_loop(0, count // 2, forward_two, 0)
    normal, scale = norm_parts(second[...] + branch[...])
    out[...] = normal.astype(bf16)
    d_third = norm_back(normal, scale, cot[...].astype(f32))
    branch[...] = d_third
    low[...] = d_third.astype(bf16)
    up_sum = 4.0 * jnp.sum(low[...].astype(f32), axis=0, keepdims=True)
    line = lax.broadcasted_iota(jnp.int32, (16, up_sum.shape[1]), 0)

    def backward(j):
        value = (slope[j].astype(f32) * dot_nt(low[...], hout[j])).astype(bf16)
        branch[...] += dot_nt(value, hin[j])

    def backward_two(i, _):
        backward(2 * i)
        backward(2 * i + 1)
        return 0

    lax.fori_loop(0, count // 2, backward_two, 0)
    total = branch[...]
    for c in range(cores):
        part = slice(c * adapt, (c + 1) * adapt)
        value = (down_slope[:, part] * (4.0 * dot_nt(low[...], ups[c][...]))).astype(bf16)
        total = total + dot_nt(value, downs[c][...])
        adapter_grads[c][adapt : 2 * adapt, :] = dot_tn(value, second_low[...]).astype(bf16)
        adapter_grads[c][:adapt, :] = (4.0 * dot_tn(adapted[:, part], low[...])).astype(bf16)
        down_sum = jnp.sum(value.astype(f32), axis=0, keepdims=True)
        down_sum = jnp.concatenate(
            [down_sum, jnp.zeros((1, up_sum.shape[1] - adapt), f32)], axis=1
        )
        biases_low = jnp.where(line == 0, up_sum, jnp.where(line == 1, down_sum, 0.0))
        adapter_grads[c][2 * adapt :, :] = biases_low.astype(bf16)
    d_second = norm_back(second[...], scale2, total)
    d_cross[...] = d_second
    for result, weight in zip(d_crossed, cross_outs):
        result[...] = dot_nt(d_second.astype(bf16), weight[...]).astype(bf16)


def at_core(cores, rows, width):
    return pl.BlockSpec((rows, width), lambda i, core: (core[0], 0))


def down_from_core(cores, shape):
    def spec(k):
        return pl.BlockSpec(
            (1,) + shape, lambda i, core: (lax.rem(core[0] + cores - k, cores), 0, 0)
        )

    return [spec(k) for k in range(cores)]


def one_step(kernel, core, operands, specs, outs, scratch):
    whole = lambda shape: pl.BlockSpec(shape, lambda i, core: (0,) * len(shape))
    specs = [whole(op.shape) if spec is None else spec for op, spec in zip(operands, specs)]
    return pl.pallas_call(
        kernel,
        out_shape=tuple(outs),
        grid_spec=pltpu.PrefetchScalarGridSpec(
            num_scalar_prefetch=1,
            grid=(1,),
            in_specs=specs,
            out_specs=tuple(whole(out.shape) for out in outs),
            scratch_shapes=scratch,
        ),
        compiler_params=kernel_params(),
    )(core, *operands)


def feed_forward(core, crossed, crossed_others, cross_outs, first, cot, downs, biases, ups, up_bias, hins, houts):
    rows, width = first.shape
    cores, _, hidden = hins.shape
    adapt = downs.shape[2]
    heads = crossed.shape[1]
    chunk = min(512, hidden)
    count = cores * hidden // chunk
    hbm = pl.BlockSpec(memory_space=pl.ANY)
    operands = [crossed] + list(crossed_others)
    specs = [at_core(cores, rows, heads)] + [None] * (cores - 1)
    operands += [cross_outs] * cores + [first, cot]
    specs += down_from_core(cores, cross_outs.shape[1:]) + [None, at_core(cores, rows, width)]
    operands += [downs] * cores + [bias[None] for bias in biases] + [ups] * cores + [up_bias[None]]
    specs += down_from_core(cores, downs.shape[1:]) + [None] * cores
    specs += down_from_core(cores, ups.shape[1:]) + [None]
    operands += [hins, houts]
    specs += [hbm, hbm]
    shape = jax.ShapeDtypeStruct
    outs = (
        [shape((rows, width), bf16), shape((rows, width), f32)]
        + [shape((rows, heads), bf16)] * cores
        + [shape((2 * adapt + 16, width), bf16)] * cores
    )
    scratch = [
        pltpu.VMEM((count, width, chunk), bf16),
        pltpu.VMEM((count, chunk, width), bf16),
        pltpu.SemaphoreType.DMA((count,)),
        pltpu.SemaphoreType.DMA((count,)),
        pltpu.VMEM((count, rows, chunk), bf16),
        pltpu.VMEM((rows, chunk), f32),
        pltpu.VMEM((rows, chunk), f32),
        pltpu.VMEM((rows, width), f32),
        pltpu.VMEM((rows, width), f32),
        pltpu.VMEM((rows, width), bf16),
        pltpu.VMEM((rows, adapt * cores), bf16),
        pltpu.VMEM((rows, adapt * cores), f32),
        pltpu.VMEM((rows, width), bf16),
    ]
    result = one_step(
        functools.partial(ffn_kernel, cores, chunk), core, operands, specs, outs, scratch
    )
    at = 2 + cores
    return result[0], result[1], list(result[2:at]), list(result[at:])


def after_self_kernel(cores, core, *refs):
    refs = list(refs)
    attended, refs = refs[:cores], refs[cores:]
    outputs, refs = refs[:cores], refs[cores:]
    queries, refs = refs[:cores], refs[cores:]
    tokens, first, scale = refs[:3]
    total = tokens[...].astype(f32)
    for value, weight in zip(attended, outputs):
        total = total + dot(value[...], weight[0])
    normal, inverse = norm_parts(total)
    first[...] = normal
    scale[...] = inverse
    low = normal.astype(bf16)
    for result, weight in zip(refs[3:], queries):
        result[...] = (dot(low, weight[0]) * (0.125 * LOG2E)).astype(bf16)


def after_self(core, attended, attended_others, outputs, queries, tokens):
    cores, heads, width = outputs.shape
    rows = tokens.shape[0] // cores
    operands = [attended] + list(attended_others) + [outputs] * cores + [queries] * cores + [tokens]
    specs = [at_core(cores, rows, heads)] + [None] * (cores - 1)
    specs += down_from_core(cores, outputs.shape[1:]) + down_from_core(cores, queries.shape[1:])
    specs += [at_core(cores, rows, width)]
    shape = jax.ShapeDtypeStruct
    outs = [shape((rows, width), f32), shape((rows, 1), f32)] + [shape((rows, heads), bf16)] * cores
    result = one_step(
        functools.partial(after_self_kernel, cores), core, operands, specs, outs, []
    )
    return result[0], result[1], list(result[2:])


def before_self_kernel(cores, core, *refs):
    refs = list(refs)
    grads, refs = refs[:cores], refs[cores:]
    queries, refs = refs[:cores], refs[cores:]
    outputs, refs = refs[:cores], refs[cores:]
    d_cross, first, scale, kept = refs[:4]
    sent, refs = refs[4 : 3 + cores], refs[3 + cores :]
    d_attended, d_tokens = refs[:cores], refs[cores]
    total = d_cross[...]
    for value, weight in zip(grads, queries):
        total = total + dot_nt(value[...], weight[0])
    total = norm_back(first[...], scale[...], total)
    d_tokens[...] = total
    low = total.astype(bf16)
    for result, weight in zip(d_attended, outputs):
        result[...] = dot_nt(low, weight[0]).astype(bf16)
    width = kept.shape[1]
    for k, result in enumerate([kept] + sent):
        owner = lax.rem(core[0] + cores - k, cores)
        part = pl.ds(pl.multiple_of(owner * width, width), width)
        result[...] = d_tokens[:, part].astype(result.dtype)


def before_self(core, grads, grads_others, queries, outputs, d_cross, first, scale):
    cores, heads, width = outputs.shape
    rows = first.shape[0]
    operands = [grads] + list(grads_others) + [queries] * cores + [outputs] * cores
    operands += [d_cross, first, scale]
    specs = [at_core(cores, rows, heads)] + [None] * (cores - 1)
    specs += down_from_core(cores, queries.shape[1:]) + down_from_core(cores, outputs.shape[1:])
    specs += [None] * 3
    shape = jax.ShapeDtypeStruct
    outs = [shape((rows, width // cores), f32)] + [shape((rows, width // cores), bf16)] * (cores - 1)
    outs += [shape((rows, heads), bf16)] * cores
    result = one_step(
        functools.partial(before_self_kernel, cores), core, operands, specs, outs,
        [pltpu.VMEM((rows, width), f32)],
    )
    return list(result[:cores]), list(result[cores:])


def beside_kernel(core, *refs):
    which = pl.program_id(0)
    for k, part in enumerate(refs[:-1]):

        @pl.when(which == k)
        def _(part=part):
            refs[-1][...] = part[...].astype(f32)


def beside(core, parts):
    rows, width = parts[0].shape
    cores = len(parts)
    count = 2

    def part_spec(k):
        def place(which, block, core):
            return (jnp.where(which == k, block, jnp.where(which < k, 0, count - 1)), 0)

        return pl.BlockSpec((rows // count, width), place)

    return pl.pallas_call(
        beside_kernel,
        out_shape=jax.ShapeDtypeStruct((rows, cores * width), f32),
        grid_spec=pltpu.PrefetchScalarGridSpec(
            num_scalar_prefetch=1,
            grid=(cores, count),
            in_specs=[part_spec(k) for k in range(cores)],
            out_specs=pl.BlockSpec(
                (rows // count, width),
                lambda which, block, core: (block, lax.rem(core[0] + cores - which, cores)),
            ),
        ),
    )(core, *parts)


def add_kernel(count, each, cut, *refs):
    for i in range(count):
        total = refs[i * each][...].astype(f32)
        for ref in refs[i * each + 1 : i * each + each]:
            total = total + ref[...].astype(f32)
        if cut is None:
            refs[count * each + i][...] = total.astype(bf16)
        else:
            refs[each][...] = total[:cut].astype(bf16)
            refs[each + 1][...] = total[cut:]


def add_up(lists, cut=None):
    each = len(lists[0])
    shape = jax.ShapeDtypeStruct
    outs = [shape(parts[0].shape, bf16) for parts in lists]
    if cut is not None:
        rows, width = lists[0][0].shape
        outs = [shape((cut, width), bf16), shape((rows - cut, width), f32)]
    return pl.pallas_call(
        functools.partial(add_kernel, len(lists), each, cut),
        out_shape=tuple(outs),
        compiler_params=pltpu.CompilerParams(vmem_limit_bytes=60 << 20),
    )(*[part for parts in lists for part in parts])


SMALL = 48


def pack_kernel(count, *refs):
    parts, refs = refs[:count], refs[count:]
    keys, values, biases, out = refs
    rows = parts[0].shape[0]
    total = parts[0][...].astype(f32)
    for part in parts[1:]:
        total = total + part[...].astype(f32)
    out[:rows, :] = total.astype(bf16)
    out[rows : rows + 32, :] = jnp.zeros((32, out.shape[1]), bf16)
    cols = keys.shape[1]
    out[rows : rows + 32, :cols] = keys[...].astype(bf16)
    out[rows : rows + 32, cols : 2 * cols] = values[...].astype(bf16)
    out[rows + 32 :, :] = biases[...].astype(bf16)


def pack(parts, keys, values, biases):
    rows, width = parts[0].shape
    return pl.pallas_call(
        functools.partial(pack_kernel, len(parts)),
        out_shape=jax.ShapeDtypeStruct((rows + SMALL, width), bf16),
    )(*parts, keys, values, biases)


def gather_kernel(count, rows, last, place, *refs):
    parts, refs = refs[:count], refs[count:]
    total = parts[0][rows:, :].astype(f32)
    for part in parts[1:]:
        total = total + part[rows:, :].astype(f32)
    if last is None:
        (out,) = refs
        joined = out
        out[count * rows :, :] = total.astype(bf16)
    else:
        keys, values, down, down_bias, up, up_bias, joined = refs
        prefix, cols = keys.shape
        keys[...] = total[:prefix, :cols]
        values[...] = total[:prefix, cols : 2 * cols]
        up_bias[...] = total[32:33]
        down_bias[...] = total[33:34, : down_bias.shape[1]]
    for k, part in enumerate(parts):
        owner = jnp.bitwise_xor(place[0], k)
        joined[pl.ds(pl.multiple_of(owner * rows, 16), rows), :] = part[:rows, :]
    if last is not None:
        up[...] = joined[: up.shape[0], :].astype(f32)
        down[...] = joined[up.shape[0] :, :].astype(f32).T


def gather_rows(place, parts, last):
    count = len(parts)
    length, width = parts[0].shape
    rows = length - SMALL
    shape = jax.ShapeDtypeStruct
    if last is None:
        outs, scratch = [shape((count * rows + SMALL, width), bf16)], []
    else:
        prefix, cols, adapt = last
        outs = [
            shape((prefix, cols), f32),
            shape((prefix, cols), f32),
            shape((width, adapt), f32),
            shape((1, adapt), f32),
            shape((adapt, width), f32),
            shape((1, width), f32),
        ]
        scratch = [pltpu.VMEM((count * rows, width), bf16)]
    return one_step(
        functools.partial(gather_kernel, count, rows, last),
        place,
        parts,
        [None] * count,
        outs,
        scratch,
    )


def product(left, right):
    return jnp.dot(left, right, preferred_element_type=f32)


def turn(value, distance):
    size = lax.axis_size("head")
    return lax.ppermute(value, "head", [(i, (i + distance) % size) for i in range(size)])


def others(value):
    return [turn(value, k) for k in range(1, lax.axis_size("head"))]


def in_order(parts, axis):
    size = len(parts)
    core = lax.axis_index("head")
    if size == 2:
        first, second = parts
        return jnp.where(
            core == 0,
            jnp.concatenate([first, second], axis=axis),
            jnp.concatenate([second, first], axis=axis),
        )
    ring = jnp.concatenate([parts[-k % size] for k in range(size)] * 2, axis=axis)
    length = parts[0].shape[axis]
    return lax.dynamic_slice_in_dim(ring, (size - core) % size * length, size * length, axis)


def shift(value, distance):
    devices = range(lax.axis_size("seq"))
    return lax.ppermute(value, "seq", [(i, i + distance) for i in devices if i + distance in devices])


def after(value, *first):
    return lax.optimization_barrier((value, first))[0]


class Ring:
    def __init__(self, size, step):
        self.size, self.step = size, step
        self.place = lax.axis_index("seq") // step % size

    def exchange(self, values):
        pairs = [[(i, i ^ k * self.step) for i in range(lax.axis_size("seq"))] for k in range(self.size)]
        return [lax.ppermute(values[k], "seq", pairs[k]) for k in range(1, self.size)]

    def cut(self, value, k):
        length = value.shape[0] // self.size
        return lax.dynamic_slice_in_dim(value, (self.place ^ k) * length, length, 0)

    def scatter(self, value):
        return self.exchange([self.cut(value, k) for k in range(self.size)])


def on_device(
    tokens,
    memory,
    cotangent,
    tgt_lengths,
    mem_lengths,
    self_query,
    self_key,
    self_value,
    self_output,
    cross_query,
    cross_key,
    cross_value,
    cross_output,
    hidden_in,
    hidden_out,
    prefix_keys,
    prefix_values,
    adapter_down,
    adapter_down_bias,
    adapter_up,
    adapter_up_bias,
):
    rows, width = tokens.shape
    cols = self_query.shape[1]
    prefix = prefix_keys.shape[0]
    shards = lax.axis_size("seq")
    position = lax.axis_index("seq")
    core = lax.axis_index("head")
    cores = lax.axis_size("head")
    total = rows * shards
    core_index = jnp.reshape(core, (1,)).astype(jnp.int32)

    def part_of(value, owner, axis=0):
        length = value.shape[axis] // cores
        return lax.dynamic_slice_in_dim(value, owner % cores * length, length, axis)

    def mine(value, axis=0):
        return part_of(value, core, axis)

    def dealt(parts):
        return [parts[0]] + [turn(parts[k], -k) for k in range(1, cores)]

    def over_cores(parts):
        arrived = [part.astype(f32) for part in dealt(parts)]
        return sum(arrived[1:], arrived[0])

    self_far = min(max(-(-(SEQ_MAX - rows) // 128) * 128, 0), rows)
    cross_far = min(max(-(-(SEQ_MAX + DRIFT - rows) // 128) * 128, 0), rows)
    self_base = rows + self_far
    far_rows = 2 * cross_far
    at = jnp.stack([position * rows, core]).astype(jnp.int32)
    self_seen, own_seen, halo_seen, main_seen, far_seen = see(
        (
            Span(((self_base, 0, self_base + rows),)),
            Span(((0, 0, rows),), BLOCK),
            Span(((self_base, 0, self_base),)),
            Span(((rows, 0, 3 * rows),), causal=False),
            Span(
                ((rows + cross_far, 0, cross_far), (cross_far - 2 * rows, cross_far, far_rows)),
                causal=False,
            ),
        ),
        total,
        rows,
        tgt_lengths,
        mem_lengths,
        at,
    )

    tokens_cols = mine(tokens, 1)
    tokens_end = tokens_cols[rows - self_far :]
    token_near = shift(tokens_cols, 1)
    token_far = shift(tokens_end, 2)
    down_biases = [adapter_down_bias] + others(adapter_down_bias)

    prefix_pad = ((0, 32 - prefix), (0, 0))
    prefix_rows = (
        jnp.pad(prefix_keys.astype(bf16), prefix_pad),
        jnp.pad(prefix_values.astype(bf16), prefix_pad),
        prefix,
    )

    query = (product(tokens, self_query) * (0.125 * LOG2E)).astype(bf16)

    own_keys = product(tokens, self_key).astype(bf16)
    own_values = product(tokens, self_value).astype(bf16)

    def all_cores(value, *first):
        return lax.all_gather(after(value, *first), "head", axis=0)

    self_outputs = all_cores(self_output, query)
    cross_queries = all_cores(cross_query, query)
    arrived = (token_near, token_far)
    ready = (query, own_keys, own_values, self_seen)
    arrived, ready = lax.optimization_barrier((arrived, ready))
    token_near, token_far = arrived
    query, own_keys, own_values, self_seen = ready
    memory_late = after(memory, token_near)
    memory_cols = mine(memory_late, 1)
    memory_keys = product(memory_late, cross_key).astype(bf16)
    memory_values = product(memory_late, cross_value).astype(bf16)

    token_near = [token_near] + others(token_near)
    token_far = [token_far] + others(token_far)
    memory_near = (
        shift(after(memory_cols, token_near, token_far), 1),
        shift(after(memory_cols, token_near, token_far), -1),
    )
    attended, self_lse, self_keys, self_values = attend(
        after(query, memory_keys, memory_values),
        [Rows(token_far, self_far), Rows(token_near, rows), (own_keys, own_values)],
        None,
        *self_seen,
        prefix_rows,
        None,
        True,
        (self_key, self_value),
    )

    def to_rows(value):
        return [turn(part_of(value, core + k), k) for k in range(1, cores)]

    def to_heads(parts):
        parts = [parts[0]] + [turn(parts[k], -k) for k in range(1, cores)]
        return in_order([parts[-k % cores] for k in range(cores)], 0)

    cross_outputs = all_cores(cross_output, memory_keys)
    hidden_ins = all_cores(hidden_in, memory_keys)
    hidden_outs = all_cores(hidden_out, memory_keys)
    downs = all_cores(after(adapter_down, memory_keys).astype(bf16))
    ups = all_cores(after(adapter_up, memory_keys).astype(bf16))
    attended_rows = to_rows(attended)
    attended_rows, memory_near = lax.optimization_barrier((attended_rows, memory_near))
    memory_near = [[part] + others(part) for part in memory_near]
    memory_far = (
        shift(after(memory_cols[rows - cross_far :], memory_near), 2),
        shift(after(memory_cols[:cross_far], memory_near), -2),
    )
    first, first_scale, cross_q = after_self(
        core_index, attended, attended_rows, self_outputs, cross_queries, tokens
    )

    cross_q = to_heads(cross_q)
    *state, main_keys, main_values = attend(
        cross_q,
        [Rows(memory_near[0], rows), (memory_keys, memory_values), Rows(memory_near[1], rows)],
        None,
        *main_seen,
        None,
        None,
        False,
        (cross_key, cross_value),
    )
    state, memory_far = lax.optimization_barrier((state, memory_far))
    memory_far = [Rows([part] + others(part), cross_far) for part in memory_far]
    crossed, cross_lse, far_keys, far_values = attend(
        cross_q, memory_far, None, *far_seen, None, state, True, (cross_key, cross_value)
    )

    (
        outputs_rows,
        d_cross,
        d_crossed,
        adapter_grads,
    ) = feed_forward(
        core_index,
        crossed,
        to_rows(crossed),
        cross_outputs,
        first,
        cotangent,
        downs,
        down_biases,
        ups,
        adapter_up_bias,
        hidden_ins,
        hidden_outs,
    )
    d_crossed = to_heads(d_crossed)
    adapter_grads = dealt(after(adapter_grads, d_crossed))
    ups_count = adapter_up.shape[0]
    staged = shards % 4 == 0 and shards & (shards - 1) == 0 and 2 * ups_count % shards == 0
    if staged:
        plane, column = Ring(4, 1), Ring(shards // 4, 4)

    far_grads, query_state = attend_back(
        cross_q, d_crossed, crossed, far_keys, far_values, *far_seen[:2], cross_lse, far_seen[2],
        cross_key, cross_value, (0, cross_far, 2 * cross_far), cores,
    )
    far_grads, query_state, adapter_grads = lax.optimization_barrier(
        (far_grads, query_state, adapter_grads)
    )
    far_parts = [dealt(part) for part in far_grads]
    adapter_grads, bias_grads = add_up([adapter_grads], 2 * ups_count)
    if staged:
        adapter_arrived = plane.scatter(adapter_grads)
        adapter_kept = plane.cut(adapter_grads, 0)
    far_low = add_up(after(far_parts, adapter_grads))
    far_arrived = (shift(far_low[0], -2), shift(far_low[1], 2))
    query_state = after(query_state, far_low)
    near_grads, cross_q_grad = attend_back(
        cross_q, d_crossed, crossed, main_keys, main_values, *main_seen[:2], cross_lse,
        main_seen[2], cross_key, cross_value, (0, rows, 2 * rows, 3 * rows), cores, None, query_state, None,
        True,
    )
    far_arrived, near_grads, cross_q_grad = lax.optimization_barrier(
        (far_arrived, near_grads, cross_q_grad)
    )
    if staged:
        adapter_arrived, cross_q_grad = lax.optimization_barrier((adapter_arrived, cross_q_grad))
    grads_rows = to_rows(cross_q_grad)
    near_parts = [dealt(after(part, grads_rows)) for part in near_grads]
    d_tokens, d_attended = before_self(
        core_index, cross_q_grad, grads_rows, cross_queries, self_outputs, d_cross, first,
        first_scale,
    )
    d_attended = to_heads(d_attended)
    near_low = add_up(after([near_parts[0], near_parts[2]], d_attended))
    near_arrived = (shift(near_low[0], -1), shift(near_low[1], 1))
    outputs_other = others(after(outputs_rows, near_low))
    d_tokens_cols = to_heads(after(d_tokens, near_low))
    d_attended = after(d_attended, near_low)

    halo_grads, prefix_key_grad, prefix_value_grad, query_state = attend_back(
        query, d_attended, attended, self_keys, self_values, *halo_seen[:2], self_lse, halo_seen[2],
        self_key, self_value, (0, self_far, self_base), cores, prefix_rows,
    )
    halo_grads, query_state, near_arrived, outputs_other, d_tokens_cols = lax.optimization_barrier(
        (halo_grads, query_state, near_arrived, outputs_other, d_tokens_cols)
    )
    halo_parts = [dealt(part) for part in halo_grads]
    if staged:
        (adapter_grads,) = add_up([[adapter_kept] + after(adapter_arrived, query_state)])
        adapter_arrived = column.scatter(adapter_grads)
        adapter_kept = column.cut(adapter_grads, 0)
        halo_parts = after(halo_parts, adapter_grads)
    halo_low = add_up(halo_parts)
    halo_arrived = (shift(halo_low[0], -2), shift(halo_low[1], -1))
    pad = ((rows - cross_far, 0), (0, 0))
    back = ((0, rows - cross_far), (0, 0))
    near_own, near_arrived, far_arrived, outputs_rows, outputs_other = after(
        (near_parts[1], near_arrived, far_arrived, outputs_rows, outputs_other), halo_low
    )
    memory_sum = sum(
        [part.astype(f32) for part in near_own + list(near_arrived)],
        jnp.pad(far_arrived[0], pad).astype(f32) + jnp.pad(far_arrived[1], back).astype(f32),
    ).astype(bf16)
    outputs = in_order([outputs_rows] + outputs_other, 0)
    query_state = after(query_state, halo_low, memory_sum, outputs)
    ((here_grads,),) = attend_back(
        query, d_attended, attended, own_keys, own_values, *own_seen[:2], self_lse, own_seen[2],
        self_key, self_value, (0, rows), cores, None, query_state, self_query,
    )
    here_grads, halo_arrived, memory_sum = lax.optimization_barrier(
        (here_grads, halo_arrived, memory_sum)
    )
    if staged:
        adapter_arrived, here_grads = lax.optimization_barrier((adapter_arrived, here_grads))
    here_sum = over_cores(here_grads)
    memory_other = others(after(memory_sum, here_sum))
    kept = [adapter_kept] + adapter_arrived if staged else [adapter_grads]
    both = pack(kept, prefix_key_grad, prefix_value_grad, bias_grads)
    if staged:
        both_arrived = column.exchange([both] * column.size)
    grad_memory = beside(core_index, [memory_sum] + memory_other)
    token_sum = (
        d_tokens_cols.astype(f32)
        + here_sum
        + jnp.pad(halo_arrived[0], ((rows - self_far, 0), (0, 0))).astype(f32)
        + halo_arrived[1].astype(f32)
    ).astype(bf16)
    token_other = others(token_sum)
    grad_tokens = beside(core_index, [token_sum] + token_other)
    if staged:
        place = jnp.reshape(column.place, (1,)).astype(jnp.int32)
        (both,) = gather_rows(place, [both] + both_arrived, None)
        parts = [both] + plane.exchange([both] * plane.size)
        place = jnp.reshape(plane.place, (1,)).astype(jnp.int32)
    else:
        parts, place = [lax.psum(both, "seq")], core_index * 0
    parts = after(parts, grad_tokens)
    sizes = (prefix, cols, ups_count)
    prefix_k, prefix_v, grad_down, grad_down_bias, grad_up, grad_up_bias = gather_rows(place, parts, sizes)
    return (
        outputs,
        grad_tokens,
        grad_memory,
        prefix_k,
        prefix_v,
        grad_down,
        grad_down_bias[0],
        grad_up,
        grad_up_bias[0],
    )


def solution(mesh):
    in_specs = (
        P("seq", None),
        P("seq", None),
        P("seq", None),
        P(),
        P(),
        P(None, "head"),
        P(None, "head"),
        P(None, "head"),
        P("head", None),
        P(None, "head"),
        P(None, "head"),
        P(None, "head"),
        P("head", None),
        P(None, "head"),
        P("head", None),
        P(None, "head"),
        P(None, "head"),
        P(None, "head"),
        P("head"),
        P("head", None),
        P(),
    )
    out_specs = (
        P("seq", None),
        P("seq", None),
        P("seq", None),
        P(None, "head"),
        P(None, "head"),
        P(None, "head"),
        P("head"),
        P("head", None),
        P(),
    )
    return jax.shard_map(
        on_device, mesh=mesh, in_specs=in_specs, out_specs=out_specs, check_vma=False
    )
```

time: 1750 us -> 573 us (0.33)
  matrix products: 869 us -> 13.1 us
  other arithmetic: 432 us -> 21.8 us
  Pallas kernels: 0 us -> 222 us
  blocking collectives: 105 us -> 0 us
  waiting for transfers between devices: 217 us -> 160 us
  starting transfers between devices: 65 us -> 108 us
    dot_general x169 -> x5, matrix products: 869 us -> 13.1 us  [product(): return jnp.dot(left, right, preferred_element_type=f32)]
    convert_element_type x35 -> x7, other arithmetic: 238 us -> 8.89 us  [the longest x1 3.6 us: on_device(): memory_sum = sum([part.astype(f32) for part in near_own + list(near_arriv...]
    pallas_call x0 -> x21, Pallas kernels: none -> 222 us  [the longest x4 81.1 us: attend_back(): pl.pallas_call(functools.partial(attend_back_kernel, 0 if prefix is None...]
    reduce_sum x39 -> x0, other arithmetic: 160 us -> none  [the longest x16 124 us: attend(): row_total = jnp.sum(weights, axis=1, keepdims=True)]
    psum x1 -> x0, blocking collectives: 105 us -> none  [on_device(): lax.psum(prefix_key_grad.astype(jnp.bfloat16), 'seq').astype(jnp.float32)]
    psum x7 -> x0, waiting for transfers between devices: 97 us -> none  [the longest x1 29.1 us: on_device(): lax.psum(product(attended, self_output).astype(jnp.bfloat16), 'head')]
    ppermute x20 -> x50, starting transfers between devices: 64.5 us -> 108 us  [the longest x12 58.2 us: exchange(): lax.ppermute(values[k], 'seq', pairs[k])]
    ppermute x20 -> x50, waiting for transfers between devices: 120 us -> 158 us  [the longest x12 88.2 us: shift(): lax.ppermute(value, 'seq', [(i, i + distance) for i in devices if i + dis...]
  transfers between devices with their start and end apart: 27 -> 57, of which waited for: 7 -> 27; matrix products, arithmetic and copies ran while one was open for 45% -> 7% of each run, Pallas kernels for 0% -> 30%
where the time goes in v1:
time: 573 us; the launch traced here: 562 us
  Pallas kernels  222 us (39%)
  waiting for transfers between devices  160 us (28%)
  starting transfers between devices  108 us (19%)
  local copies, waits for them, and re-layouts  22.2 us (4%)
  other arithmetic  21.8 us (4%)
  between operations  15.3 us (3%)
  matrix products  13.1 us (2%)
    ppermute x12, waiting for transfers between devices, shift(): lax.ppermute(value, 'seq', [(i, i + distance) for i in devices if i + dis...  88.2 us
    pallas_call x4, Pallas kernels, attend_back(): pl.pallas_call(functools.partial(attend_back_kernel, 0 if prefix is None...  81.1 us
    pallas_call x5, Pallas kernels, one_step(): pl.pallas_call(kernel, out_shape=tuple(outs), grid_spec=pltpu.PrefetchSca...  61 us
    ppermute x12, starting transfers between devices, exchange(): lax.ppermute(values[k], 'seq', pairs[k])  58.2 us
    pallas_call x3, Pallas kernels, attend(): pl.pallas_call(functools.partial(attend_kernel, 0 if prefix is None else...  50.3 us
    ppermute x12, starting transfers between devices, shift(): lax.ppermute(value, 'seq', [(i, i + distance) for i in devices if i + dis...  44.3 us
    ppermute x12, waiting for transfers between devices, exchange(): lax.ppermute(values[k], 'seq', pairs[k])  43.9 us
    ppermute x26, waiting for transfers between devices, turn(): lax.ppermute(value, 'head', [(i, (i + distance) % size) for i in range(si...  25.4 us
  transfers between devices with their start and end apart: 57, of which 27 were waited for; matrix products, arithmetic and copies ran while one was open for 7% of the time, Pallas kernels for 30%

profile of v1, /device:TPU:0, one launch (start us, length us, event | category | flops | bytes accessed | tf_op | source)
XLA Modules:
  0.0 562.3 jit_solution(11097562312554933532)
XLA Ops:
  7.2 4.1 multiply_convert_fusion.refs_0_
  14.0 5.9 %collective-permute-start = (bf16[1024,512]{1,0:T(8,128)(2,1)}, bf16[1024,512]{1,0:T(8,128)(2,1)}, u32[]{:S(2)}, u32[]{:S(2)}) collective-permute-start(bf16[1024,512]{1,0:T(8,128)(2,1)} %constant_dynamic-slice_fusion.13), channel_id=1, source_target_pairs={{0,2},{2,4},{4,6},{6,8},{8,10},{10,12},{12,14},{14,16},{16,18},{18... | collective-permute-start | bytes 3145736 | tf_op jit(solution)/shard_map/ppermute | solution.py:1101
  32.1 27.2 %collective-permute-done.1.refs_5_ = bf16[768,512]{1,0:T(8,128)(2,1)} collective-permute-done((bf16[768,512]{1,0:T(8,128)(2,1)}, bf16[768,512]{1,0:T(8,128)(2,1)}, u32[]{:S(2)}, u32[]{:S(2)}) %collective-permute-start.1) | collective-permute-done | bytes 786464 | tf_op jit(solution)/shard_map/ppermute | solution.py:1101
  77.1 19.8 %shard_map.269 = (bf16[1024,512]{1,0:T(8,128)(2,1)}, f32[8,1024]{1,0:T(8,128)}, bf16[2944,512]{1,0:T(8,128)(2,1)}, bf16[2944,512]{1,0:T(8,128)(2,1)}) custom-call(s32[8,4]{1,0:T(8,128)} %get-tuple-element.199.info, bf16[1024,512]{1,0:T(8,128)(2,1)} %multiply_convert_fusion.refs_0_, s32[1,1024]{1,0:T(1,128)} %get-tuple-element.204.refs_1_, ...), custom_call_target="tpu_custom_call" | custom-call | tf_op jit(solution)/shard_map/pallas_call | solution.py:326
  100.0 17.1 %collective-permute-done.5.refs_5_ = bf16[1024,512]{1,0:T(8,128)(2,1)} collective-permute-done((bf16[1024,512]{1,0:T(8,128)(2,1)}, bf16[1024,512]{1,0:T(8,128)(2,1)}, u32[]{:S(2)}, u32[]{:S(2)}) %collective-permute-start.5) | collective-permute-done | bytes 1048608 | tf_op jit(solution)/shard_map/ppermute | solution.py:1101
  117.1 4.7 collective-permute-done.6.refs_9_
  127.7 14.6 %collective-permute-start.10 = (bf16[896,512]{1,0:T(8,128)(2,1)}, bf16[896,512]{1,0:T(8,128)(2,1)S(1)}, u32[]{:S(2)}, u32[]{:S(2)}) collective-permute-start(bf16[896,512]{1,0:T(8,128)(2,1)} %get-tuple-element.226), channel_id=1, source_target_pairs={{0,4},{2,6},{4,8},{6,10},{8,12},{10,14},{12,16},{14,18},{16,20},{1... | collective-permute-start | bytes 2752520 | tf_op jit(solution)/shard_map/ppermute | solution.py:1101
  142.4 6.7 %shard_map.270 = (f32[512,1024]{1,0:T(8,128)}, f32[512,1]{1,0:T(8,128)}, bf16[512,512]{1,0:T(8,128)(2,1)}, bf16[512,512]{1,0:T(8,128)(2,1)}) custom-call(s32[1]{0:T(128)} %bitcast.1.core, bf16[1024,512]{1,0:T(8,128)(2,1)} %get-tuple-element.209.refs_0_.refs_2_, bf16[512,512]{1,0:T(8,128)(2,1)} %copy-done.30, bf16[2,512,1024]{2,1,0:T(8,128)(2,1)} %bitcast.26, ...), custom_call_target="tpu_custom_call" | custom-call | tf_op jit(solution)/shard_map/pallas_call | solution.py:800
  153.9 22.2 %shard_map.271 = (f32[8,1024]{1,0:T(8,128)}, f32[8,1024]{1,0:T(8,128)}, f32[512,1024]{1,0:T(8,128)}, bf16[3200,512]{1,0:T(8,128)(2,1)}, bf16[3200,512]{1,0:T(8,128)(2,1)}) custom-call(s32[8,4]{1,0:T(8,128)} %get-tuple-element.218.info, bf16[1024,512]{1,0:T(8,128)(2,1)} %maximum_select_fusion.2.refs_0_, s32[1,1024]{1,0:T(1,128)} %get-tuple-element.219.refs_1_.refs_5_, ...), custom_call_target="tpu_custom_call" | custom-call | tf_op jit(solution)/shard_map/pallas_call | solution.py:326
  176.2 5.1 collective-permute-done.10.refs_5_
  186.1 8.3 %shard_map.272 = (bf16[1024,512]{1,0:T(8,128)(2,1)}, f32[8,1024]{1,0:T(8,128)}, bf16[1920,512]{1,0:T(8,128)(2,1)}, bf16[1920,512]{1,0:T(8,128)(2,1)}) custom-call(s32[12,4]{1,0:T(8,128)} %get-tuple-element.195.info, bf16[1024,512]{1,0:T(8,128)(2,1)} %maximum_select_fusion.2.refs_0_, s32[2,1024]{1,0:T(2,128)} %get-tuple-element.216.refs_1_.refs_5_, ...), custom_call_target="tpu_custom_call" | custom-call | tf_op jit(solution)/shard_map/pallas_call | solution.py:326
  198.3 41.6 %shard_map.273 = (bf16[512,1024]{1,0:T(8,128)(2,1)}, f32[512,1024]{1,0:T(8,128)}, bf16[512,512]{1,0:T(8,128)(2,1)}, bf16[512,512]{1,0:T(8,128)(2,1)}, bf16[528,1...) custom-call(s32[1]{0:T(128)} %bitcast.1.core, bf16[1024,512]{1,0:T(8,128)(2,1)} %get-tuple-element.233.refs_0_.refs_2_, ...), custom_call_target="tpu_custom_call" | custom-call | tf_op jit(solution)/shard_map/pallas_call | solution.py:800
  244.8 9.4 %shard_map.274 = (bf16[896,512]{1,0:T(8,128)(2,1)}, bf16[896,512]{1,0:T(8,128)(2,1)}, bf16[896,512]{1,0:T(8,128)(2,1)}, bf16[896,512]{1,0:T(8,128)(2,1)}, f32[512,1024]{1,0:T(8,128)}) custom-call(s32[12,4]{1,0:T(8,128)} %get-tuple-element.195.info, bf16[1024,512]{1,0:T(8,128)(2,1)} %maximum_select_fusion.2.refs_0_, ...), custom_call_target="tpu_custom_call" | custom-call | tf_op jit(solution)/shard_map/pallas_call | solution.py:541
  264.1 5.0 collective-permute-start.21
  274.6 35.4 %shard_map.277 = (bf16[1024,512]{1,0:T(8,128)(2,1)}, bf16[1024,512]{1,0:T(8,128)(2,1)}, bf16[1024,512]{1,0:T(8,128)(2,1)}, bf16[1024,512]{1,0:T(8,128)(2,1)}, bf...) custom-call(s32[8,4]{1,0:T(8,128)} %get-tuple-element.218.info, ...), custom_call_target="tpu_custom_call" | custom-call | tf_op jit(solution)/shard_map/pallas_call | solution.py:541
  310.1 3.6 collective-permute-done.21
  313.7 5.5 collective-permute-done.23.refs_2_
  323.3 7.8 %shard_map.278 = (f32[512,512]{1,0:T(8,128)}, bf16[512,512]{1,0:T(8,128)(2,1)}, bf16[512,512]{1,0:T(8,128)(2,1)}, bf16[512,512]{1,0:T(8,128)(2,1)}) custom-call(s32[1]{0:T(128)} %bitcast.1.core, bf16[1024,512]{1,0:T(8,128)(2,1)} %get-tuple-element.281.refs_0_, bf16[512,512]{1,0:T(8,128)(2,1)} %copy-done.31, bf16[2,1024,512]{2,1,0:T(8,128)(2,1)} %bitcast.32, ...), custom_call_target="tpu_custom_call" | custom-call | tf_op jit(solution)/shard_map/pallas_call | solution.py:800
  337.8 3.8 shard_map.279
  343.0 5.5 collective-permute-start.31
  348.5 12.5 %shard_map.280 = (bf16[768,512]{1,0:T(8,128)(2,1)}, bf16[768,512]{1,0:T(8,128)(2,1)}, bf16[1024,512]{1,0:T(8,128)(2,1)}, bf16[1024,512]{1,0:T(8,128)(2,1)}, f32[...) custom-call(s32[8,4]{1,0:T(8,128)} %get-tuple-element.284.info, ...), custom_call_target="tpu_custom_call" | custom-call | tf_op jit(solution)/shard_map/pallas_call | solution.py:541
  362.6 7.3 %collective-permute-done.30 = bf16[1024,512]{1,0:T(8,128)(2,1)} collective-permute-done((bf16[1024,512]{1,0:T(8,128)(2,1)}, bf16[1024,512]{1,0:T(8,128)(2,1)}, u32[]{:S(2)}, u32[]{:S(2)}) %collective-permute-start.30) | collective-permute-done | bytes 1048608 | tf_op jit(solution)/shard_map/ppermute | solution.py:1101
  369.9 23.1 %collective-permute-done.31 = bf16[1024,512]{1,0:T(8,128)(2,1)} collective-permute-done((bf16[1024,512]{1,0:T(8,128)(2,1)}, bf16[1024,512]{1,0:T(8,128)(2,1)}, u32[]{:S(2)}, u32[]{:S(2)}) %collective-permute-start.31) | collective-permute-done | bytes 1048608 | tf_op jit(solution)/shard_map/ppermute | solution.py:1101
  405.0 21.2 %collective-permute-start.36 = (bf16[32,1024]{1,0:T(8,128)(2,1)S(1)}, bf16[32,1024]{1,0:T(8,128)(2,1)S(1)}, u32[]{:S(2)}, u32[]{:S(2)}) collective-permute-start(bf16[32,1024]{1,0:T(8,128)(2,1)S(1)} %get-tuple-element.390), channel_id=1, source_target_pairs={{0,8},{2,10},{4,12},{6,14},{8,0},{10,2},{12,4},{14,6},{16,24},{18,... | collective-permute-start | bytes 196616 | tf_op jit(solution)/shard_map/ppermute | solution.py:1115
  426.2 24.5 %collective-permute-start.37 = (bf16[32,1024]{1,0:T(8,128)(2,1)S(1)}, bf16[32,1024]{1,0:T(8,128)(2,1)S(1)}, u32[]{:S(2)}, u32[]{:S(2)}) collective-permute-start(bf16[32,1024]{1,0:T(8,128)(2,1)S(1)} %get-tuple-element.389), channel_id=1, source_target_pairs={{0,16},{2,18},{4,20},{6,22},{8,24},{10,26},{12,28},{14,30},{16,0},... | collective-permute-start | bytes 196616 | tf_op jit(solution)/shard_map/ppermute | solution.py:1115
  455.3 4.2 maximum_select_fusion.1
  459.5 23.7 %shard_map.283 = (bf16[1024,512]{1,0:T(8,128)(2,1)}, bf16[1024,512]{1,0:T(8,128)(2,1)}) custom-call(s32[8,4]{1,0:T(8,128)} %get-tuple-element.345.info, bf16[1024,512]{1,0:T(8,128)(2,1)} %multiply_convert_fusion.refs_0_, bf16[1024,512]{1,0:T(8,128)(2,1)} %maximum_select_fusion.4.refs_1_, bf16[1024,512]{1,0:T(8,128)(2,1)} %get-tuple-element.209.refs_0_.refs_2_, ...), custom_call_target="tpu_custom_call" | custom-call | tf_op jit(solution)/shard_map/pallas_call | solution.py:541
  485.6 21.5 %collective-permute-done.38.refs_3_ = bf16[32,1024]{1,0:T(8,128)(2,1)S(1)} collective-permute-done((bf16[32,1024]{1,0:T(8,128)(2,1)S(1)}, bf16[32,1024]{1,0:T(8,128)(2,1)S(1)}, u32[]{:S(2)}, u32[]{:S(2)}) %collective-permute-start.38) | collective-permute-done | bytes 65568 | tf_op jit(solution)/shard_map/ppermute | solution.py:1115
  524.0 7.3 %collective-permute-done.45.refs_2_ = bf16[80,1024]{1,0:T(8,128)(2,1)S(1)} collective-permute-done((bf16[80,1024]{1,0:T(8,128)(2,1)}, bf16[80,1024]{1,0:T(8,128)(2,1)S(1)}, u32[]{:S(2)}, u32[]{:S(2)}) %collective-permute-start.45) | collective-permute-done | bytes 163872 | tf_op jit(solution)/shard_map/ppermute | solution.py:1115
  537.5 4.5 shard_map.285
  542.9 4.5 shard_map.284
  547.4 3.8 collective-permute-done.48.refs_2_
  (239 shorter events, 135.3 us)
Async XLA Ops:
  7.2 135.2 %all-gather.15.cloned.1.call-start = ((), (), s32[]{:S(2)}) async-start(), calls=%async_computation | async-start | bytes 3145728 | tf_op jit(solution)/shard_map/all_gather | solution.py:1214
  11.3 131.1 %all-gather.17.cloned.1.call-start = ((), (), s32[]{:S(2)}) async-start(), calls=%async_computation.1 | async-start | bytes 3145728 | tf_op jit(solution)/shard_map/all_gather | solution.py:1214
  12.1 185.4 %all-gather.21.cloned.1.call-start = ((), (), s32[]{:S(2)}) async-start(), calls=%async_computation.3 | async-start | bytes 1572864 | tf_op jit(solution)/shard_map/all_gather | solution.py:1214
  14.0 45.3 %collective-permute-start = (bf16[1024,512]{1,0:T(8,128)(2,1)}, bf16[1024,512]{1,0:T(8,128)(2,1)}, u32[]{:S(2)}, u32[]{:S(2)}) collective-permute-start(bf16[1024,512]{1,0:T(8,128)(2,1)} %constant_dynamic-slice_fusion.13), channel_id=1, source_target_pairs={{0,2},{2,4},{4,6},{6,8},{8,10},{10,12},{12,14},{14,16},{16,18},{18... | collective-permute-start | bytes 3145736 | tf_op jit(solution)/shard_map/ppermute | solution.py:1101
  20.8 38.5 %collective-permute-start.1 = (bf16[768,512]{1,0:T(8,128)(2,1)}, bf16[768,512]{1,0:T(8,128)(2,1)}, u32[]{:S(2)}, u32[]{:S(2)}) collective-permute-start(bf16[768,512]{1,0:T(8,128)(2,1)} %dynamic-slice), channel_id=1, source_target_pairs={{0,4},{2,6},{4,8},{6,10},{8,12},{10,14},{12,16},{14,18},{16,20},{1... | collective-permute-start | bytes 2359304 | tf_op jit(solution)/shard_map/ppermute | solution.py:1101
  62.5 135.0 %all-gather.23.cloned.1.call-start = ((), (), s32[]{:S(2)}) async-start(), calls=%async_computation.4 | async-start | bytes 1572864 | tf_op jit(solution)/shard_map/all_gather | solution.py:1214
  63.9 133.6 %all-gather.19.cloned.1.call-start = ((), (), s32[]{:S(2)}) async-start(), calls=%async_computation.2 | async-start | bytes 3145728 | tf_op jit(solution)/shard_map/all_gather | solution.py:1214
  64.5 133.0 %all-gather.25.cloned.1.call-start = ((), (), s32[]{:S(2)}) async-start(), calls=%async_computation.5 | async-start | bytes 12582912 | tf_op jit(solution)/shard_map/all_gather | solution.py:1214
  65.1 132.5 %all-gather.27.cloned.1.call-start = ((), (), s32[]{:S(2)}) async-start(), calls=%async_computation.6 | async-start | bytes 12582912 | tf_op jit(solution)/shard_map/all_gather | solution.py:1214
  70.1 47.1 %collective-permute-start.5 = (bf16[1024,512]{1,0:T(8,128)(2,1)}, bf16[1024,512]{1,0:T(8,128)(2,1)}, u32[]{:S(2)}, u32[]{:S(2)}) collective-permute-start(bf16[1024,512]{1,0:T(8,128)(2,1)} %constant_dynamic-slice_fusion.11), channel_id=1, source_target_pairs={{0,2},{2,4},{4,6},{6,8},{8,10},{10,12},{12,14},{14,16},{16,18},{18... | collective-permute-start | bytes 3145736 | tf_op jit(solution)/shard_map/ppermute | solution.py:1101
  72.3 49.5 %collective-permute-start.6 = (bf16[1024,512]{1,0:T(8,128)(2,1)}, bf16[1024,512]{1,0:T(8,128)(2,1)}, u32[]{:S(2)}, u32[]{:S(2)}) collective-permute-start(bf16[1024,512]{1,0:T(8,128)(2,1)} %constant_dynamic-slice_fusion.11), channel_id=1, source_target_pairs={{2,0},{4,2},{6,4},{8,6},{10,8},{12,10},{14,12},{16,14},{18,16},{20... | collective-permute-start | bytes 3145736 | tf_op jit(solution)/shard_map/ppermute | solution.py:1101
  126.4 49.8 %collective-permute-start.11 = (bf16[896,512]{1,0:T(8,128)(2,1)}, bf16[896,512]{1,0:T(8,128)(2,1)S(1)}, u32[]{:S(2)}, u32[]{:S(2)}) collective-permute-start(bf16[896,512]{1,0:T(8,128)(2,1)} %get-tuple-element.227), channel_id=1, source_target_pairs={{4,0},{6,2},{8,4},{10,6},{12,8},{14,10},{16,12},{18,14},{20,16},{2... | collective-permute-start | bytes 2752520 | tf_op jit(solution)/shard_map/ppermute | solution.py:1101
  127.7 53.6 %collective-permute-start.10 = (bf16[896,512]{1,0:T(8,128)(2,1)}, bf16[896,512]{1,0:T(8,128)(2,1)S(1)}, u32[]{:S(2)}, u32[]{:S(2)}) collective-permute-start(bf16[896,512]{1,0:T(8,128)(2,1)} %get-tuple-element.226), channel_id=1, source_target_pairs={{0,4},{2,6},{4,8},{6,10},{8,12},{10,14},{12,16},{14,18},{16,20},{1... | collective-permute-start | bytes 2752520 | tf_op jit(solution)/shard_map/ppermute | solution.py:1101
  262.8 47.3 %collective-permute-start.20 = (bf16[896,512]{1,0:T(8,128)(2,1)}, bf16[896,512]{1,0:T(8,128)(2,1)S(1)}, u32[]{:S(2)}, u32[]{:S(2)}) collective-permute-start(bf16[896,512]{1,0:T(8,128)(2,1)} %get-tuple-element.265), channel_id=1, source_target_pairs={{4,0},{6,2},{8,4},{10,6},{12,8},{14,10},{16,12},{18,14},{20,16},{2... | collective-permute-start | bytes 2752520 | tf_op jit(solution)/shard_map/ppermute | solution.py:1101
  264.1 49.7 %collective-permute-start.21 = (bf16[896,512]{1,0:T(8,128)(2,1)}, bf16[896,512]{1,0:T(8,128)(2,1)S(1)}, u32[]{:S(2)}, u32[]{:S(2)}) collective-permute-start(bf16[896,512]{1,0:T(8,128)(2,1)} %get-tuple-element.266), channel_id=1, source_target_pairs={{0,4},{2,6},{4,8},{6,10},{8,12},{10,14},{12,16},{14,18},{16,20},{1... | collective-permute-start | bytes 2752520 | tf_op jit(solution)/shard_map/ppermute | solution.py:1101
  270.0 43.7 %collective-permute-start.22 = (bf16[128,1024]{1,0:T(8,128)(2,1)}, bf16[128,1024]{1,0:T(8,128)(2,1)S(1)}, u32[]{:S(2)}, u32[]{:S(2)}) collective-permute-start(bf16[128,1024]{1,0:T(8,128)(2,1)} %get-tuple-element.386), channel_id=1, source_target_pairs={{0,2},{2,0},{4,6},{6,4},{8,10},{10,8},{12,14},{14,12},{16,18},{18,... | collective-permute-start | bytes 786440 | tf_op jit(solution)/shard_map/ppermute | solution.py:1115
  271.8 47.5 %collective-permute-start.23 = (bf16[128,1024]{1,0:T(8,128)(2,1)S(1)}, bf16[128,1024]{1,0:T(8,128)(2,1)S(1)}, u32[]{:S(2)}, u32[]{:S(2)}) collective-permute-start(bf16[128,1024]{1,0:T(8,128)(2,1)S(1)} %get-tuple-element.385), channel_id=1, source_target_pairs={{0,4},{2,6},{4,0},{6,2},{8,12},{10,14},{12,8},{14,10},{16,20},{18,... | collective-permute-start | bytes 786440 | tf_op jit(solution)/shard_map/ppermute | solution.py:1115
  274.6 44.6 %collective-permute-start.24 = (bf16[128,1024]{1,0:T(8,128)(2,1)S(1)}, bf16[128,1024]{1,0:T(8,128)(2,1)S(1)}, u32[]{:S(2)}, u32[]{:S(2)}) collective-permute-start(bf16[128,1024]{1,0:T(8,128)(2,1)S(1)} %get-tuple-element.384), channel_id=1, source_target_pairs={{0,6},{2,4},{4,2},{6,0},{8,14},{10,12},{12,10},{14,8},{16,22},{18,... | collective-permute-start | bytes 786440 | tf_op jit(solution)/shard_map/ppermute | solution.py:1115
  341.6 21.1 %collective-permute-start.32 = (bf16[512,1024]{1,0:T(8,128)(2,1)S(1)}, bf16[512,1024]{1,0:T(8,128)(2,1)}, u32[]{:S(2)}, u32[]{:S(2)}) collective-permute-start(bf16[512,1024]{1,0:T(8,128)(2,1)S(1)} %copy-done.9), channel_id=1, source_target_pairs={{0,1},{1,0},{2,3},{3,2},{4,5},{5,4},{6,7},{7,6},{8,9},{9,8},{10,11... | collective-permute-start | bytes 3145736 | tf_op jit(solution)/shard_map/ppermute | solution.py:1077
  341.7 28.2 %collective-permute-start.30 = (bf16[1024,512]{1,0:T(8,128)(2,1)}, bf16[1024,512]{1,0:T(8,128)(2,1)}, u32[]{:S(2)}, u32[]{:S(2)}) collective-permute-start(bf16[1024,512]{1,0:T(8,128)(2,1)} %get-tuple-element.301), channel_id=1, source_target_pairs={{2,0},{4,2},{6,4},{8,6},{10,8},{12,10},{14,12},{16,14},{18,16},{20... | collective-permute-start | bytes 3145736 | tf_op jit(solution)/shard_map/ppermute | solution.py:1101
  343.0 50.0 %collective-permute-start.31 = (bf16[1024,512]{1,0:T(8,128)(2,1)}, bf16[1024,512]{1,0:T(8,128)(2,1)}, u32[]{:S(2)}, u32[]{:S(2)}) collective-permute-start(bf16[1024,512]{1,0:T(8,128)(2,1)} %get-tuple-element.302), channel_id=1, source_target_pairs={{0,2},{2,4},{4,6},{6,8},{8,10},{10,12},{12,14},{14,16},{16,18},{18... | collective-permute-start | bytes 3145736 | tf_op jit(solution)/shard_map/ppermute | solution.py:1101
  393.5 57.2 %collective-permute-start.26 = (bf16[1024,512]{1,0:T(8,128)(2,1)}, bf16[1024,512]{1,0:T(8,128)(2,1)S(1)}, u32[]{:S(2)}, u32[]{:S(2)}) collective-permute-start(bf16[1024,512]{1,0:T(8,128)(2,1)} %get-tuple-element.283), channel_id=1, source_target_pairs={{0,1},{1,0},{2,3},{3,2},{4,5},{5,4},{6,7},{7,6},{8,9},{9,8},{10,11... | collective-permute-start | bytes 3145736 | tf_op jit(solution)/shard_map/ppermute | solution.py:1077
  401.7 81.6 %collective-permute-start.40 = (bf16[1024,512]{1,0:T(8,128)(2,1)}, bf16[1024,512]{1,0:T(8,128)(2,1)}, u32[]{:S(2)}, u32[]{:S(2)}) collective-permute-start(bf16[1024,512]{1,0:T(8,128)(2,1)} %get-tuple-element.341), channel_id=1, source_target_pairs={{2,0},{4,2},{6,4},{8,6},{10,8},{12,10},{14,12},{16,14},{18,16},{20... | collective-permute-start | bytes 3145736 | tf_op jit(solution)/shard_map/ppermute | solution.py:1101
  403.0 80.3 %collective-permute-start.39 = (bf16[768,512]{1,0:T(8,128)(2,1)}, bf16[768,512]{1,0:T(8,128)(2,1)}, u32[]{:S(2)}, u32[]{:S(2)}) collective-permute-start(bf16[768,512]{1,0:T(8,128)(2,1)} %get-tuple-element.340), channel_id=1, source_target_pairs={{4,0},{6,2},{8,4},{10,6},{12,8},{14,10},{16,12},{18,14},{20,16},{2... | collective-permute-start | bytes 2359304 | tf_op jit(solution)/shard_map/ppermute | solution.py:1101
  405.0 78.3 %collective-permute-start.36 = (bf16[32,1024]{1,0:T(8,128)(2,1)S(1)}, bf16[32,1024]{1,0:T(8,128)(2,1)S(1)}, u32[]{:S(2)}, u32[]{:S(2)}) collective-permute-start(bf16[32,1024]{1,0:T(8,128)(2,1)S(1)} %get-tuple-element.390), channel_id=1, source_target_pairs={{0,8},{2,10},{4,12},{6,14},{8,0},{10,2},{12,4},{14,6},{16,24},{18,... | collective-permute-start | bytes 196616 | tf_op jit(solution)/shard_map/ppermute | solution.py:1115
  426.2 59.4 %collective-permute-start.37 = (bf16[32,1024]{1,0:T(8,128)(2,1)S(1)}, bf16[32,1024]{1,0:T(8,128)(2,1)S(1)}, u32[]{:S(2)}, u32[]{:S(2)}) collective-permute-start(bf16[32,1024]{1,0:T(8,128)(2,1)S(1)} %get-tuple-element.389), channel_id=1, source_target_pairs={{0,16},{2,18},{4,20},{6,22},{8,24},{10,26},{12,28},{14,30},{16,0},... | collective-permute-start | bytes 196616 | tf_op jit(solution)/shard_map/ppermute | solution.py:1115
  451.7 55.4 %collective-permute-start.38 = (bf16[32,1024]{1,0:T(8,128)(2,1)S(1)}, bf16[32,1024]{1,0:T(8,128)(2,1)S(1)}, u32[]{:S(2)}, u32[]{:S(2)}) collective-permute-start(bf16[32,1024]{1,0:T(8,128)(2,1)S(1)} %get-tuple-element.388), channel_id=1, source_target_pairs={{0,24},{2,26},{4,28},{6,30},{8,16},{10,18},{12,20},{14,22},{16,8},... | collective-permute-start | bytes 196616 | tf_op jit(solution)/shard_map/ppermute | solution.py:1115
  507.1 30.4 %collective-permute-start.43 = (bf16[1024,512]{1,0:T(8,128)(2,1)S(1)}, bf16[1024,512]{1,0:T(8,128)(2,1)}, u32[]{:S(2)}, u32[]{:S(2)}) collective-permute-start(bf16[1024,512]{1,0:T(8,128)(2,1)S(1)} %add_convert_fusion.1.refs_0_), channel_id=1, source_target_pairs={{0,1},{1,0},{2,3},{3,2},{4,5},{5,4},{6,7},{7,6},{8,9},{9,8},{10,11... | collective-permute-start | bytes 3145736 | tf_op jit(solution)/shard_map/ppermute | solution.py:1077
  514.1 27.8 %collective-permute-start.42 = (bf16[1024,512]{1,0:T(8,128)(2,1)}, bf16[1024,512]{1,0:T(8,128)(2,1)S(1)}, u32[]{:S(2)}, u32[]{:S(2)}) collective-permute-start(bf16[1024,512]{1,0:T(8,128)(2,1)} %add_convert_fusion.refs_0_), channel_id=1, source_target_pairs={{0,1},{1,0},{2,3},{3,2},{4,5},{5,4},{6,7},{7,6},{8,9},{9,8},{10,11... | collective-permute-start | bytes 3145736 | tf_op jit(solution)/shard_map/ppermute | solution.py:1077
  516.1 15.2 %collective-permute-start.45 = (bf16[80,1024]{1,0:T(8,128)(2,1)}, bf16[80,1024]{1,0:T(8,128)(2,1)S(1)}, u32[]{:S(2)}, u32[]{:S(2)}) collective-permute-start(bf16[80,1024]{1,0:T(8,128)(2,1)} %shard_map.286.refs_0_), channel_id=1, source_target_pairs={{0,16},{2,18},{4,20},{6,22},{8,24},{10,26},{12,28},{14,30},{16,0},... | collective-permute-start | bytes 491528 | tf_op jit(solution)/shard_map/ppermute | solution.py:1115
  534.0 17.3 %collective-permute-start.48 = (bf16[176,1024]{1,0:T(8,128)(2,1)}, bf16[176,1024]{1,0:T(8,128)(2,1)S(1)}, u32[]{:S(2)}, u32[]{:S(2)}) collective-permute-start(bf16[176,1024]{1,0:T(8,128)(2,1)} %shard_map.287.refs_0_), channel_id=1, source_target_pairs={{0,4},{2,6},{4,0},{6,2},{8,12},{10,14},{12,8},{14,10},{16,20},{18,... | collective-permute-start | bytes 1081352 | tf_op jit(solution)/shard_map/ppermute | solution.py:1115
  534.0 17.3 %collective-permute-start.49 = (bf16[176,1024]{1,0:T(8,128)(2,1)}, bf16[176,1024]{1,0:T(8,128)(2,1)S(1)}, u32[]{:S(2)}, u32[]{:S(2)}) collective-permute-start(bf16[176,1024]{1,0:T(8,128)(2,1)} %shard_map.287.refs_0_), channel_id=1, source_target_pairs={{0,6},{2,4},{4,2},{6,0},{8,14},{10,12},{12,10},{14,8},{16,22},{18,... | collective-permute-start | bytes 1081352 | tf_op jit(solution)/shard_map/ppermute | solution.py:1115
  (75 other events, 547.9 us)
Sparse Core Ops, SparseCore 0:
  11.4 13.2 all-gather.14
  26.3 11.7 all-gather.16
  62.6 23.3 all-gather.20
  87.4 10.2 all-gather.22
  99.1 11.7 all-gather.18
  112.3 21.0 all-gather.24
  134.9 23.8 all-gather.26

commit v2 on v1

--- a/solution.py
+++ b/solution.py
@@ -57,7 +57,7 @@
 
 def over_tiles(info, segments, block, tile):
     def one_segment(segment, carry):
-        first, count, low, high = (info[4 * segment + i, block] for i in range(4))
+        first, count, low, high = (info[6 * segment + i, block] for i in range(4))
 
         def full(i, carry):
             tile(pl.multiple_of(first + i * BLOCK, 128), segment, False)
@@ -78,8 +78,19 @@
         lax.fori_loop(0, segments, one_segment, 0)
 
 
+def span_of(info, segment):
+    return info[6 * segment + 4, 0], info[6 * segment + 5, 0]
+
+
+def in_spans(info, segments, test):
+    result = test(*span_of(info, 0))
+    for segment in range(1, segments):
+        result = result | test(*span_of(info, segment))
+    return result
+
+
 def owned(info, segments, cores, before, length):
-    owner = lax.rem(info[4 * segments + 2, 0] + cores - before, cores)
+    owner = lax.rem(info[6 * segments, 0] + cores - before, cores)
     return pl.ds(pl.multiple_of(owner * length, length), length)
 
 
@@ -100,17 +111,13 @@
     refs = list(refs)
     q, start, end = refs[:3]
     del refs[:3]
-    if pieces is None:
-        k, v = refs[:2]
-        del refs[:2]
-    else:
-        wk, wv = refs[:2]
-        del refs[:2]
-        parts = []
-        for length, raw in pieces:
-            count = cores if raw else 2
-            parts.append(refs[:count])
-            del refs[:count]
+    wk, wv = refs[:2]
+    del refs[:2]
+    parts = []
+    for length, raw in pieces:
+        count = cores if raw else 2
+        parts.append(refs[:count])
+        del refs[:count]
     if prefix:
         pk, pv = refs[:2]
         del refs[:2]
@@ -119,9 +126,8 @@
         del refs[:3]
     outs = refs[: 2 if last else 3]
     del refs[: len(outs)]
-    if pieces is not None:
-        k, v = refs[:2]
-        del refs[:2]
+    k, v = refs[:2]
+    del refs[:2]
     vt = refs.pop(0)
     if last:
         out, lse = outs
@@ -131,7 +137,6 @@
         top, total, acc = outs
     block = pl.program_id(0)
     heads = q.shape[1] // HEAD_DIM
-    least, most = info[4 * segments, 0], info[4 * segments + 1, 0]
 
     def bring(piece, offset, length, sem):
         window = pl.ds(offset, length)
@@ -144,7 +149,9 @@
         def rows_at(row, size):
             window = pl.ds(offset + row, size)
 
-            @pl.when((offset + row < most) & (offset + row + size > least))
+            needed = lambda least, most: (offset + row < most) & (offset + row + size > least)
+
+            @pl.when(in_spans(info, segments, needed))
             def _():
                 source = pl.ds(row, size)
                 depth = piece[0].shape[1]
@@ -173,32 +180,32 @@
 
     @pl.when(block == 0)
     def _():
-        if pieces is None:
-            over_range(least, most, turn_over)
-        else:
-            offset, ready = 0, []
-            for (length, raw), piece in zip(pieces, parts):
-                if not raw:
-                    ready.append((offset, length))
-                    for copy in bring(piece, offset, length, refs[0]):
-                        copy.start()
-                offset += length
-            rest = slice(offset, k.shape[0])
-            k[rest, :] = jnp.zeros((k.shape[0] - offset, k.shape[1]), bf16)
-            v[rest, :] = jnp.zeros((k.shape[0] - offset, k.shape[1]), bf16)
-            vt[:, rest] = jnp.zeros((k.shape[1], k.shape[0] - offset), bf16)
-            offset = 0
-            for (length, raw), piece in zip(pieces, parts):
-                if raw:
-                    project(piece, offset, length)
-                offset += length
-            offset = 0
-            for (length, raw), piece in zip(pieces, parts):
-                if not raw:
-                    for copy in bring(piece, offset, length, refs[0]):
-                        copy.wait()
-                    over_range(jnp.maximum(least, offset), jnp.minimum(most, offset + length), turn_over)
-                offset += length
+        offset, ready = 0, []
+        for (length, raw), piece in zip(pieces, parts):
+            if not raw:
+                for copy in bring(piece, offset, length, refs[0]):
+                    copy.start()
+            offset += length
+        rest = slice(offset, k.shape[0])
+        k[rest, :] = jnp.zeros((k.shape[0] - offset, k.shape[1]), bf16)
+        v[rest, :] = jnp.zeros((k.shape[0] - offset, k.shape[1]), bf16)
+        vt[:, rest] = jnp.zeros((k.shape[1], k.shape[0] - offset), bf16)
+        offset = 0
+        for (length, raw), piece in zip(pieces, parts):
+            if raw:
+                project(piece, offset, length)
+            offset += length
+        offset = 0
+        for (length, raw), piece in zip(pieces, parts):
+            if not raw:
+                for copy in bring(piece, offset, length, refs[0]):
+                    copy.wait()
+                for segment in range(segments):
+                    least, most = span_of(info, segment)
+                    over_range(
+                        jnp.maximum(least, offset), jnp.minimum(most, offset + length), turn_over
+                    )
+            offset += length
 
     qs = []
     for pair in range(heads // 2):
@@ -266,10 +273,9 @@
 class Rows(NamedTuple):
     parts: list
     length: int
-    place: int = 0
-
-
-def attend(query, keys, values, start, end, info, prefix=None, state=None, last=True, weights=None):
+
+
+def attend(query, keys, weights, start, end, info, prefix=None, state=None, last=True):
     rows, cols = query.shape
     heads = cols // HEAD_DIM
     by_rows = pl.BlockSpec((BLOCK, cols), lambda b, info: (b, 0))
@@ -278,31 +284,22 @@
     segments = start.shape[0]
     operands = [query, start, end]
     specs = [by_rows, by_lanes(segments), by_lanes(segments)]
-    pieces, cores = None, 1
-    if weights is None:
-        window = keys.shape[0]
-        operands += [keys, values]
-        specs += [whole(window)] * 2
-    else:
-        pieces = tuple(
-            (piece.length, True) if isinstance(piece, Rows) else (piece[0].shape[0], False)
-            for piece in keys
-        )
-        window = sum(length for length, raw in pieces) + PAD
-        operands += list(weights)
-        specs += [whole(weights[0].shape[0])] * 2
-        for (length, raw), piece in zip(pieces, keys):
-            if raw:
-                cores = len(piece.parts)
-                operands += list(piece.parts)
-                place = piece.place
-                specs += [
-                    pl.BlockSpec((length, part.shape[1]), lambda b, info, place=place: (place, 0))
-                    for part in piece.parts
-                ]
-            else:
-                operands += list(piece)
-                specs += [pl.BlockSpec(memory_space=pl.ANY)] * 2
+    cores = 1
+    pieces = tuple(
+        (piece.length, True) if isinstance(piece, Rows) else (piece[0].shape[0], False)
+        for piece in keys
+    )
+    window = sum(length for length, raw in pieces) + PAD
+    operands += list(weights)
+    specs += [whole(weights[0].shape[0])] * 2
+    for (length, raw), piece in zip(pieces, keys):
+        if raw:
+            cores = len(piece.parts)
+            operands += list(piece.parts)
+            specs += [whole(length, part.shape[1]) for part in piece.parts]
+        else:
+            operands += list(piece)
+            specs += [pl.BlockSpec(memory_space=pl.ANY)] * 2
     if prefix is not None:
         operands += [prefix[0], prefix[1]]
         specs += [whole(32), whole(32)]
@@ -319,10 +316,9 @@
     else:
         outs = [shape((n, rows), f32) for n in (heads, heads, cols)]
         out_specs = list(state_specs)
-    if weights is not None:
-        outs += [shape((window, cols), bf16)] * 2
-        out_specs += [whole(window)] * 2
-        scratch.append(pltpu.SemaphoreType.DMA((2,)))
+    outs += [shape((window, cols), bf16)] * 2
+    out_specs += [whole(window)] * 2
+    scratch.append(pltpu.SemaphoreType.DMA((2,)))
     return pl.pallas_call(
         functools.partial(
             attend_kernel, 0 if prefix is None else prefix[2], state is not None, last, segments,
@@ -340,48 +336,72 @@
     )(info, *operands)
 
 
-def attend_back_kernel(prefix, resume, own, final, cuts, cores, segments, info, *refs):
+def attend_back_kernel(
+    prefix, resume, own, final, lengths, cuts, cores, segments, info, *refs
+):
     refs = list(refs)
-    q, d_out, out, k, v, start, end, lse, wk, wv = refs[:10]
-    del refs[:10]
+    q, d_out, out, start, end, lse, wk, wv = refs[:8]
+    del refs[:8]
+    sources = [refs[2 * i : 2 * i + 2] for i in range(len(lengths))]
+    del refs[: 2 * len(lengths)]
     if prefix:
         pk, pv = refs[:2]
         del refs[:2]
     if resume:
         dq_in = refs.pop(0)
-    if own:
+    if own is not None:
         wq = refs.pop(0)
-    pieces = len(cuts) - 1
+    pieces = len(cuts)
     grads = [refs[i * cores : i * cores + cores] for i in range(pieces)]
     del refs[: pieces * cores]
     if prefix:
         dpk, dpv = refs[:2]
         del refs[:2]
-    if not own:
+    if own is None:
         dq_out = refs.pop(0)
-    kt, dk, dv = refs[:3]
-    del refs[:3]
-    if own:
-        dq, dq_low = refs
-    elif final:
-        (dq,) = refs
-    else:
-        dq = dq_out
+    k, v, kt, dk, dv, dq, sem = refs[:7]
+    if own is not None:
+        dq_low = refs[7]
     block = pl.program_id(0)
     heads = q.shape[1] // HEAD_DIM
     pairs = heads // 2
 
     @pl.when(block == 0)
     def _():
-        def prepare(window):
-            kt[:, window] = k[window, :].T
-            dk[window, :] = jnp.zeros((128, dk.shape[1]), f32)
-            dv[window, :] = jnp.zeros((128, dv.shape[1]), f32)
-
-        over_range(info[4 * segments, 0], info[4 * segments + 1, 0], prepare)
+        copies, offset = [], 0
+        for i, (length, source) in enumerate(zip(lengths, sources)):
+            for j, (there, here) in enumerate(zip(source, (k, v))):
+                copies.append(
+                    pltpu.make_async_copy(
+                        there.at[pl.ds(0, length), :],
+                        here.at[pl.ds(offset, length), :],
+                        sem.at[2 * i + j],
+                    )
+                )
+            offset += length
+        for copy in copies:
+            copy.start()
+        if offset < k.shape[0]:
+            rest = slice(offset, k.shape[0])
+            k[rest, :] = jnp.zeros((k.shape[0] - offset, k.shape[1]), bf16)
+            v[rest, :] = jnp.zeros((k.shape[0] - offset, k.shape[1]), bf16)
         if prefix:
             dpk[...] = jnp.zeros(dpk.shape, f32)
             dpv[...] = jnp.zeros(dpv.shape, f32)
+
+        def clear(window):
+            dk[window, :] = jnp.zeros((128, dk.shape[1]), f32)
+            dv[window, :] = jnp.zeros((128, dv.shape[1]), f32)
+
+        def turn_over(window):
+            kt[:, window] = k[window, :].T
+
+        for segment in range(segments):
+            over_range(*span_of(info, segment), clear)
+        for copy in copies:
+            copy.wait()
+        for segment in range(segments):
+            over_range(*span_of(info, segment), turn_over)
 
     qs, ds, delta, q_stack, d_stack = [], [], [], [], []
     for pair in range(pairs):
@@ -436,33 +456,37 @@
             dk[window, cols] += dot(jnp.concatenate(gs, axis=1), q_stack[pair])
 
     over_tiles(info, segments, block, tile)
-    if own:
+    if own is None and final:
+        dq_out[...] = (dq[...] * 0.125).T.astype(bf16)
+    elif own is None:
+        dq_out[...] = dq[...]
+    else:
         dq_low[pl.ds(pl.multiple_of(block * BLOCK, BLOCK), BLOCK), :] = (
             (dq[...] * 0.125).T.astype(bf16)
         )
-    elif final:
-        dq_out[...] = (dq[...] * 0.125).T.astype(bf16)
 
     @pl.when(block == pl.num_programs(0) - 1)
     def _():
-        least, most = info[4 * segments, 0], info[4 * segments + 1, 0]
-
         def project(row, size, piece, offset):
             window = pl.ds(row, size)
             target = pl.ds(offset, size)
-            touched = (row < most) & (row + size > least)
+            touched = in_spans(
+                info, segments, lambda least, most: (row < most) & (row + size > least)
+            )
             width = grads[piece][0].shape[1]
 
             @pl.when(touched)
             def _():
                 place = row + lax.broadcasted_iota(jnp.int32, (size, dk.shape[1]), 0)
-                there = (place >= least) & (place < most)
+                there = in_spans(
+                    info, segments, lambda least, most: (place >= least) & (place < most)
+                )
                 dk_low = jnp.where(there, dk[window, :] * LN2, 0.0).astype(bf16)
                 dv_low = jnp.where(there, dv[window, :], 0.0).astype(bf16)
                 for core in range(cores):
                     part = owned(info, segments, cores, core, width)
                     value = dot_nt(dk_low, wk[part, :]) + dot_nt(dv_low, wv[part, :])
-                    if own:
+                    if own == piece:
                         value += dot_nt(dq_low[target, :], wq[part, :])
                     grads[piece][core][target, :] = value.astype(bf16)
 
@@ -470,79 +494,81 @@
             def _():
                 for core in range(cores):
                     value = jnp.zeros((size, width), f32)
-                    if own:
+                    if own == piece:
                         part = owned(info, segments, cores, core, width)
                         value = dot_nt(dq_low[target, :], wq[part, :])
                     grads[piece][core][target, :] = value.astype(bf16)
 
-        for piece in range(pieces):
-            length = cuts[piece + 1] - cuts[piece]
+        for piece, (begin, length) in enumerate(cuts):
             whole = length // BLOCK
 
-            def step(i, carry, piece=piece):
+            def step(i, carry, piece=piece, begin=begin):
                 offset = pl.multiple_of(i * BLOCK, BLOCK)
-                project(pl.multiple_of(cuts[piece] + offset, 128), BLOCK, piece, offset)
+                project(pl.multiple_of(begin + offset, 128), BLOCK, piece, offset)
                 return carry
 
             lax.fori_loop(0, whole, step, 0)
             rest = length - whole * BLOCK
             if rest:
-                project(cuts[piece] + whole * BLOCK, rest, piece, whole * BLOCK)
+                project(begin + whole * BLOCK, rest, piece, whole * BLOCK)
 
 
 def attend_back(
-    query, d_out, out, keys, values, start, end, lse, info, key_weight, value_weight, cuts, cores,
-    prefix=None, state=None, query_weight=None, final=False,
+    query, d_out, out, sources, weights, start, end, info, lse, cuts, cores, prefix=None, own=None,
+    state=None, final=False, pad=0,
 ):
     rows, cols = query.shape
-    window = cuts[-1] + (0 if query_weight is not None else PAD)
-    width = key_weight.shape[0]
+    lengths = tuple(length for _, _, length in sources)
+    window = sum(lengths) + pad
+    width = weights[0].shape[0]
     heads = cols // HEAD_DIM
-    own = query_weight is not None
     segments = start.shape[0]
     by_rows = pl.BlockSpec((BLOCK, cols), lambda b, info: (b, 0))
     by_lanes = lambda count: pl.BlockSpec((count, BLOCK), lambda b, info: (0, b))
     whole = lambda count, wide=cols: pl.BlockSpec((count, wide), lambda b, info: (0, 0))
-    operands = [query, d_out, out, keys, values, start, end, lse, key_weight, value_weight]
-    specs = [by_rows] * 3 + [whole(window)] * 2 + [by_lanes(segments)] * 2 + [by_lanes(heads)]
-    specs += [whole(width)] * 2
+    operands = [query, d_out, out, start, end, lse] + list(weights[:2])
+    specs = [by_rows] * 3 + [by_lanes(segments)] * 2 + [by_lanes(heads)] + [whole(width)] * 2
+    for keys, values, _ in sources:
+        operands += [keys, values]
+        specs += [pl.BlockSpec(memory_space=pl.ANY)] * 2
     if prefix is not None:
         operands += [prefix[0], prefix[1]]
         specs += [whole(32), whole(32)]
     if state is not None:
         operands.append(state)
         specs.append(by_lanes(cols))
-    if own:
-        operands.append(query_weight)
+    if own is not None:
+        operands.append(weights[2])
         specs.append(whole(width))
     shape = jax.ShapeDtypeStruct
     outs, out_specs = [], []
-    for piece in range(len(cuts) - 1):
-        length = cuts[piece + 1] - cuts[piece]
+    for _, length in cuts:
         outs += [shape((length, width // cores), bf16)] * cores
         out_specs += [whole(length, width // cores)] * cores
     if prefix is not None:
         outs += [shape((32, cols), f32)] * 2
         out_specs += [whole(32)] * 2
+    if own is None and final:
+        outs.append(shape((rows, cols), bf16))
+        out_specs.append(by_rows)
+    elif own is None:
+        outs.append(shape((cols, rows), f32))
+        out_specs.append(by_lanes(cols))
     scratch = [
+        pltpu.VMEM((window, cols), bf16),
+        pltpu.VMEM((window, cols), bf16),
         pltpu.VMEM((cols, window), bf16),
         pltpu.VMEM((window, cols), f32),
         pltpu.VMEM((window, cols), f32),
+        pltpu.VMEM((cols, BLOCK), f32),
+        pltpu.SemaphoreType.DMA((2 * len(sources),)),
     ]
-    if own:
-        scratch += [pltpu.VMEM((cols, BLOCK), f32), pltpu.VMEM((rows, cols), bf16)]
-    elif final:
-        scratch.append(pltpu.VMEM((cols, BLOCK), f32))
-        outs.append(shape((rows, cols), bf16))
-        out_specs.append(by_rows)
-    else:
-        outs.append(shape((cols, rows), f32))
-        out_specs.append(by_lanes(cols))
+    if own is not None:
+        scratch.append(pltpu.VMEM((rows, cols), bf16))
     result = pl.pallas_call(
         functools.partial(
-            attend_back_kernel,
-            0 if prefix is None else prefix[2], state is not None, own, final, tuple(cuts), cores,
-            segments,
+            attend_back_kernel, 0 if prefix is None else prefix[2], state is not None, own, final,
+            lengths, tuple(cuts), cores, segments,
         ),
         out_shape=tuple(outs),
         grid_spec=pltpu.PrefetchScalarGridSpec(
@@ -554,15 +580,12 @@
         ),
         compiler_params=kernel_params(),
     )(info, *operands)
-    pieces = [
-        list(result[i * cores : i * cores + cores]) for i in range(len(cuts) - 1)
-    ]
-    return pieces, *result[(len(cuts) - 1) * cores :]
+    pieces = [list(result[i * cores : i * cores + cores]) for i in range(len(cuts))]
+    return pieces, *result[len(cuts) * cores :]
 
 
 class Span(NamedTuple):
     segments: tuple
-    step: int = 128
     causal: bool = True
 
 
@@ -600,7 +623,6 @@
     ]
     for i, span in enumerate(spans):
         starts_out, ends_out, info = refs[3 * i : 3 * i + 3]
-        lowest, highest = 1 << 20, 0
         for segment, (base, low, high) in enumerate(span.segments):
             clip = lambda value: jnp.clip(value + base, low, high)
             if span.causal:
@@ -611,23 +633,23 @@
                 corners = [(ends[1][b], ends[2][b]) for b in range(blocks)]
             starts_out[segment : segment + 1, :] = clip(lows)
             ends_out[segment : segment + 1, :] = clip(highs)
+            lowest, highest = 1 << 20, 0
             for b, ((s0, s1), (e0, e1)) in enumerate(corners):
                 s0, s1, e0, e1 = clip(s0), clip(s1), clip(e0), clip(e1)
                 some = e1 > s0
-                first = jnp.where(some, s0 // span.step * span.step, 0)
+                first = jnp.where(some, s0 // 128 * 128, 0)
                 count = jnp.where(some, (e1 - first + BLOCK - 1) // BLOCK, 0)
                 from_ = jnp.clip((s1 - first + BLOCK - 1) // BLOCK, 0, count)
                 to = jnp.clip((e0 - first) // BLOCK, from_, count)
                 for row, value in enumerate((first, count, from_, to)):
-                    info[4 * segment + row, b] = value
+                    info[6 * segment + row, b] = value
                 lowest = jnp.where(some, jnp.minimum(lowest, first), lowest)
                 highest = jnp.where(some, jnp.maximum(highest, first + count * BLOCK), highest)
-        tail = 4 * len(span.segments)
+            for b in range(blocks):
+                info[6 * segment + 4, b] = jnp.minimum(lowest, highest)
+                info[6 * segment + 5, b] = highest
         for b in range(blocks):
-            info[tail, b] = jnp.minimum(lowest, highest)
-            info[tail + 1, b] = highest
-            info[tail + 2, b] = core
-            info[tail + 3, b] = 0
+            info[6 * len(span.segments), b] = core
 
 
 def see(spans, total, rows, tgt, mem, at):
@@ -635,7 +657,7 @@
     for span in spans:
         count = len(span.segments)
         outs += [jax.ShapeDtypeStruct((count, rows), jnp.int32)] * 2
-        outs.append(jax.ShapeDtypeStruct((4 * count + 4, rows // BLOCK), jnp.int32))
+        outs.append(jax.ShapeDtypeStruct((6 * count + 1, rows // BLOCK), jnp.int32))
         specs += [pl.BlockSpec((count, rows), lambda i, *scalars: (0, 0))] * 2
         specs.append(pl.BlockSpec(memory_space=pltpu.SMEM))
     result = pl.pallas_call(
@@ -990,7 +1012,7 @@
     )(*[part for parts in lists for part in parts])
 
 
-SMALL = 48
+SMALL = 32
 
 
 def pack_kernel(count, *refs):
@@ -1001,11 +1023,12 @@
     for part in parts[1:]:
         total = total + part[...].astype(f32)
     out[:rows, :] = total.astype(bf16)
-    out[rows : rows + 32, :] = jnp.zeros((32, out.shape[1]), bf16)
-    cols = keys.shape[1]
-    out[rows : rows + 32, :cols] = keys[...].astype(bf16)
-    out[rows : rows + 32, cols : 2 * cols] = values[...].astype(bf16)
-    out[rows + 32 :, :] = biases[...].astype(bf16)
+    zero = jnp.zeros((SMALL, out.shape[1] - 2 * keys.shape[1]), f32)
+    beside_ = [keys[...], values[...]] + ([zero] if zero.shape[1] else [])
+    line = lax.broadcasted_iota(jnp.int32, (SMALL, out.shape[1]), 0)
+    rest = jnp.where(line == SMALL - 2, biases[0:1], biases[1:2])
+    small = jnp.where(line < SMALL - 2, jnp.concatenate(beside_, axis=1), rest)
+    out[rows:, :] = small.astype(bf16)
 
 
 def pack(parts, keys, values, biases):
@@ -1030,8 +1053,8 @@
         prefix, cols = keys.shape
         keys[...] = total[:prefix, :cols]
         values[...] = total[:prefix, cols : 2 * cols]
-        up_bias[...] = total[32:33]
-        down_bias[...] = total[33:34, : down_bias.shape[1]]
+        up_bias[...] = total[SMALL - 2 : SMALL - 1]
+        down_bias[...] = total[SMALL - 1 : SMALL, : down_bias.shape[1]]
     for k, part in enumerate(parts):
         owner = jnp.bitwise_xor(place[0], k)
         joined[pl.ds(pl.multiple_of(owner * rows, 16), rows), :] = part[:rows, :]
@@ -1066,6 +1089,43 @@
         outs,
         scratch,
     )
+
+
+def stack_kernel(cores, core, *refs):
+    out = refs[-1]
+    rows = refs[0].shape[0]
+    for k, part in enumerate(refs[:-1]):
+        owner = lax.rem(core[0] + cores - k, cores)
+        out[pl.ds(pl.multiple_of(owner * rows, 16), rows), :] = part[...].astype(out.dtype)
+
+
+def stacked(core, parts):
+    rows, width = parts[0].shape
+    cores = len(parts)
+    out = jax.ShapeDtypeStruct((cores * rows, width), bf16)
+    return one_step(
+        functools.partial(stack_kernel, cores), core, list(parts), [None] * cores, [out], []
+    )[0]
+
+
+def sum_kernel(places, *refs):
+    out = refs[-1]
+    for row in range(0, out.shape[0], 128):
+        total = jnp.zeros((128, out.shape[1]), f32)
+        for ref, place in zip(refs[:-1], places):
+            if place <= row < place + ref.shape[0]:
+                total = total + ref[row - place : row - place + 128, :].astype(f32)
+        out[row : row + 128, :] = total.astype(bf16)
+
+
+def sum_of(wholes, shorter):
+    parts = list(wholes) + [part for part, _ in shorter]
+    places = [0] * len(wholes) + [place for _, place in shorter]
+    return pl.pallas_call(
+        functools.partial(sum_kernel, tuple(places)),
+        out_shape=jax.ShapeDtypeStruct(wholes[0].shape, bf16),
+        compiler_params=pltpu.CompilerParams(vmem_limit_bytes=60 << 20),
+    )(*parts)
 
 
 def product(left, right):
@@ -1174,16 +1234,19 @@
     self_base = rows + self_far
     far_rows = 2 * cross_far
     at = jnp.stack([position * rows, core]).astype(jnp.int32)
-    self_seen, own_seen, halo_seen, main_seen, far_seen = see(
+    base = 3 * rows + PAD
+    far_spans = lambda at: (
+        (at + rows + cross_far, at, at + cross_far),
+        (at + cross_far - 2 * rows, at + cross_far, at + far_rows),
+    )
+    own_seen, halo_seen, main_seen, far_seen, here_seen, around_seen = see(
         (
-            Span(((self_base, 0, self_base + rows),)),
-            Span(((0, 0, rows),), BLOCK),
+            Span(((0, 0, rows),)),
             Span(((self_base, 0, self_base),)),
-            Span(((rows, 0, 3 * rows),), causal=False),
-            Span(
-                ((rows + cross_far, 0, cross_far), (cross_far - 2 * rows, cross_far, far_rows)),
-                causal=False,
-            ),
+            Span(((rows, 0, 3 * rows),), False),
+            Span(far_spans(0), False),
+            Span(((0, 0, rows),), False),
+            Span(((rows, 0, rows), (rows, 2 * rows, 3 * rows)) + far_spans(base), False),
         ),
         total,
         rows,
@@ -1193,9 +1256,11 @@
     )
 
     tokens_cols = mine(tokens, 1)
+    memory_cols = mine(after(memory, tokens_cols), 1)
     tokens_end = tokens_cols[rows - self_far :]
     token_near = shift(tokens_cols, 1)
     token_far = shift(tokens_end, 2)
+    memory_after = shift(memory_cols, -1)
     down_biases = [adapter_down_bias] + others(adapter_down_bias)
 
     prefix_pad = ((0, 32 - prefix), (0, 0))
@@ -1216,30 +1281,27 @@
     self_outputs = all_cores(self_output, query)
     cross_queries = all_cores(cross_query, query)
     arrived = (token_near, token_far)
-    ready = (query, own_keys, own_values, self_seen)
+    memory_keys = product(memory, cross_key).astype(bf16)
+    memory_values = product(memory, cross_value).astype(bf16)
+    *state, own_keys, own_values = attend(
+        query, [(own_keys, own_values)], (self_key, self_value), *own_seen, prefix_rows, last=False
+    )
+    arrived = (token_near, token_far, memory_after)
+    ready = (state, memory_keys, memory_values)
     arrived, ready = lax.optimization_barrier((arrived, ready))
-    token_near, token_far = arrived
-    query, own_keys, own_values, self_seen = ready
-    memory_late = after(memory, token_near)
-    memory_cols = mine(memory_late, 1)
-    memory_keys = product(memory_late, cross_key).astype(bf16)
-    memory_values = product(memory_late, cross_value).astype(bf16)
+    token_near, token_far, memory_after = arrived
+    state, memory_keys, memory_values = ready
 
     token_near = [token_near] + others(token_near)
     token_far = [token_far] + others(token_far)
-    memory_near = (
-        shift(after(memory_cols, token_near, token_far), 1),
-        shift(after(memory_cols, token_near, token_far), -1),
-    )
-    attended, self_lse, self_keys, self_values = attend(
-        after(query, memory_keys, memory_values),
-        [Rows(token_far, self_far), Rows(token_near, rows), (own_keys, own_values)],
-        None,
-        *self_seen,
-        prefix_rows,
-        None,
-        True,
+    memory_after = [memory_after] + others(after(memory_after, token_near, token_far))
+    memory_before = shift(after(memory_cols, token_near, token_far), 1)
+    attended, self_lse, halo_keys, halo_values = attend(
+        query,
+        [Rows(token_far, self_far), Rows(token_near, rows)],
         (self_key, self_value),
+        *halo_seen,
+        state=state,
     )
 
     def to_rows(value):
@@ -1249,14 +1311,16 @@
         parts = [parts[0]] + [turn(parts[k], -k) for k in range(1, cores)]
         return in_order([parts[-k % cores] for k in range(cores)], 0)
 
-    cross_outputs = all_cores(cross_output, memory_keys)
-    hidden_ins = all_cores(hidden_in, memory_keys)
-    hidden_outs = all_cores(hidden_out, memory_keys)
-    downs = all_cores(after(adapter_down, memory_keys).astype(bf16))
-    ups = all_cores(after(adapter_up, memory_keys).astype(bf16))
+    cross_outputs = all_cores(cross_output, state)
+    hidden_ins = all_cores(hidden_in, state)
+    hidden_outs = all_cores(hidden_out, state)
+    downs = all_cores(after(adapter_down, state).astype(bf16))
+    ups = all_cores(after(adapter_up, state).astype(bf16))
     attended_rows = to_rows(attended)
-    attended_rows, memory_near = lax.optimization_barrier((attended_rows, memory_near))
-    memory_near = [[part] + others(part) for part in memory_near]
+    attended_rows, memory_before, memory_after = lax.optimization_barrier(
+        (attended_rows, memory_before, memory_after)
+    )
+    memory_near = [[memory_before] + others(memory_before), memory_after]
     memory_far = (
         shift(after(memory_cols[rows - cross_far :], memory_near), 2),
         shift(after(memory_cols[:cross_far], memory_near), -2),
@@ -1269,17 +1333,14 @@
     *state, main_keys, main_values = attend(
         cross_q,
         [Rows(memory_near[0], rows), (memory_keys, memory_values), Rows(memory_near[1], rows)],
-        None,
+        (cross_key, cross_value),
         *main_seen,
-        None,
-        None,
-        False,
-        (cross_key, cross_value),
+        last=False,
     )
     state, memory_far = lax.optimization_barrier((state, memory_far))
     memory_far = [Rows([part] + others(part), cross_far) for part in memory_far]
     crossed, cross_lse, far_keys, far_values = attend(
-        cross_q, memory_far, None, *far_seen, None, state, True, (cross_key, cross_value)
+        cross_q, memory_far, (cross_key, cross_value), *far_seen, state=state
     )
 
     (
@@ -1303,91 +1364,129 @@
     )
     d_crossed = to_heads(d_crossed)
     adapter_grads = dealt(after(adapter_grads, d_crossed))
+    outputs_other = others(after(outputs_rows, d_crossed))
     ups_count = adapter_up.shape[0]
     staged = shards % 4 == 0 and shards & (shards - 1) == 0 and 2 * ups_count % shards == 0
     if staged:
         plane, column = Ring(4, 1), Ring(shards // 4, 4)
 
-    far_grads, query_state = attend_back(
-        cross_q, d_crossed, crossed, far_keys, far_values, *far_seen[:2], cross_lse, far_seen[2],
-        cross_key, cross_value, (0, cross_far, 2 * cross_far), cores,
-    )
-    far_grads, query_state, adapter_grads = lax.optimization_barrier(
-        (far_grads, query_state, adapter_grads)
-    )
-    far_parts = [dealt(part) for part in far_grads]
     adapter_grads, bias_grads = add_up([adapter_grads], 2 * ups_count)
+    adapter_arrived = []
     if staged:
+        adapter_kept = plane.cut(adapter_grads, 0)
         adapter_arrived = plane.scatter(adapter_grads)
-        adapter_kept = plane.cut(adapter_grads, 0)
-    far_low = add_up(after(far_parts, adapter_grads))
-    far_arrived = (shift(far_low[0], -2), shift(far_low[1], 2))
-    query_state = after(query_state, far_low)
-    near_grads, cross_q_grad = attend_back(
-        cross_q, d_crossed, crossed, main_keys, main_values, *main_seen[:2], cross_lse,
-        main_seen[2], cross_key, cross_value, (0, rows, 2 * rows, 3 * rows), cores, None, query_state, None,
-        True,
-    )
-    far_arrived, near_grads, cross_q_grad = lax.optimization_barrier(
-        (far_arrived, near_grads, cross_q_grad)
-    )
+        d_crossed = after(d_crossed, adapter_kept)
+
+    cross_weights = (cross_key, cross_value)
+    around_grads, query_state = attend_back(
+        cross_q,
+        d_crossed,
+        crossed,
+        [(main_keys, main_values, base), (far_keys, far_values, far_rows + PAD)],
+        cross_weights,
+        *around_seen,
+        cross_lse,
+        [(0, rows), (2 * rows, rows), (base, cross_far), (base + cross_far, cross_far)],
+        cores,
+    )
+    around_grads, query_state, adapter_arrived, outputs_other = lax.optimization_barrier(
+        (around_grads, query_state, adapter_arrived, outputs_other)
+    )
+    around_parts = [dealt(part) for part in around_grads]
     if staged:
-        adapter_arrived, cross_q_grad = lax.optimization_barrier((adapter_arrived, cross_q_grad))
+        (adapter_grads,) = add_up([[adapter_kept] + adapter_arrived])
+        around_parts = after(around_parts, adapter_grads)
+    memory_low = add_up(around_parts)
+    memory_arrived = [shift(memory_low[i], distance) for i, distance in enumerate((-1, 1, -2, 2))]
+    adapter_arrived = []
+    if staged:
+        adapter_kept = column.cut(adapter_grads, 0)
+        adapter_arrived = column.scatter(after(adapter_grads, memory_low))
+        query_state = after(query_state, adapter_kept)
+    query_state = after(query_state, memory_low)
+    (memory_own,), cross_q_grad = attend_back(
+        cross_q,
+        d_crossed,
+        crossed,
+        [(memory_keys, memory_values, rows)],
+        cross_weights,
+        *here_seen,
+        cross_lse,
+        [(0, rows)],
+        cores,
+        state=query_state,
+        final=True,
+        pad=PAD,
+    )
+    cross_q_grad, memory_own, memory_near, adapter_arrived = lax.optimization_barrier(
+        (cross_q_grad, memory_own, memory_arrived[:2], adapter_arrived)
+    )
     grads_rows = to_rows(cross_q_grad)
-    near_parts = [dealt(after(part, grads_rows)) for part in near_grads]
+    memory_own = dealt(after(memory_own, grads_rows))
     d_tokens, d_attended = before_self(
         core_index, cross_q_grad, grads_rows, cross_queries, self_outputs, d_cross, first,
         first_scale,
     )
     d_attended = to_heads(d_attended)
-    near_low = add_up(after([near_parts[0], near_parts[2]], d_attended))
-    near_arrived = (shift(near_low[0], -1), shift(near_low[1], 1))
-    outputs_other = others(after(outputs_rows, near_low))
-    d_tokens_cols = to_heads(after(d_tokens, near_low))
-    d_attended = after(d_attended, near_low)
-
+    d_tokens_cols = to_heads(d_tokens)
+    memory_own, d_attended, d_tokens_cols = lax.optimization_barrier(
+        (memory_own, d_attended, d_tokens_cols)
+    )
+
+    self_weights = (self_key, self_value, self_query)
     halo_grads, prefix_key_grad, prefix_value_grad, query_state = attend_back(
-        query, d_attended, attended, self_keys, self_values, *halo_seen[:2], self_lse, halo_seen[2],
-        self_key, self_value, (0, self_far, self_base), cores, prefix_rows,
-    )
-    halo_grads, query_state, near_arrived, outputs_other, d_tokens_cols = lax.optimization_barrier(
-        (halo_grads, query_state, near_arrived, outputs_other, d_tokens_cols)
+        query,
+        d_attended,
+        attended,
+        [(halo_keys, halo_values, self_base + PAD)],
+        self_weights,
+        *halo_seen,
+        self_lse,
+        [(0, self_far), (self_far, rows)],
+        cores,
+        prefix_rows,
+    )
+    halo_grads, query_state, memory_far = lax.optimization_barrier(
+        (halo_grads, query_state, memory_arrived[2:])
     )
     halo_parts = [dealt(part) for part in halo_grads]
-    if staged:
-        (adapter_grads,) = add_up([[adapter_kept] + after(adapter_arrived, query_state)])
-        adapter_arrived = column.scatter(adapter_grads)
-        adapter_kept = column.cut(adapter_grads, 0)
-        halo_parts = after(halo_parts, adapter_grads)
-    halo_low = add_up(halo_parts)
-    halo_arrived = (shift(halo_low[0], -2), shift(halo_low[1], -1))
-    pad = ((rows - cross_far, 0), (0, 0))
-    back = ((0, rows - cross_far), (0, 0))
-    near_own, near_arrived, far_arrived, outputs_rows, outputs_other = after(
-        (near_parts[1], near_arrived, far_arrived, outputs_rows, outputs_other), halo_low
-    )
-    memory_sum = sum(
-        [part.astype(f32) for part in near_own + list(near_arrived)],
-        jnp.pad(far_arrived[0], pad).astype(f32) + jnp.pad(far_arrived[1], back).astype(f32),
-    ).astype(bf16)
-    outputs = in_order([outputs_rows] + outputs_other, 0)
-    query_state = after(query_state, halo_low, memory_sum, outputs)
-    ((here_grads,),) = attend_back(
-        query, d_attended, attended, own_keys, own_values, *own_seen[:2], self_lse, own_seen[2],
-        self_key, self_value, (0, rows), cores, None, query_state, self_query,
-    )
-    here_grads, halo_arrived, memory_sum = lax.optimization_barrier(
-        (here_grads, halo_arrived, memory_sum)
-    )
-    if staged:
-        adapter_arrived, here_grads = lax.optimization_barrier((adapter_arrived, here_grads))
-    here_sum = over_cores(here_grads)
-    memory_other = others(after(memory_sum, here_sum))
     kept = [adapter_kept] + adapter_arrived if staged else [adapter_grads]
     both = pack(kept, prefix_key_grad, prefix_value_grad, bias_grads)
+    halo_low = add_up(after(halo_parts, both))
+    halo_arrived = (shift(halo_low[0], -2), shift(halo_low[1], -1))
+    memory_own, memory_near, memory_far, outputs_rows, outputs_other = after(
+        (memory_own, memory_near, memory_far, outputs_rows, outputs_other), halo_low
+    )
+    memory_sum = sum_of(
+        memory_own + list(memory_near), [(memory_far[0], rows - cross_far), (memory_far[1], 0)]
+    )
+    grad_memory = beside(core_index, [memory_sum] + others(memory_sum))
+    outputs = stacked(core_index, [outputs_rows] + outputs_other)
+    query_state, grad_memory, outputs = lax.optimization_barrier((query_state, grad_memory, outputs))
+    both_arrived = []
     if staged:
-        both_arrived = column.exchange([both] * column.size)
-    grad_memory = beside(core_index, [memory_sum] + memory_other)
+        both_arrived = column.exchange([after(both, grad_memory)] * column.size)
+    ((here_grads,),) = attend_back(
+        query,
+        d_attended,
+        attended,
+        [(own_keys, own_values, rows + PAD)],
+        self_weights,
+        *own_seen,
+        self_lse,
+        [(0, rows)],
+        cores,
+        own=0,
+        state=query_state,
+    )
+    here_grads, halo_arrived, both_arrived = lax.optimization_barrier(
+        (here_grads, halo_arrived, both_arrived)
+    )
+    here_sum = over_cores(here_grads)
+    if staged:
+        place = jnp.reshape(column.place, (1,)).astype(jnp.int32)
+        (both,) = gather_rows(place, [both] + both_arrived, None)
+        parts = [both] + plane.exchange([both] * plane.size)
     token_sum = (
         d_tokens_cols.astype(f32)
         + here_sum
@@ -1397,9 +1496,6 @@
     token_other = others(token_sum)
     grad_tokens = beside(core_index, [token_sum] + token_other)
     if staged:
-        place = jnp.reshape(column.place, (1,)).astype(jnp.int32)
-        (both,) = gather_rows(place, [both] + both_arrived, None)
-        parts = [both] + plane.exchange([both] * plane.size)
         place = jnp.reshape(plane.place, (1,)).astype(jnp.int32)
     else:
         parts, place = [lax.psum(both, "seq")], core_index * 0

time: 573 us -> 542 us (0.946); the launches traced: 562 us -> 539 us
  waiting for transfers between devices: 160 us -> 98.6 us
  starting transfers between devices: 108 us -> 142 us
  Pallas kernels: 222 us -> 234 us
  other arithmetic: 21.8 us -> 13.3 us
    ppermute x12, waiting for transfers between devices: 88.2 us -> 31.8 us  [shift(): lax.ppermute(value, 'seq', [(i, i + distance) for i in devices if i + dis...]
    ppermute x12, starting transfers between devices: 44.3 us -> 63.6 us  [shift(): lax.ppermute(value, 'seq', [(i, i + distance) for i in devices if i + dis...]
    ppermute x12, starting transfers between devices: 58.2 us -> 73.2 us  [exchange(): lax.ppermute(values[k], 'seq', pairs[k])]
    ppermute x12, waiting for transfers between devices: 43.9 us -> 33.3 us  [exchange(): lax.ppermute(values[k], 'seq', pairs[k])]
    pallas_call x3 -> x4, Pallas kernels: 50.3 us -> 55.3 us  [attend(): pl.pallas_call(functools.partial(attend_kernel, 0 if prefix is None else...]
    select_n x5 -> x4, other arithmetic: 12.4 us -> 8.39 us  [in_order(): jnp.where(core == 0, jnp.concatenate([first, second], axis=axis), jnp.con...]
    pallas_call x5 -> x6, Pallas kernels: 61 us -> 64.5 us  [one_step(): pl.pallas_call(kernel, out_shape=tuple(outs), grid_spec=pltpu.PrefetchSca...]
    pallas_call x5 -> x4, Pallas kernels: 15.5 us -> 13.7 us  [add_up(): pl.pallas_call(functools.partial(add_kernel, len(lists), each, cut), out_...]
  transfers between devices with their start and end apart: 57 -> 57, of which waited for: 27 -> 24; matrix products, arithmetic and copies ran while one was open for 7% -> 5% of each run, Pallas kernels for 30% -> 33%
where the time goes in v2:
time: 542 us; the launch traced here: 539 us
  Pallas kernels  234 us (43%)
  starting transfers between devices  142 us (26%)
  waiting for transfers between devices  98.6 us (18%)
  local copies, waits for them, and re-layouts  22.4 us (4%)
  between operations  15.2 us (3%)
  other arithmetic  13.3 us (2%)
  matrix products  13 us (2%)
    pallas_call x4, Pallas kernels, attend_back(): pl.pallas_call(functools.partial(attend_back_kernel, 0 if prefix is None...  81.3 us
    ppermute x12, starting transfers between devices, exchange(): lax.ppermute(values[k], 'seq', pairs[k])  73.2 us
    pallas_call x6, Pallas kernels, one_step(): pl.pallas_call(kernel, out_shape=tuple(outs), grid_spec=pltpu.PrefetchSca...  64.5 us
    ppermute x12, starting transfers between devices, shift(): lax.ppermute(value, 'seq', [(i, i + distance) for i in devices if i + dis...  63.6 us
    pallas_call x4, Pallas kernels, attend(): pl.pallas_call(functools.partial(attend_kernel, 0 if prefix is None else...  55.3 us
    ppermute x12, waiting for transfers between devices, exchange(): lax.ppermute(values[k], 'seq', pairs[k])  33.3 us
    ppermute x12, waiting for transfers between devices, shift(): lax.ppermute(value, 'seq', [(i, i + distance) for i in devices if i + dis...  31.8 us
    ppermute x26, waiting for transfers between devices, turn(): lax.ppermute(value, 'head', [(i, (i + distance) % size) for i in range(si...  30.9 us
  transfers between devices with their start and end apart: 57, of which 24 were waited for; matrix products, arithmetic and copies ran while one was open for 5% of the time, Pallas kernels for 33%

profile of v2, /device:TPU:0, one launch (start us, length us, event | category | flops | bytes accessed | tf_op | source)
XLA Modules:
  0.0 538.9 jit_solution(1743437944350003390)
XLA Ops:
  14.0 6.0 %collective-permute-start = (bf16[1024,512]{1,0:T(8,128)(2,1)}, bf16[1024,512]{1,0:T(8,128)(2,1)}, u32[]{:S(2)}, u32[]{:S(2)}) collective-permute-start(bf16[1024,512]{1,0:T(8,128)(2,1)} %constant_dynamic-slice_fusion.13), channel_id=1, source_target_pairs={{0,2},{2,4},{4,6},{6,8},{8,10},{10,12},{12,14},{14,16},{16,18},{18... | collective-permute-start | bytes 3145736 | tf_op jit(solution)/shard_map/ppermute | solution.py:1161
  23.3 5.4 collective-permute-start.1
  38.8 17.3 %shard_map.269 = (f32[8,1024]{1,0:T(8,128)}, f32[8,1024]{1,0:T(8,128)}, f32[512,1024]{1,0:T(8,128)}, bf16[1152,512]{1,0:T(8,128)(2,1)}, bf16[1152,512]{1,0:T(8,128)(2,1)}) custom-call(s32[7,4]{1,0:T(8,128)} %get-tuple-element.204.info, bf16[1024,512]{1,0:T(8,128)(2,1)} %multiply_convert_fusion.refs_0_, s32[1,1024]{1,0:T(1,128)} %get-tuple-element.205.refs_1_.refs_3_, ...), custom_call_target="tpu_custom_call" | custom-call | tf_op jit(solution)/shard_map/pallas_call | solution.py:322
  60.6 5.5 %collective-permute-done.2.refs_9_ = bf16[1024,512]{1,0:T(8,128)(2,1)} collective-permute-done((bf16[1024,512]{1,0:T(8,128)(2,1)}, bf16[1024,512]{1,0:T(8,128)(2,1)}, u32[]{:S(2)}, u32[]{:S(2)}) %collective-permute-start.2) | collective-permute-done | bytes 1048608 | tf_op jit(solution)/shard_map/ppermute | solution.py:1161
  74.9 4.6 collective-permute-start.6
  79.6 8.2 %shard_map.270 = (bf16[1024,512]{1,0:T(8,128)(2,1)}, f32[8,1024]{1,0:T(8,128)}, bf16[1920,512]{1,0:T(8,128)(2,1)}, bf16[1920,512]{1,0:T(8,128)(2,1)}) custom-call(s32[7,4]{1,0:T(8,128)} %get-tuple-element.199.info, bf16[1024,512]{1,0:T(8,128)(2,1)} %multiply_convert_fusion.refs_0_, s32[1,1024]{1,0:T(1,128)} %get-tuple-element.201.refs_1_.refs_3_, ...), custom_call_target="tpu_custom_call" | custom-call | tf_op jit(solution)/shard_map/pallas_call | solution.py:322
  91.6 9.9 %collective-permute-done.6.refs_5_ = bf16[1024,512]{1,0:T(8,128)(2,1)} collective-permute-done((bf16[1024,512]{1,0:T(8,128)(2,1)}, bf16[1024,512]{1,0:T(8,128)(2,1)}, u32[]{:S(2)}, u32[]{:S(2)}) %collective-permute-start.6) | collective-permute-done | bytes 1048608 | tf_op jit(solution)/shard_map/ppermute | solution.py:1161
  105.8 19.5 %collective-permute-start.10 = (bf16[896,512]{1,0:T(8,128)(2,1)}, bf16[896,512]{1,0:T(8,128)(2,1)S(1)}, u32[]{:S(2)}, u32[]{:S(2)}) collective-permute-start(bf16[896,512]{1,0:T(8,128)(2,1)} %get-tuple-element.238), channel_id=1, source_target_pairs={{0,4},{2,6},{4,8},{6,10},{8,12},{10,14},{12,16},{14,18},{16,20},{1... | collective-permute-start | bytes 2752520 | tf_op jit(solution)/shard_map/ppermute | solution.py:1161
  125.4 7.4 %shard_map.271 = (f32[512,1024]{1,0:T(8,128)}, f32[512,1]{1,0:T(8,128)}, bf16[512,512]{1,0:T(8,128)(2,1)}, bf16[512,512]{1,0:T(8,128)(2,1)}) custom-call(s32[1]{0:T(128)} %bitcast.1.core, bf16[1024,512]{1,0:T(8,128)(2,1)} %get-tuple-element.215.refs_0_.refs_2_, bf16[512,512]{1,0:T(8,128)(2,1)} %copy-done.30, bf16[2,512,1024]{2,1,0:T(8,128)(2,1)} %bitcast.26, ...), custom_call_target="tpu_custom_call" | custom-call | tf_op jit(solution)/shard_map/pallas_call | solution.py:822
  137.9 21.5 %shard_map.272 = (f32[8,1024]{1,0:T(8,128)}, f32[8,1024]{1,0:T(8,128)}, f32[512,1024]{1,0:T(8,128)}, bf16[3200,512]{1,0:T(8,128)(2,1)}, bf16[3200,512]{1,0:T(8,128)(2,1)}) custom-call(s32[7,4]{1,0:T(8,128)} %get-tuple-element.227.info, bf16[1024,512]{1,0:T(8,128)(2,1)} %maximum_select_fusion.1.refs_0_, s32[1,1024]{1,0:T(1,128)} %get-tuple-element.228.refs_1_, ...), custom_call_target="tpu_custom_call" | custom-call | tf_op jit(solution)/shard_map/pallas_call | solution.py:322
  159.4 5.1 collective-permute-done.10.refs_5_
  169.3 8.4 %shard_map.273 = (bf16[1024,512]{1,0:T(8,128)(2,1)}, f32[8,1024]{1,0:T(8,128)}, bf16[1920,512]{1,0:T(8,128)(2,1)}, bf16[1920,512]{1,0:T(8,128)(2,1)}) custom-call(s32[13,4]{1,0:T(8,128)} %get-tuple-element.224.info, bf16[1024,512]{1,0:T(8,128)(2,1)} %maximum_select_fusion.1.refs_0_, s32[2,1024]{1,0:T(2,128)} %get-tuple-element.225.refs_1_, ...), custom_call_target="tpu_custom_call" | custom-call | tf_op jit(solution)/shard_map/pallas_call | solution.py:322
  181.5 41.4 %shard_map.274 = (bf16[512,1024]{1,0:T(8,128)(2,1)}, f32[512,1024]{1,0:T(8,128)}, bf16[512,512]{1,0:T(8,128)(2,1)}, bf16[512,512]{1,0:T(8,128)(2,1)}, bf16[528,1...) custom-call(s32[1]{0:T(128)} %bitcast.1.core, bf16[1024,512]{1,0:T(8,128)(2,1)} %get-tuple-element.245.refs_0_.refs_2_, ...), custom_call_target="tpu_custom_call" | custom-call | tf_op jit(solution)/shard_map/pallas_call | solution.py:822
  236.6 5.1 collective-permute-start.18
  243.2 14.4 %shard_map.276 = (bf16[1024,512]{1,0:T(8,128)(2,1)}, bf16[1024,512]{1,0:T(8,128)(2,1)}, bf16[1024,512]{1,0:T(8,128)(2,1)}, bf16[1024,512]{1,0:T(8,128)(2,1)}, bf...) custom-call(s32[25,4]{1,0:T(8,128)} %get-tuple-element.263.info, ...), custom_call_target="tpu_custom_call" | custom-call | tf_op jit(solution)/shard_map/pallas_call | solution.py:568
  267.0 5.5 %shard_map.278 = (bf16[1024,512]{1,0:T(8,128)(2,1)}, bf16[1024,512]{1,0:T(8,128)(2,1)}, bf16[896,512]{1,0:T(8,128)(2,1)}, bf16[896,512]{1,0:T(8,128)(2,1)}) custom-call(bf16[1024,512]{1,0:T(8,128)(2,1)} %get-tuple-element.294.refs_0_, bf16[1024,512]{1,0:T(8,128)(2,1)} %copy-done.14, bf16[1024,512]{1,0:T(8,128)(2,1)} %get-tuple-element.296.refs_2_, ...), custom_call_target="tpu_custom_call" | custom-call | tf_op jit(solution)/shard_map/pallas_call | solution.py:1008
  273.7 14.9 %collective-permute-start.27 = (bf16[1024,512]{1,0:T(8,128)(2,1)}, bf16[1024,512]{1,0:T(8,128)(2,1)S(1)}, u32[]{:S(2)}, u32[]{:S(2)}) collective-permute-start(bf16[1024,512]{1,0:T(8,128)(2,1)} %get-tuple-element.303), channel_id=1, source_target_pairs={{0,2},{2,4},{4,6},{6,8},{8,10},{10,12},{12,14},{14,16},{16,18},{18... | collective-permute-start | bytes 3145736 | tf_op jit(solution)/shard_map/ppermute | solution.py:1161
  288.7 30.6 %collective-permute-start.28 = (bf16[32,1024]{1,0:T(8,128)(2,1)S(1)}, bf16[32,1024]{1,0:T(8,128)(2,1)S(1)}, u32[]{:S(2)}, u32[]{:S(2)}) collective-permute-start(bf16[32,1024]{1,0:T(8,128)(2,1)S(1)} %get-tuple-element.397), channel_id=1, source_target_pairs={{0,8},{2,10},{4,12},{6,14},{8,0},{10,2},{12,4},{14,6},{16,24},{18,... | collective-permute-start | bytes 196616 | tf_op jit(solution)/shard_map/ppermute | solution.py:1175
  322.4 28.7 %shard_map.279 = (bf16[1024,512]{1,0:T(8,128)(2,1)}, bf16[1024,512]{1,0:T(8,128)(2,1)}, bf16[1024,512]{1,0:T(8,128)(2,1)}) custom-call(s32[7,4]{1,0:T(8,128)} %get-tuple-element.200.info, bf16[1024,512]{1,0:T(8,128)(2,1)} %maximum_select_fusion.1.refs_0_, bf16[1024,512]{1,0:T(8,128)(2,1)} %maximum_select_fusion.2.refs_1_, ...), custom_call_target="tpu_custom_call" | custom-call | tf_op jit(solution)/shard_map/pallas_call | solution.py:568
  356.1 5.5 %collective-permute-start.36 = (bf16[896,512]{1,0:T(8,128)(2,1)}, bf16[896,512]{1,0:T(8,128)(2,1)}, u32[]{:S(2)}, u32[]{:S(2)}) collective-permute-start(bf16[896,512]{1,0:T(8,128)(2,1)} %get-tuple-element.305), channel_id=1, source_target_pairs={{0,4},{2,6},{4,8},{6,10},{8,12},{10,14},{12,16},{14,18},{16,20},{1... | collective-permute-start | bytes 2752520 | tf_op jit(solution)/shard_map/ppermute | solution.py:1161
  361.6 7.8 %shard_map.280 = (f32[512,512]{1,0:T(8,128)}, bf16[512,512]{1,0:T(8,128)(2,1)}, bf16[512,512]{1,0:T(8,128)(2,1)}, bf16[512,512]{1,0:T(8,128)(2,1)}) custom-call(s32[1]{0:T(128)} %bitcast.1.core, bf16[1024,512]{1,0:T(8,128)(2,1)} %get-tuple-element.313.refs_0_, bf16[512,512]{1,0:T(8,128)(2,1)} %copy-done.31, bf16[2,1024,512]{2,1,0:T(8,128)(2,1)} %bitcast.32, ...), custom_call_target="tpu_custom_call" | custom-call | tf_op jit(solution)/shard_map/pallas_call | solution.py:822
  375.4 13.9 %shard_map.281 = (bf16[768,512]{1,0:T(8,128)(2,1)}, bf16[768,512]{1,0:T(8,128)(2,1)}, bf16[1024,512]{1,0:T(8,128)(2,1)}, bf16[1024,512]{1,0:T(8,128)(2,1)}, f32[...) custom-call(s32[7,4]{1,0:T(8,128)} %get-tuple-element.199.info, ...), custom_call_target="tpu_custom_call" | custom-call | tf_op jit(solution)/shard_map/pallas_call | solution.py:568
  389.3 11.2 %collective-permute-done.36.refs_5_ = bf16[896,512]{1,0:T(8,128)(2,1)} collective-permute-done((bf16[896,512]{1,0:T(8,128)(2,1)}, bf16[896,512]{1,0:T(8,128)(2,1)}, u32[]{:S(2)}, u32[]{:S(2)}) %collective-permute-start.36) | collective-permute-done | bytes 917536 | tf_op jit(solution)/shard_map/ppermute | solution.py:1161
  408.9 4.4 shard_map.284.refs_0_
  419.1 4.7 shard_map.285
  423.8 13.0 %collective-permute-start.42 = (bf16[64,1024]{1,0:T(8,128)(2,1)S(1)}, bf16[64,1024]{1,0:T(8,128)(2,1)S(1)}, u32[]{:S(2)}, u32[]{:S(2)}) collective-permute-start(bf16[64,1024]{1,0:T(8,128)(2,1)S(1)} %copy-done.32), channel_id=1, source_target_pairs={{0,8},{2,10},{4,12},{6,14},{8,0},{10,2},{12,4},{14,6},{16,24},{18,... | collective-permute-start | bytes 393224 | tf_op jit(solution)/shard_map/ppermute | solution.py:1175
  436.8 15.7 %collective-permute-start.43 = (bf16[64,1024]{1,0:T(8,128)(2,1)S(1)}, bf16[64,1024]{1,0:T(8,128)(2,1)S(1)}, u32[]{:S(2)}, u32[]{:S(2)}) collective-permute-start(bf16[64,1024]{1,0:T(8,128)(2,1)S(1)} %copy-done.32), channel_id=1, source_target_pairs={{0,16},{2,18},{4,20},{6,22},{8,24},{10,26},{12,28},{14,30},{16,0},... | collective-permute-start | bytes 393224 | tf_op jit(solution)/shard_map/ppermute | solution.py:1175
  453.9 24.3 %shard_map.287 = (bf16[1024,512]{1,0:T(8,128)(2,1)}, bf16[1024,512]{1,0:T(8,128)(2,1)}) custom-call(s32[7,4]{1,0:T(8,128)} %get-tuple-element.204.info, bf16[1024,512]{1,0:T(8,128)(2,1)} %multiply_convert_fusion.refs_0_, bf16[1024,512]{1,0:T(8,128)(2,1)} %maximum_select_fusion.3.refs_1_, bf16[1024,512]{1,0:T(8,128)(2,1)} %get-tuple-element.215.refs_0_.refs_2_, ...), custom_call_target="tpu_custom_call" | custom-call | tf_op jit(solution)/shard_map/pallas_call | solution.py:568
  478.2 9.5 %collective-permute-done.42.refs_1_ = bf16[64,1024]{1,0:T(8,128)(2,1)S(1)} collective-permute-done((bf16[64,1024]{1,0:T(8,128)(2,1)S(1)}, bf16[64,1024]{1,0:T(8,128)(2,1)S(1)}, u32[]{:S(2)}, u32[]{:S(2)}) %collective-permute-start.42) | collective-permute-done | bytes 131104 | tf_op jit(solution)/shard_map/ppermute | solution.py:1175
  487.7 15.7 %collective-permute-done.43.refs_2_ = bf16[64,1024]{1,0:T(8,128)(2,1)S(1)} collective-permute-done((bf16[64,1024]{1,0:T(8,128)(2,1)S(1)}, bf16[64,1024]{1,0:T(8,128)(2,1)S(1)}, u32[]{:S(2)}, u32[]{:S(2)}) %collective-permute-start.43) | collective-permute-done | bytes 131104 | tf_op jit(solution)/shard_map/ppermute | solution.py:1175
  515.6 4.5 shard_map.288
  521.9 6.3 %collective-permute-done.48.refs_2_ = bf16[160,1024]{1,0:T(8,128)(2,1)S(1)} collective-permute-done((bf16[160,1024]{1,0:T(8,128)(2,1)}, bf16[160,1024]{1,0:T(8,128)(2,1)S(1)}, u32[]{:S(2)}, u32[]{:S(2)}) %collective-permute-start.48) | collective-permute-done | bytes 327712 | tf_op jit(solution)/shard_map/ppermute | solution.py:1175
  (238 shorter events, 127.8 us)
Async XLA Ops:
  7.2 118.2 %all-gather.15.cloned.1.call-start = ((), (), s32[]{:S(2)}) async-start(), calls=%async_computation | async-start | bytes 3145728 | tf_op jit(solution)/shard_map/all_gather | solution.py:1279
  11.3 114.1 %all-gather.17.cloned.1.call-start = ((), (), s32[]{:S(2)}) async-start(), calls=%async_computation.1 | async-start | bytes 3145728 | tf_op jit(solution)/shard_map/all_gather | solution.py:1279
  12.1 168.6 %all-gather.21.cloned.1.call-start = ((), (), s32[]{:S(2)}) async-start(), calls=%async_computation.3 | async-start | bytes 1572864 | tf_op jit(solution)/shard_map/all_gather | solution.py:1279
  14.0 52.1 %collective-permute-start = (bf16[1024,512]{1,0:T(8,128)(2,1)}, bf16[1024,512]{1,0:T(8,128)(2,1)}, u32[]{:S(2)}, u32[]{:S(2)}) collective-permute-start(bf16[1024,512]{1,0:T(8,128)(2,1)} %constant_dynamic-slice_fusion.13), channel_id=1, source_target_pairs={{0,2},{2,4},{4,6},{6,8},{8,10},{10,12},{12,14},{14,16},{16,18},{18... | collective-permute-start | bytes 3145736 | tf_op jit(solution)/shard_map/ppermute | solution.py:1161
  21.1 45.0 %collective-permute-start.2 = (bf16[1024,512]{1,0:T(8,128)(2,1)}, bf16[1024,512]{1,0:T(8,128)(2,1)}, u32[]{:S(2)}, u32[]{:S(2)}) collective-permute-start(bf16[1024,512]{1,0:T(8,128)(2,1)} %constant_dynamic-slice_fusion.12), channel_id=1, source_target_pairs={{2,0},{4,2},{6,4},{8,6},{10,8},{12,10},{14,12},{16,14},{18,16},{20... | collective-permute-start | bytes 3145736 | tf_op jit(solution)/shard_map/ppermute | solution.py:1161
  23.3 37.3 %collective-permute-start.1 = (bf16[768,512]{1,0:T(8,128)(2,1)}, bf16[768,512]{1,0:T(8,128)(2,1)}, u32[]{:S(2)}, u32[]{:S(2)}) collective-permute-start(bf16[768,512]{1,0:T(8,128)(2,1)} %dynamic-slice), channel_id=1, source_target_pairs={{0,4},{2,6},{4,8},{6,10},{8,12},{10,14},{12,16},{14,18},{16,20},{1... | collective-permute-start | bytes 2359304 | tf_op jit(solution)/shard_map/ppermute | solution.py:1161
  67.0 113.7 %all-gather.23.cloned.1.call-start = ((), (), s32[]{:S(2)}) async-start(), calls=%async_computation.4 | async-start | bytes 1572864 | tf_op jit(solution)/shard_map/all_gather | solution.py:1279
  67.9 112.8 %all-gather.19.cloned.1.call-start = ((), (), s32[]{:S(2)}) async-start(), calls=%async_computation.2 | async-start | bytes 3145728 | tf_op jit(solution)/shard_map/all_gather | solution.py:1279
  68.5 112.2 %all-gather.25.cloned.1.call-start = ((), (), s32[]{:S(2)}) async-start(), calls=%async_computation.5 | async-start | bytes 12582912 | tf_op jit(solution)/shard_map/all_gather | solution.py:1279
  69.1 111.7 %all-gather.27.cloned.1.call-start = ((), (), s32[]{:S(2)}) async-start(), calls=%async_computation.6 | async-start | bytes 12582912 | tf_op jit(solution)/shard_map/all_gather | solution.py:1279
  74.8 16.0 %collective-permute-start.7 = (bf16[1024,512]{1,0:T(8,128)(2,1)}, bf16[1024,512]{1,0:T(8,128)(2,1)S(1)}, u32[]{:S(2)}, u32[]{:S(2)}) collective-permute-start(bf16[1024,512]{1,0:T(8,128)(2,1)} %collective-permute-done.2.refs_9_), channel_id=1, source_target_pairs={{0,1},{1,0},{2,3},{3,2},{4,5},{5,4},{6,7},{7,6},{8,9},{9,8},{10,11... | collective-permute-start | bytes 3145736 | tf_op jit(solution)/shard_map/ppermute | solution.py:1137
  74.9 26.6 %collective-permute-start.6 = (bf16[1024,512]{1,0:T(8,128)(2,1)}, bf16[1024,512]{1,0:T(8,128)(2,1)}, u32[]{:S(2)}, u32[]{:S(2)}) collective-permute-start(bf16[1024,512]{1,0:T(8,128)(2,1)} %constant_dynamic-slice_fusion.12), channel_id=1, source_target_pairs={{0,2},{2,4},{4,6},{6,8},{8,10},{10,12},{12,14},{14,16},{16,18},{18... | collective-permute-start | bytes 3145736 | tf_op jit(solution)/shard_map/ppermute | solution.py:1161
  104.5 54.8 %collective-permute-start.11 = (bf16[896,512]{1,0:T(8,128)(2,1)}, bf16[896,512]{1,0:T(8,128)(2,1)S(1)}, u32[]{:S(2)}, u32[]{:S(2)}) collective-permute-start(bf16[896,512]{1,0:T(8,128)(2,1)} %get-tuple-element.239), channel_id=1, source_target_pairs={{4,0},{6,2},{8,4},{10,6},{12,8},{14,10},{16,12},{18,14},{20,16},{2... | collective-permute-start | bytes 2752520 | tf_op jit(solution)/shard_map/ppermute | solution.py:1161
  105.8 58.6 %collective-permute-start.10 = (bf16[896,512]{1,0:T(8,128)(2,1)}, bf16[896,512]{1,0:T(8,128)(2,1)S(1)}, u32[]{:S(2)}, u32[]{:S(2)}) collective-permute-start(bf16[896,512]{1,0:T(8,128)(2,1)} %get-tuple-element.238), channel_id=1, source_target_pairs={{0,4},{2,6},{4,8},{6,10},{8,12},{10,14},{12,16},{14,18},{16,20},{1... | collective-permute-start | bytes 2752520 | tf_op jit(solution)/shard_map/ppermute | solution.py:1161
  227.9 29.7 %collective-permute-start.21 = (bf16[512,1024]{1,0:T(8,128)(2,1)S(1)}, bf16[512,1024]{1,0:T(8,128)(2,1)}, u32[]{:S(2)}, u32[]{:S(2)}) collective-permute-start(bf16[512,1024]{1,0:T(8,128)(2,1)S(1)} %copy-done.9), channel_id=1, source_target_pairs={{0,1},{1,0},{2,3},{3,2},{4,5},{5,4},{6,7},{7,6},{8,9},{9,8},{10,11... | collective-permute-start | bytes 3145736 | tf_op jit(solution)/shard_map/ppermute | solution.py:1137
  236.6 21.0 %collective-permute-start.18 = (bf16[128,1024]{1,0:T(8,128)(2,1)S(1)}, bf16[128,1024]{1,0:T(8,128)(2,1)S(1)}, u32[]{:S(2)}, u32[]{:S(2)}) collective-permute-start(bf16[128,1024]{1,0:T(8,128)(2,1)S(1)} %get-tuple-element.393), channel_id=1, source_target_pairs={{0,2},{2,0},{4,6},{6,4},{8,10},{10,8},{12,14},{14,12},{16,18},{18,... | collective-permute-start | bytes 786440 | tf_op jit(solution)/shard_map/ppermute | solution.py:1175
  241.7 16.0 %collective-permute-start.20 = (bf16[128,1024]{1,0:T(8,128)(2,1)S(1)}, bf16[128,1024]{1,0:T(8,128)(2,1)S(1)}, u32[]{:S(2)}, u32[]{:S(2)}) collective-permute-start(bf16[128,1024]{1,0:T(8,128)(2,1)S(1)} %get-tuple-element.391), channel_id=1, source_target_pairs={{0,6},{2,4},{4,2},{6,0},{8,14},{10,12},{12,10},{14,8},{16,22},{18,... | collective-permute-start | bytes 786440 | tf_op jit(solution)/shard_map/ppermute | solution.py:1175
  272.4 78.7 %collective-permute-start.26 = (bf16[1024,512]{1,0:T(8,128)(2,1)}, bf16[1024,512]{1,0:T(8,128)(2,1)S(1)}, u32[]{:S(2)}, u32[]{:S(2)}) collective-permute-start(bf16[1024,512]{1,0:T(8,128)(2,1)} %get-tuple-element.302), channel_id=1, source_target_pairs={{2,0},{4,2},{6,4},{8,6},{10,8},{12,10},{14,12},{16,14},{18,16},{20... | collective-permute-start | bytes 3145736 | tf_op jit(solution)/shard_map/ppermute | solution.py:1161
  273.7 77.5 %collective-permute-start.27 = (bf16[1024,512]{1,0:T(8,128)(2,1)}, bf16[1024,512]{1,0:T(8,128)(2,1)S(1)}, u32[]{:S(2)}, u32[]{:S(2)}) collective-permute-start(bf16[1024,512]{1,0:T(8,128)(2,1)} %get-tuple-element.303), channel_id=1, source_target_pairs={{0,2},{2,4},{4,6},{6,8},{8,10},{10,12},{12,14},{14,16},{16,18},{18... | collective-permute-start | bytes 3145736 | tf_op jit(solution)/shard_map/ppermute | solution.py:1161
  288.7 62.4 %collective-permute-start.28 = (bf16[32,1024]{1,0:T(8,128)(2,1)S(1)}, bf16[32,1024]{1,0:T(8,128)(2,1)S(1)}, u32[]{:S(2)}, u32[]{:S(2)}) collective-permute-start(bf16[32,1024]{1,0:T(8,128)(2,1)S(1)} %get-tuple-element.397), channel_id=1, source_target_pairs={{0,8},{2,10},{4,12},{6,14},{8,0},{10,2},{12,4},{14,6},{16,24},{18,... | collective-permute-start | bytes 196616 | tf_op jit(solution)/shard_map/ppermute | solution.py:1175
  319.3 31.8 %collective-permute-start.29 = (bf16[32,1024]{1,0:T(8,128)(2,1)S(1)}, bf16[32,1024]{1,0:T(8,128)(2,1)S(1)}, u32[]{:S(2)}, u32[]{:S(2)}) collective-permute-start(bf16[32,1024]{1,0:T(8,128)(2,1)S(1)} %get-tuple-element.396), channel_id=1, source_target_pairs={{0,16},{2,18},{4,20},{6,22},{8,24},{10,26},{12,28},{14,30},{16,0},... | collective-permute-start | bytes 196616 | tf_op jit(solution)/shard_map/ppermute | solution.py:1175
  319.3 31.8 %collective-permute-start.30 = (bf16[32,1024]{1,0:T(8,128)(2,1)S(1)}, bf16[32,1024]{1,0:T(8,128)(2,1)S(1)}, u32[]{:S(2)}, u32[]{:S(2)}) collective-permute-start(bf16[32,1024]{1,0:T(8,128)(2,1)S(1)} %get-tuple-element.395), channel_id=1, source_target_pairs={{0,24},{2,26},{4,28},{6,30},{8,16},{10,18},{12,20},{14,22},{16,8},... | collective-permute-start | bytes 196616 | tf_op jit(solution)/shard_map/ppermute | solution.py:1175
  354.7 20.7 %collective-permute-start.32 = (bf16[1024,512]{1,0:T(8,128)(2,1)}, bf16[1024,512]{1,0:T(8,128)(2,1)}, u32[]{:S(2)}, u32[]{:S(2)}) collective-permute-start(bf16[1024,512]{1,0:T(8,128)(2,1)} %get-tuple-element.315), channel_id=1, source_target_pairs={{0,1},{1,0},{2,3},{3,2},{4,5},{5,4},{6,7},{7,6},{8,9},{9,8},{10,11... | collective-permute-start | bytes 3145736 | tf_op jit(solution)/shard_map/ppermute | solution.py:1137
  354.8 34.4 %collective-permute-start.35 = (bf16[896,512]{1,0:T(8,128)(2,1)}, bf16[896,512]{1,0:T(8,128)(2,1)S(1)}, u32[]{:S(2)}, u32[]{:S(2)}) collective-permute-start(bf16[896,512]{1,0:T(8,128)(2,1)} %get-tuple-element.304), channel_id=1, source_target_pairs={{4,0},{6,2},{8,4},{10,6},{12,8},{14,10},{16,12},{18,14},{20,16},{2... | collective-permute-start | bytes 2752520 | tf_op jit(solution)/shard_map/ppermute | solution.py:1161
  356.1 44.4 %collective-permute-start.36 = (bf16[896,512]{1,0:T(8,128)(2,1)}, bf16[896,512]{1,0:T(8,128)(2,1)}, u32[]{:S(2)}, u32[]{:S(2)}) collective-permute-start(bf16[896,512]{1,0:T(8,128)(2,1)} %get-tuple-element.305), channel_id=1, source_target_pairs={{0,4},{2,6},{4,8},{6,10},{8,12},{10,14},{12,16},{14,18},{16,20},{1... | collective-permute-start | bytes 2752520 | tf_op jit(solution)/shard_map/ppermute | solution.py:1161
  413.5 64.7 %collective-permute-start.41 = (bf16[1024,512]{1,0:T(8,128)(2,1)}, bf16[1024,512]{1,0:T(8,128)(2,1)S(1)}, u32[]{:S(2)}, u32[]{:S(2)}) collective-permute-start(bf16[1024,512]{1,0:T(8,128)(2,1)} %get-tuple-element.354), channel_id=1, source_target_pairs={{2,0},{4,2},{6,4},{8,6},{10,8},{12,10},{14,12},{16,14},{18,16},{20... | collective-permute-start | bytes 3145736 | tf_op jit(solution)/shard_map/ppermute | solution.py:1161
  414.8 63.4 %collective-permute-start.40 = (bf16[768,512]{1,0:T(8,128)(2,1)}, bf16[768,512]{1,0:T(8,128)(2,1)}, u32[]{:S(2)}, u32[]{:S(2)}) collective-permute-start(bf16[768,512]{1,0:T(8,128)(2,1)} %get-tuple-element.353), channel_id=1, source_target_pairs={{4,0},{6,2},{8,4},{10,6},{12,8},{14,10},{16,12},{18,14},{20,16},{2... | collective-permute-start | bytes 2359304 | tf_op jit(solution)/shard_map/ppermute | solution.py:1161
  423.8 63.9 %collective-permute-start.42 = (bf16[64,1024]{1,0:T(8,128)(2,1)S(1)}, bf16[64,1024]{1,0:T(8,128)(2,1)S(1)}, u32[]{:S(2)}, u32[]{:S(2)}) collective-permute-start(bf16[64,1024]{1,0:T(8,128)(2,1)S(1)} %copy-done.32), channel_id=1, source_target_pairs={{0,8},{2,10},{4,12},{6,14},{8,0},{10,2},{12,4},{14,6},{16,24},{18,... | collective-permute-start | bytes 393224 | tf_op jit(solution)/shard_map/ppermute | solution.py:1175
  436.8 66.7 %collective-permute-start.43 = (bf16[64,1024]{1,0:T(8,128)(2,1)S(1)}, bf16[64,1024]{1,0:T(8,128)(2,1)S(1)}, u32[]{:S(2)}, u32[]{:S(2)}) collective-permute-start(bf16[64,1024]{1,0:T(8,128)(2,1)S(1)} %copy-done.32), channel_id=1, source_target_pairs={{0,16},{2,18},{4,20},{6,22},{8,24},{10,26},{12,28},{14,30},{16,0},... | collective-permute-start | bytes 393224 | tf_op jit(solution)/shard_map/ppermute | solution.py:1175
  452.5 51.0 %collective-permute-start.44 = (bf16[64,1024]{1,0:T(8,128)(2,1)S(1)}, bf16[64,1024]{1,0:T(8,128)(2,1)S(1)}, u32[]{:S(2)}, u32[]{:S(2)}) collective-permute-start(bf16[64,1024]{1,0:T(8,128)(2,1)S(1)} %copy-done.32), channel_id=1, source_target_pairs={{0,24},{2,26},{4,28},{6,30},{8,16},{10,18},{12,20},{14,22},{16,8},... | collective-permute-start | bytes 393224 | tf_op jit(solution)/shard_map/ppermute | solution.py:1175
  511.1 17.1 %collective-permute-start.48 = (bf16[160,1024]{1,0:T(8,128)(2,1)}, bf16[160,1024]{1,0:T(8,128)(2,1)S(1)}, u32[]{:S(2)}, u32[]{:S(2)}) collective-permute-start(bf16[160,1024]{1,0:T(8,128)(2,1)} %shard_map.289.refs_0_), channel_id=1, source_target_pairs={{0,4},{2,6},{4,0},{6,2},{8,12},{10,14},{12,8},{14,10},{16,20},{18,... | collective-permute-start | bytes 983048 | tf_op jit(solution)/shard_map/ppermute | solution.py:1175
  511.1 17.1 %collective-permute-start.49 = (bf16[160,1024]{1,0:T(8,128)(2,1)}, bf16[160,1024]{1,0:T(8,128)(2,1)S(1)}, u32[]{:S(2)}, u32[]{:S(2)}) collective-permute-start(bf16[160,1024]{1,0:T(8,128)(2,1)} %shard_map.289.refs_0_), channel_id=1, source_target_pairs={{0,6},{2,4},{4,2},{6,0},{8,14},{10,12},{12,10},{14,8},{16,22},{18,... | collective-permute-start | bytes 983048 | tf_op jit(solution)/shard_map/ppermute | solution.py:1175
  (74 other events, 501.5 us)
Sparse Core Ops, SparseCore 0:
  11.4 13.2 all-gather.14
  26.3 11.7 all-gather.16
  67.1 26.1 all-gather.20
  94.7 10.3 all-gather.22
  106.5 11.5 all-gather.18
  119.5 21.0 all-gather.24
  142.1 21.4 all-gather.26

commit v3 on v2

--- a/solution.py
+++ b/solution.py
@@ -963,7 +963,7 @@
 def beside(core, parts):
     rows, width = parts[0].shape
     cores = len(parts)
-    count = 2
+    count = 1
 
     def part_spec(k):
         def place(which, block, core):
@@ -1366,7 +1366,7 @@
     adapter_grads = dealt(after(adapter_grads, d_crossed))
     outputs_other = others(after(outputs_rows, d_crossed))
     ups_count = adapter_up.shape[0]
-    staged = shards % 4 == 0 and shards & (shards - 1) == 0 and 2 * ups_count % shards == 0
+    staged = shards >= 4 and shards & (shards - 1) == 0 and 2 * ups_count % (16 * shards) == 0
     if staged:
         plane, column = Ring(4, 1), Ring(shards // 4, 4)
 
@@ -1487,6 +1487,7 @@
         place = jnp.reshape(column.place, (1,)).astype(jnp.int32)
         (both,) = gather_rows(place, [both] + both_arrived, None)
         parts = [both] + plane.exchange([both] * plane.size)
+    d_tokens_cols = after(d_tokens_cols, both)
     token_sum = (
         d_tokens_cols.astype(f32)
         + here_sum

time: 542 us -> 533 us (0.983); the launches traced: 539 us -> 523 us
  waiting for transfers between devices: 98.6 us -> 76.7 us
  Pallas kernels: 234 us -> 241 us
    ppermute x12, waiting for transfers between devices: 33.3 us -> 22.1 us  [exchange(): lax.ppermute(values[k], 'seq', pairs[k])]
    ppermute x12, starting transfers between devices: 63.6 us -> 53.8 us  [shift(): lax.ppermute(value, 'seq', [(i, i + distance) for i in devices if i + dis...]
    ppermute x12, waiting for transfers between devices: 31.8 us -> 23.6 us  [shift(): lax.ppermute(value, 'seq', [(i, i + distance) for i in devices if i + dis...]
    ppermute x12, starting transfers between devices: 73.2 us -> 80.4 us  [exchange(): lax.ppermute(values[k], 'seq', pairs[k])]
    pallas_call x4, Pallas kernels: 81.3 us -> 88.5 us  [attend_back(): pl.pallas_call(functools.partial(attend_back_kernel, 0 if prefix is None...]
    unnamed x98 -> x102, local copies, waits for them, and re-layouts: 10.3 us -> 10.9 us
  transfers between devices with their start and end apart: 57 -> 57, of which waited for: 24 -> 23; matrix products, arithmetic and copies ran while one was open for 5% -> 5% of each run, Pallas kernels for 33% -> 35%
where the time goes in v3:
time: 533 us; the launch traced here: 523 us
  Pallas kernels  241 us (45%)
  starting transfers between devices  140 us (26%)
  waiting for transfers between devices  76.7 us (14%)
  local copies, waits for them, and re-layouts  23 us (4%)
  between operations  15.2 us (3%)
  other arithmetic  13.5 us (3%)
  matrix products  13 us (2%)
    pallas_call x4, Pallas kernels, attend_back(): pl.pallas_call(functools.partial(attend_back_kernel, 0 if prefix is None...  88.5 us
    ppermute x12, starting transfers between devices, exchange(): lax.ppermute(values[k], 'seq', pairs[k])  80.4 us
    pallas_call x6, Pallas kernels, one_step(): pl.pallas_call(kernel, out_shape=tuple(outs), grid_spec=pltpu.PrefetchSca...  64.3 us
    pallas_call x4, Pallas kernels, attend(): pl.pallas_call(functools.partial(attend_kernel, 0 if prefix is None else...  57.4 us
    ppermute x12, starting transfers between devices, shift(): lax.ppermute(value, 'seq', [(i, i + distance) for i in devices if i + dis...  53.8 us
    ppermute x26, waiting for transfers between devices, turn(): lax.ppermute(value, 'head', [(i, (i + distance) % size) for i in range(si...  28.4 us
    ppermute x12, waiting for transfers between devices, shift(): lax.ppermute(value, 'seq', [(i, i + distance) for i in devices if i + dis...  23.6 us
    ppermute x12, waiting for transfers between devices, exchange(): lax.ppermute(values[k], 'seq', pairs[k])  22.1 us
  transfers between devices with their start and end apart: 57, of which 23 were waited for; matrix products, arithmetic and copies ran while one was open for 5% of the time, Pallas kernels for 35%

profile of v3, /device:TPU:0, one launch (start us, length us, event | category | flops | bytes accessed | tf_op | source)
XLA Modules:
  0.0 522.7 jit_solution(6976237380848017251)
XLA Ops:
  7.2 4.1 multiply_convert_fusion.refs_0_
  14.0 6.0 %collective-permute-start = (bf16[1024,512]{1,0:T(8,128)(2,1)}, bf16[1024,512]{1,0:T(8,128)(2,1)}, u32[]{:S(2)}, u32[]{:S(2)}) collective-permute-start(bf16[1024,512]{1,0:T(8,128)(2,1)} %constant_dynamic-slice_fusion.13), channel_id=1, source_target_pairs={{0,2},{2,4},{4,6},{6,8},{8,10},{10,12},{12,14},{14,16},{16,18},{18... | collective-permute-start | bytes 3145736 | tf_op jit(solution)/shard_map/ppermute | solution.py:1161
  23.3 5.4 %collective-permute-start.1 = (bf16[768,512]{1,0:T(8,128)(2,1)}, bf16[768,512]{1,0:T(8,128)(2,1)}, u32[]{:S(2)}, u32[]{:S(2)}) collective-permute-start(bf16[768,512]{1,0:T(8,128)(2,1)} %dynamic-slice), channel_id=1, source_target_pairs={{0,4},{2,6},{4,8},{6,10},{8,12},{10,14},{12,16},{14,18},{16,20},{1... | collective-permute-start | bytes 2359304 | tf_op jit(solution)/shard_map/ppermute | solution.py:1161
  38.8 17.4 %shard_map.269 = (f32[8,1024]{1,0:T(8,128)}, f32[8,1024]{1,0:T(8,128)}, f32[512,1024]{1,0:T(8,128)}, bf16[1152,512]{1,0:T(8,128)(2,1)}, bf16[1152,512]{1,0:T(8,128)(2,1)}) custom-call(s32[7,4]{1,0:T(8,128)} %get-tuple-element.205.info, bf16[1024,512]{1,0:T(8,128)(2,1)} %multiply_convert_fusion.refs_0_, s32[1,1024]{1,0:T(1,128)} %get-tuple-element.206.refs_1_.refs_3_, ...), custom_call_target="tpu_custom_call" | custom-call | tf_op jit(solution)/shard_map/pallas_call | solution.py:322
  60.7 5.4 %collective-permute-done.2.refs_9_ = bf16[1024,512]{1,0:T(8,128)(2,1)} collective-permute-done((bf16[1024,512]{1,0:T(8,128)(2,1)}, bf16[1024,512]{1,0:T(8,128)(2,1)}, u32[]{:S(2)}, u32[]{:S(2)}) %collective-permute-start.2) | collective-permute-done | bytes 1048608 | tf_op jit(solution)/shard_map/ppermute | solution.py:1161
  74.9 4.6 collective-permute-start.6
  79.6 8.2 %shard_map.270 = (bf16[1024,512]{1,0:T(8,128)(2,1)}, f32[8,1024]{1,0:T(8,128)}, bf16[1920,512]{1,0:T(8,128)(2,1)}, bf16[1920,512]{1,0:T(8,128)(2,1)}) custom-call(s32[7,4]{1,0:T(8,128)} %get-tuple-element.200.info, bf16[1024,512]{1,0:T(8,128)(2,1)} %multiply_convert_fusion.refs_0_, s32[1,1024]{1,0:T(1,128)} %get-tuple-element.202.refs_1_.refs_3_, ...), custom_call_target="tpu_custom_call" | custom-call | tf_op jit(solution)/shard_map/pallas_call | solution.py:322
  91.6 9.9 %collective-permute-done.6.refs_5_ = bf16[1024,512]{1,0:T(8,128)(2,1)} collective-permute-done((bf16[1024,512]{1,0:T(8,128)(2,1)}, bf16[1024,512]{1,0:T(8,128)(2,1)}, u32[]{:S(2)}, u32[]{:S(2)}) %collective-permute-start.6) | collective-permute-done | bytes 1048608 | tf_op jit(solution)/shard_map/ppermute | solution.py:1161
  105.7 19.5 %collective-permute-start.10 = (bf16[896,512]{1,0:T(8,128)(2,1)}, bf16[896,512]{1,0:T(8,128)(2,1)S(1)}, u32[]{:S(2)}, u32[]{:S(2)}) collective-permute-start(bf16[896,512]{1,0:T(8,128)(2,1)} %get-tuple-element.239), channel_id=1, source_target_pairs={{0,4},{2,6},{4,8},{6,10},{8,12},{10,14},{12,16},{14,18},{16,20},{1... | collective-permute-start | bytes 2752520 | tf_op jit(solution)/shard_map/ppermute | solution.py:1161
  125.3 7.3 %shard_map.271 = (f32[512,1024]{1,0:T(8,128)}, f32[512,1]{1,0:T(8,128)}, bf16[512,512]{1,0:T(8,128)(2,1)}, bf16[512,512]{1,0:T(8,128)(2,1)}) custom-call(s32[1]{0:T(128)} %bitcast.1.core, bf16[1024,512]{1,0:T(8,128)(2,1)} %get-tuple-element.216.refs_0_.refs_2_, bf16[512,512]{1,0:T(8,128)(2,1)} %copy-done.32, bf16[2,512,1024]{2,1,0:T(8,128)(2,1)} %bitcast.26, ...), custom_call_target="tpu_custom_call" | custom-call | tf_op jit(solution)/shard_map/pallas_call | solution.py:822
  137.6 23.6 %shard_map.272 = (f32[8,1024]{1,0:T(8,128)}, f32[8,1024]{1,0:T(8,128)}, f32[512,1024]{1,0:T(8,128)}, bf16[3200,512]{1,0:T(8,128)(2,1)}, bf16[3200,512]{1,0:T(8,128)(2,1)}) custom-call(s32[7,4]{1,0:T(8,128)} %get-tuple-element.228.info, bf16[1024,512]{1,0:T(8,128)(2,1)} %maximum_select_fusion.1.refs_0_, s32[1,1024]{1,0:T(1,128)} %get-tuple-element.229.refs_1_, ...), custom_call_target="tpu_custom_call" | custom-call | tf_op jit(solution)/shard_map/pallas_call | solution.py:322
  169.1 8.3 %shard_map.273 = (bf16[1024,512]{1,0:T(8,128)(2,1)}, f32[8,1024]{1,0:T(8,128)}, bf16[1920,512]{1,0:T(8,128)(2,1)}, bf16[1920,512]{1,0:T(8,128)(2,1)}) custom-call(s32[13,4]{1,0:T(8,128)} %get-tuple-element.225.info, bf16[1024,512]{1,0:T(8,128)(2,1)} %maximum_select_fusion.1.refs_0_, s32[2,1024]{1,0:T(2,128)} %get-tuple-element.226.refs_1_, ...), custom_call_target="tpu_custom_call" | custom-call | tf_op jit(solution)/shard_map/pallas_call | solution.py:322
  181.4 41.4 %shard_map.274 = (bf16[512,1024]{1,0:T(8,128)(2,1)}, f32[512,1024]{1,0:T(8,128)}, bf16[512,512]{1,0:T(8,128)(2,1)}, bf16[512,512]{1,0:T(8,128)(2,1)}, bf16[528,1...) custom-call(s32[1]{0:T(128)} %bitcast.1.core, bf16[1024,512]{1,0:T(8,128)(2,1)} %get-tuple-element.246.refs_0_.refs_2_, ...), custom_call_target="tpu_custom_call" | custom-call | tf_op jit(solution)/shard_map/pallas_call | solution.py:822
  238.8 5.4 %collective-permute-start.19 = (bf16[128,1024]{1,0:T(8,128)(2,1)S(1)}, bf16[128,1024]{1,0:T(8,128)(2,1)S(1)}, u32[]{:S(2)}, u32[]{:S(2)}) collective-permute-start(bf16[128,1024]{1,0:T(8,128)(2,1)S(1)} %get-tuple-element.394), channel_id=1, source_target_pairs={{0,4},{2,6},{4,0},{6,2},{8,12},{10,14},{12,8},{14,10},{16,20},{18,... | collective-permute-start | bytes 786440 | tf_op jit(solution)/shard_map/ppermute | solution.py:1175
  244.2 21.3 %shard_map.276 = (bf16[1024,512]{1,0:T(8,128)(2,1)}, bf16[1024,512]{1,0:T(8,128)(2,1)}, bf16[1024,512]{1,0:T(8,128)(2,1)}, bf16[1024,512]{1,0:T(8,128)(2,1)}, bf...) custom-call(s32[25,4]{1,0:T(8,128)} %get-tuple-element.264.info, ...), custom_call_target="tpu_custom_call" | custom-call | tf_op jit(solution)/shard_map/pallas_call | solution.py:568
  268.7 3.9 collective-permute-done.24.refs_5_
  274.9 5.5 %shard_map.278 = (bf16[1024,512]{1,0:T(8,128)(2,1)}, bf16[1024,512]{1,0:T(8,128)(2,1)}, bf16[896,512]{1,0:T(8,128)(2,1)}, bf16[896,512]{1,0:T(8,128)(2,1)}) custom-call(bf16[1024,512]{1,0:T(8,128)(2,1)} %get-tuple-element.295.refs_0_, bf16[1024,512]{1,0:T(8,128)(2,1)} %copy-done.16, bf16[1024,512]{1,0:T(8,128)(2,1)} %get-tuple-element.297.refs_2_, ...), custom_call_target="tpu_custom_call" | custom-call | tf_op jit(solution)/shard_map/pallas_call | solution.py:1008
  281.6 5.1 collective-permute-start.27
  286.9 7.9 %collective-permute-start.28 = (bf16[32,1024]{1,0:T(8,128)(2,1)S(1)}, bf16[32,1024]{1,0:T(8,128)(2,1)S(1)}, u32[]{:S(2)}, u32[]{:S(2)}) collective-permute-start(bf16[32,1024]{1,0:T(8,128)(2,1)S(1)} %get-tuple-element.399), channel_id=1, source_target_pairs={{0,8},{2,10},{4,12},{6,14},{8,0},{10,2},{12,4},{14,6},{16,24},{18,... | collective-permute-start | bytes 196616 | tf_op jit(solution)/shard_map/ppermute | solution.py:1175
  294.7 29.2 %collective-permute-start.29 = (bf16[32,1024]{1,0:T(8,128)(2,1)S(1)}, bf16[32,1024]{1,0:T(8,128)(2,1)S(1)}, u32[]{:S(2)}, u32[]{:S(2)}) collective-permute-start(bf16[32,1024]{1,0:T(8,128)(2,1)S(1)} %get-tuple-element.398), channel_id=1, source_target_pairs={{0,16},{2,18},{4,20},{6,22},{8,24},{10,26},{12,28},{14,30},{16,0},... | collective-permute-start | bytes 196616 | tf_op jit(solution)/shard_map/ppermute | solution.py:1175
  325.9 28.9 %shard_map.279 = (bf16[1024,512]{1,0:T(8,128)(2,1)}, bf16[1024,512]{1,0:T(8,128)(2,1)}, bf16[1024,512]{1,0:T(8,128)(2,1)}) custom-call(s32[7,4]{1,0:T(8,128)} %get-tuple-element.201.info, bf16[1024,512]{1,0:T(8,128)(2,1)} %maximum_select_fusion.1.refs_0_, bf16[1024,512]{1,0:T(8,128)(2,1)} %maximum_select_fusion.2.refs_1_, ...), custom_call_target="tpu_custom_call" | custom-call | tf_op jit(solution)/shard_map/pallas_call | solution.py:568
  359.8 5.5 %collective-permute-start.36 = (bf16[896,512]{1,0:T(8,128)(2,1)}, bf16[896,512]{1,0:T(8,128)(2,1)}, u32[]{:S(2)}, u32[]{:S(2)}) collective-permute-start(bf16[896,512]{1,0:T(8,128)(2,1)} %get-tuple-element.306), channel_id=1, source_target_pairs={{0,4},{2,6},{4,8},{6,10},{8,12},{10,14},{12,16},{14,18},{16,20},{1... | collective-permute-start | bytes 2752520 | tf_op jit(solution)/shard_map/ppermute | solution.py:1161
  365.3 7.8 %shard_map.280 = (f32[512,512]{1,0:T(8,128)}, bf16[512,512]{1,0:T(8,128)(2,1)}, bf16[512,512]{1,0:T(8,128)(2,1)}, bf16[512,512]{1,0:T(8,128)(2,1)}) custom-call(s32[1]{0:T(128)} %bitcast.1.core, bf16[1024,512]{1,0:T(8,128)(2,1)} %get-tuple-element.314.refs_0_, bf16[512,512]{1,0:T(8,128)(2,1)} %copy-done.33, bf16[2,1024,512]{2,1,0:T(8,128)(2,1)} %bitcast.32, ...), custom_call_target="tpu_custom_call" | custom-call | tf_op jit(solution)/shard_map/pallas_call | solution.py:822
  379.0 13.9 %shard_map.281 = (bf16[768,512]{1,0:T(8,128)(2,1)}, bf16[768,512]{1,0:T(8,128)(2,1)}, bf16[1024,512]{1,0:T(8,128)(2,1)}, bf16[1024,512]{1,0:T(8,128)(2,1)}, f32[...) custom-call(s32[7,4]{1,0:T(8,128)} %get-tuple-element.200.info, ...), custom_call_target="tpu_custom_call" | custom-call | tf_op jit(solution)/shard_map/pallas_call | solution.py:568
  392.9 5.1 collective-permute-done.36.refs_5_
  406.5 4.4 shard_map.284.refs_0_
  420.5 11.4 %collective-permute-start.42 = (bf16[64,1024]{1,0:T(8,128)(2,1)S(1)}, bf16[64,1024]{1,0:T(8,128)(2,1)S(1)}, u32[]{:S(2)}, u32[]{:S(2)}) collective-permute-start(bf16[64,1024]{1,0:T(8,128)(2,1)S(1)} %copy-done.34), channel_id=1, source_target_pairs={{0,8},{2,10},{4,12},{6,14},{8,0},{10,2},{12,4},{14,6},{16,24},{18,... | collective-permute-start | bytes 393224 | tf_op jit(solution)/shard_map/ppermute | solution.py:1175
  431.9 19.2 %collective-permute-start.43 = (bf16[64,1024]{1,0:T(8,128)(2,1)S(1)}, bf16[64,1024]{1,0:T(8,128)(2,1)S(1)}, u32[]{:S(2)}, u32[]{:S(2)}) collective-permute-start(bf16[64,1024]{1,0:T(8,128)(2,1)S(1)} %copy-done.34), channel_id=1, source_target_pairs={{0,16},{2,18},{4,20},{6,22},{8,24},{10,26},{12,28},{14,30},{16,0},... | collective-permute-start | bytes 393224 | tf_op jit(solution)/shard_map/ppermute | solution.py:1175
  451.1 24.4 %shard_map.287 = (bf16[1024,512]{1,0:T(8,128)(2,1)}, bf16[1024,512]{1,0:T(8,128)(2,1)}) custom-call(s32[7,4]{1,0:T(8,128)} %get-tuple-element.205.info, bf16[1024,512]{1,0:T(8,128)(2,1)} %multiply_convert_fusion.refs_0_, bf16[1024,512]{1,0:T(8,128)(2,1)} %maximum_select_fusion.3.refs_1_, bf16[1024,512]{1,0:T(8,128)(2,1)} %get-tuple-element.216.refs_0_.refs_2_, ...), custom_call_target="tpu_custom_call" | custom-call | tf_op jit(solution)/shard_map/pallas_call | solution.py:568
  475.6 5.7 %collective-permute-done.42.refs_1_ = bf16[64,1024]{1,0:T(8,128)(2,1)S(1)} collective-permute-done((bf16[64,1024]{1,0:T(8,128)(2,1)S(1)}, bf16[64,1024]{1,0:T(8,128)(2,1)S(1)}, u32[]{:S(2)}, u32[]{:S(2)}) %collective-permute-start.42) | collective-permute-done | bytes 131104 | tf_op jit(solution)/shard_map/ppermute | solution.py:1175
  481.3 7.5 %collective-permute-done.43.refs_2_ = bf16[64,1024]{1,0:T(8,128)(2,1)S(1)} collective-permute-done((bf16[64,1024]{1,0:T(8,128)(2,1)S(1)}, bf16[64,1024]{1,0:T(8,128)(2,1)S(1)}, u32[]{:S(2)}, u32[]{:S(2)}) %collective-permute-start.43) | collective-permute-done | bytes 131104 | tf_op jit(solution)/shard_map/ppermute | solution.py:1175
  505.4 6.5 %collective-permute-done.48.refs_2_ = bf16[160,1024]{1,0:T(8,128)(2,1)S(1)} collective-permute-done((bf16[160,1024]{1,0:T(8,128)(2,1)S(1)}, bf16[160,1024]{1,0:T(8,128)(2,1)S(1)}, u32[]{:S(2)}, u32[]{:S(2)}) %collective-permute-start.48) | collective-permute-done | bytes 327712 | tf_op jit(solution)/shard_map/ppermute | solution.py:1175
  (242 shorter events, 127.8 us)
Async XLA Ops:
  7.2 118.1 %all-gather.15.cloned.1.call-start = ((), (), s32[]{:S(2)}) async-start(), calls=%async_computation | async-start | bytes 3145728 | tf_op jit(solution)/shard_map/all_gather | solution.py:1279
  11.3 114.0 %all-gather.17.cloned.1.call-start = ((), (), s32[]{:S(2)}) async-start(), calls=%async_computation.1 | async-start | bytes 3145728 | tf_op jit(solution)/shard_map/all_gather | solution.py:1279
  12.1 168.5 %all-gather.21.cloned.1.call-start = ((), (), s32[]{:S(2)}) async-start(), calls=%async_computation.3 | async-start | bytes 1572864 | tf_op jit(solution)/shard_map/all_gather | solution.py:1279
  14.0 52.1 %collective-permute-start = (bf16[1024,512]{1,0:T(8,128)(2,1)}, bf16[1024,512]{1,0:T(8,128)(2,1)}, u32[]{:S(2)}, u32[]{:S(2)}) collective-permute-start(bf16[1024,512]{1,0:T(8,128)(2,1)} %constant_dynamic-slice_fusion.13), channel_id=1, source_target_pairs={{0,2},{2,4},{4,6},{6,8},{8,10},{10,12},{12,14},{14,16},{16,18},{18... | collective-permute-start | bytes 3145736 | tf_op jit(solution)/shard_map/ppermute | solution.py:1161
  21.0 45.1 %collective-permute-start.2 = (bf16[1024,512]{1,0:T(8,128)(2,1)}, bf16[1024,512]{1,0:T(8,128)(2,1)}, u32[]{:S(2)}, u32[]{:S(2)}) collective-permute-start(bf16[1024,512]{1,0:T(8,128)(2,1)} %constant_dynamic-slice_fusion.12), channel_id=1, source_target_pairs={{2,0},{4,2},{6,4},{8,6},{10,8},{12,10},{14,12},{16,14},{18,16},{20... | collective-permute-start | bytes 3145736 | tf_op jit(solution)/shard_map/ppermute | solution.py:1161
  23.3 37.4 %collective-permute-start.1 = (bf16[768,512]{1,0:T(8,128)(2,1)}, bf16[768,512]{1,0:T(8,128)(2,1)}, u32[]{:S(2)}, u32[]{:S(2)}) collective-permute-start(bf16[768,512]{1,0:T(8,128)(2,1)} %dynamic-slice), channel_id=1, source_target_pairs={{0,4},{2,6},{4,8},{6,10},{8,12},{10,14},{12,16},{14,18},{16,20},{1... | collective-permute-start | bytes 2359304 | tf_op jit(solution)/shard_map/ppermute | solution.py:1161
  67.0 113.5 %all-gather.23.cloned.1.call-start = ((), (), s32[]{:S(2)}) async-start(), calls=%async_computation.4 | async-start | bytes 1572864 | tf_op jit(solution)/shard_map/all_gather | solution.py:1279
  67.9 112.6 %all-gather.19.cloned.1.call-start = ((), (), s32[]{:S(2)}) async-start(), calls=%async_computation.2 | async-start | bytes 3145728 | tf_op jit(solution)/shard_map/all_gather | solution.py:1279
  68.5 112.1 %all-gather.25.cloned.1.call-start = ((), (), s32[]{:S(2)}) async-start(), calls=%async_computation.5 | async-start | bytes 12582912 | tf_op jit(solution)/shard_map/all_gather | solution.py:1279
  69.1 111.5 %all-gather.27.cloned.1.call-start = ((), (), s32[]{:S(2)}) async-start(), calls=%async_computation.6 | async-start | bytes 12582912 | tf_op jit(solution)/shard_map/all_gather | solution.py:1279
  74.9 26.6 %collective-permute-start.6 = (bf16[1024,512]{1,0:T(8,128)(2,1)}, bf16[1024,512]{1,0:T(8,128)(2,1)}, u32[]{:S(2)}, u32[]{:S(2)}) collective-permute-start(bf16[1024,512]{1,0:T(8,128)(2,1)} %constant_dynamic-slice_fusion.12), channel_id=1, source_target_pairs={{0,2},{2,4},{4,6},{6,8},{8,10},{10,12},{12,14},{14,16},{16,18},{18... | collective-permute-start | bytes 3145736 | tf_op jit(solution)/shard_map/ppermute | solution.py:1161
  104.4 56.8 %collective-permute-start.11 = (bf16[896,512]{1,0:T(8,128)(2,1)}, bf16[896,512]{1,0:T(8,128)(2,1)S(1)}, u32[]{:S(2)}, u32[]{:S(2)}) collective-permute-start(bf16[896,512]{1,0:T(8,128)(2,1)} %get-tuple-element.240), channel_id=1, source_target_pairs={{4,0},{6,2},{8,4},{10,6},{12,8},{14,10},{16,12},{18,14},{20,16},{2... | collective-permute-start | bytes 2752520 | tf_op jit(solution)/shard_map/ppermute | solution.py:1161
  105.7 58.6 %collective-permute-start.10 = (bf16[896,512]{1,0:T(8,128)(2,1)}, bf16[896,512]{1,0:T(8,128)(2,1)S(1)}, u32[]{:S(2)}, u32[]{:S(2)}) collective-permute-start(bf16[896,512]{1,0:T(8,128)(2,1)} %get-tuple-element.239), channel_id=1, source_target_pairs={{0,4},{2,6},{4,8},{6,10},{8,12},{10,14},{12,16},{14,18},{16,20},{1... | collective-permute-start | bytes 2752520 | tf_op jit(solution)/shard_map/ppermute | solution.py:1161
  227.7 37.8 %collective-permute-start.21 = (bf16[512,1024]{1,0:T(8,128)(2,1)S(1)}, bf16[512,1024]{1,0:T(8,128)(2,1)}, u32[]{:S(2)}, u32[]{:S(2)}) collective-permute-start(bf16[512,1024]{1,0:T(8,128)(2,1)S(1)} %copy-done.10), channel_id=1, source_target_pairs={{0,1},{1,0},{2,3},{3,2},{4,5},{5,4},{6,7},{7,6},{8,9},{9,8},{10,11... | collective-permute-start | bytes 3145736 | tf_op jit(solution)/shard_map/ppermute | solution.py:1137
  236.3 29.2 %collective-permute-start.18 = (bf16[128,1024]{1,0:T(8,128)(2,1)S(1)}, bf16[128,1024]{1,0:T(8,128)(2,1)S(1)}, u32[]{:S(2)}, u32[]{:S(2)}) collective-permute-start(bf16[128,1024]{1,0:T(8,128)(2,1)S(1)} %get-tuple-element.395), channel_id=1, source_target_pairs={{0,2},{2,0},{4,6},{6,4},{8,10},{10,8},{12,14},{14,12},{16,18},{18,... | collective-permute-start | bytes 786440 | tf_op jit(solution)/shard_map/ppermute | solution.py:1175
  238.8 26.7 %collective-permute-start.19 = (bf16[128,1024]{1,0:T(8,128)(2,1)S(1)}, bf16[128,1024]{1,0:T(8,128)(2,1)S(1)}, u32[]{:S(2)}, u32[]{:S(2)}) collective-permute-start(bf16[128,1024]{1,0:T(8,128)(2,1)S(1)} %get-tuple-element.394), channel_id=1, source_target_pairs={{0,4},{2,6},{4,0},{6,2},{8,12},{10,14},{12,8},{14,10},{16,20},{18,... | collective-permute-start | bytes 786440 | tf_op jit(solution)/shard_map/ppermute | solution.py:1175
  244.2 21.3 %collective-permute-start.20 = (bf16[128,1024]{1,0:T(8,128)(2,1)S(1)}, bf16[128,1024]{1,0:T(8,128)(2,1)S(1)}, u32[]{:S(2)}, u32[]{:S(2)}) collective-permute-start(bf16[128,1024]{1,0:T(8,128)(2,1)S(1)} %get-tuple-element.393), channel_id=1, source_target_pairs={{0,6},{2,4},{4,2},{6,0},{8,14},{10,12},{12,10},{14,8},{16,22},{18,... | collective-permute-start | bytes 786440 | tf_op jit(solution)/shard_map/ppermute | solution.py:1175
  280.3 74.5 %collective-permute-start.26 = (bf16[1024,512]{1,0:T(8,128)(2,1)}, bf16[1024,512]{1,0:T(8,128)(2,1)S(1)}, u32[]{:S(2)}, u32[]{:S(2)}) collective-permute-start(bf16[1024,512]{1,0:T(8,128)(2,1)} %get-tuple-element.303), channel_id=1, source_target_pairs={{2,0},{4,2},{6,4},{8,6},{10,8},{12,10},{14,12},{16,14},{18,16},{20... | collective-permute-start | bytes 3145736 | tf_op jit(solution)/shard_map/ppermute | solution.py:1161
  281.6 73.3 %collective-permute-start.27 = (bf16[1024,512]{1,0:T(8,128)(2,1)}, bf16[1024,512]{1,0:T(8,128)(2,1)S(1)}, u32[]{:S(2)}, u32[]{:S(2)}) collective-permute-start(bf16[1024,512]{1,0:T(8,128)(2,1)} %get-tuple-element.304), channel_id=1, source_target_pairs={{0,2},{2,4},{4,6},{6,8},{8,10},{10,12},{12,14},{14,16},{16,18},{18... | collective-permute-start | bytes 3145736 | tf_op jit(solution)/shard_map/ppermute | solution.py:1161
  286.9 68.0 %collective-permute-start.28 = (bf16[32,1024]{1,0:T(8,128)(2,1)S(1)}, bf16[32,1024]{1,0:T(8,128)(2,1)S(1)}, u32[]{:S(2)}, u32[]{:S(2)}) collective-permute-start(bf16[32,1024]{1,0:T(8,128)(2,1)S(1)} %get-tuple-element.399), channel_id=1, source_target_pairs={{0,8},{2,10},{4,12},{6,14},{8,0},{10,2},{12,4},{14,6},{16,24},{18,... | collective-permute-start | bytes 196616 | tf_op jit(solution)/shard_map/ppermute | solution.py:1175
  294.7 60.1 %collective-permute-start.29 = (bf16[32,1024]{1,0:T(8,128)(2,1)S(1)}, bf16[32,1024]{1,0:T(8,128)(2,1)S(1)}, u32[]{:S(2)}, u32[]{:S(2)}) collective-permute-start(bf16[32,1024]{1,0:T(8,128)(2,1)S(1)} %get-tuple-element.398), channel_id=1, source_target_pairs={{0,16},{2,18},{4,20},{6,22},{8,24},{10,26},{12,28},{14,30},{16,0},... | collective-permute-start | bytes 196616 | tf_op jit(solution)/shard_map/ppermute | solution.py:1175
  323.9 30.9 %collective-permute-start.30 = (bf16[32,1024]{1,0:T(8,128)(2,1)S(1)}, bf16[32,1024]{1,0:T(8,128)(2,1)S(1)}, u32[]{:S(2)}, u32[]{:S(2)}) collective-permute-start(bf16[32,1024]{1,0:T(8,128)(2,1)S(1)} %get-tuple-element.397), channel_id=1, source_target_pairs={{0,24},{2,26},{4,28},{6,30},{8,16},{10,18},{12,20},{14,22},{16,8},... | collective-permute-start | bytes 196616 | tf_op jit(solution)/shard_map/ppermute | solution.py:1175
  358.4 20.6 %collective-permute-start.32 = (bf16[1024,512]{1,0:T(8,128)(2,1)}, bf16[1024,512]{1,0:T(8,128)(2,1)}, u32[]{:S(2)}, u32[]{:S(2)}) collective-permute-start(bf16[1024,512]{1,0:T(8,128)(2,1)} %get-tuple-element.316), channel_id=1, source_target_pairs={{0,1},{1,0},{2,3},{3,2},{4,5},{5,4},{6,7},{7,6},{8,9},{9,8},{10,11... | collective-permute-start | bytes 3145736 | tf_op jit(solution)/shard_map/ppermute | solution.py:1137
  358.5 34.4 %collective-permute-start.35 = (bf16[896,512]{1,0:T(8,128)(2,1)}, bf16[896,512]{1,0:T(8,128)(2,1)S(1)}, u32[]{:S(2)}, u32[]{:S(2)}) collective-permute-start(bf16[896,512]{1,0:T(8,128)(2,1)} %get-tuple-element.305), channel_id=1, source_target_pairs={{4,0},{6,2},{8,4},{10,6},{12,8},{14,10},{16,12},{18,14},{20,16},{2... | collective-permute-start | bytes 2752520 | tf_op jit(solution)/shard_map/ppermute | solution.py:1161
  359.8 38.2 %collective-permute-start.36 = (bf16[896,512]{1,0:T(8,128)(2,1)}, bf16[896,512]{1,0:T(8,128)(2,1)}, u32[]{:S(2)}, u32[]{:S(2)}) collective-permute-start(bf16[896,512]{1,0:T(8,128)(2,1)} %get-tuple-element.306), channel_id=1, source_target_pairs={{0,4},{2,6},{4,8},{6,10},{8,12},{10,14},{12,16},{14,18},{16,20},{1... | collective-permute-start | bytes 2752520 | tf_op jit(solution)/shard_map/ppermute | solution.py:1161
  411.1 64.5 %collective-permute-start.41 = (bf16[1024,512]{1,0:T(8,128)(2,1)}, bf16[1024,512]{1,0:T(8,128)(2,1)S(1)}, u32[]{:S(2)}, u32[]{:S(2)}) collective-permute-start(bf16[1024,512]{1,0:T(8,128)(2,1)} %get-tuple-element.355), channel_id=1, source_target_pairs={{2,0},{4,2},{6,4},{8,6},{10,8},{12,10},{14,12},{16,14},{18,16},{20... | collective-permute-start | bytes 3145736 | tf_op jit(solution)/shard_map/ppermute | solution.py:1161
  412.4 63.2 %collective-permute-start.40 = (bf16[768,512]{1,0:T(8,128)(2,1)}, bf16[768,512]{1,0:T(8,128)(2,1)}, u32[]{:S(2)}, u32[]{:S(2)}) collective-permute-start(bf16[768,512]{1,0:T(8,128)(2,1)} %get-tuple-element.354), channel_id=1, source_target_pairs={{4,0},{6,2},{8,4},{10,6},{12,8},{14,10},{16,12},{18,14},{20,16},{2... | collective-permute-start | bytes 2359304 | tf_op jit(solution)/shard_map/ppermute | solution.py:1161
  420.5 60.8 %collective-permute-start.42 = (bf16[64,1024]{1,0:T(8,128)(2,1)S(1)}, bf16[64,1024]{1,0:T(8,128)(2,1)S(1)}, u32[]{:S(2)}, u32[]{:S(2)}) collective-permute-start(bf16[64,1024]{1,0:T(8,128)(2,1)S(1)} %copy-done.34), channel_id=1, source_target_pairs={{0,8},{2,10},{4,12},{6,14},{8,0},{10,2},{12,4},{14,6},{16,24},{18,... | collective-permute-start | bytes 393224 | tf_op jit(solution)/shard_map/ppermute | solution.py:1175
  431.9 56.9 %collective-permute-start.43 = (bf16[64,1024]{1,0:T(8,128)(2,1)S(1)}, bf16[64,1024]{1,0:T(8,128)(2,1)S(1)}, u32[]{:S(2)}, u32[]{:S(2)}) collective-permute-start(bf16[64,1024]{1,0:T(8,128)(2,1)S(1)} %copy-done.34), channel_id=1, source_target_pairs={{0,16},{2,18},{4,20},{6,22},{8,24},{10,26},{12,28},{14,30},{16,0},... | collective-permute-start | bytes 393224 | tf_op jit(solution)/shard_map/ppermute | solution.py:1175
  451.1 37.8 %collective-permute-start.44 = (bf16[64,1024]{1,0:T(8,128)(2,1)S(1)}, bf16[64,1024]{1,0:T(8,128)(2,1)S(1)}, u32[]{:S(2)}, u32[]{:S(2)}) collective-permute-start(bf16[64,1024]{1,0:T(8,128)(2,1)S(1)} %copy-done.34), channel_id=1, source_target_pairs={{0,24},{2,26},{4,28},{6,30},{8,16},{10,18},{12,20},{14,22},{16,8},... | collective-permute-start | bytes 393224 | tf_op jit(solution)/shard_map/ppermute | solution.py:1175
  494.9 17.0 %collective-permute-start.48 = (bf16[160,1024]{1,0:T(8,128)(2,1)S(1)}, bf16[160,1024]{1,0:T(8,128)(2,1)S(1)}, u32[]{:S(2)}, u32[]{:S(2)}) collective-permute-start(bf16[160,1024]{1,0:T(8,128)(2,1)S(1)} %copy-done.8), channel_id=1, source_target_pairs={{0,4},{2,6},{4,0},{6,2},{8,12},{10,14},{12,8},{14,10},{16,20},{18,... | collective-permute-start | bytes 983048 | tf_op jit(solution)/shard_map/ppermute | solution.py:1175
  494.9 17.0 %collective-permute-start.49 = (bf16[160,1024]{1,0:T(8,128)(2,1)S(1)}, bf16[160,1024]{1,0:T(8,128)(2,1)S(1)}, u32[]{:S(2)}, u32[]{:S(2)}) collective-permute-start(bf16[160,1024]{1,0:T(8,128)(2,1)S(1)} %copy-done.8), channel_id=1, source_target_pairs={{0,6},{2,4},{4,2},{6,0},{8,14},{10,12},{12,10},{14,8},{16,22},{18,... | collective-permute-start | bytes 983048 | tf_op jit(solution)/shard_map/ppermute | solution.py:1175
  (76 other events, 438.2 us)
Sparse Core Ops, SparseCore 0:
  11.4 13.2 all-gather.14
  26.3 11.7 all-gather.16
  67.1 26.1 all-gather.20
  94.7 10.3 all-gather.22
  106.5 11.5 all-gather.18
  119.5 21.0 all-gather.24
  142.1 21.3 all-gather.26
